TPU v7x, 512 devices: a whole 4x4x16 slice. The times are simulated.
512 devices in a mesh: tx: 32 (over x, z_lo, core), slab: 16 (over z_hi, y).
Axes of the slice: x: 4, y: 4, z: 16 (z_hi: 4, z_lo: 4; z = z_hi * 4 + z_lo), core: 2. Of those that a mesh axis runs over, the one named last changes fastest.
Arguments:
- fwd_field: float32 [32, 6, 256, 32, 128], P('tx', None, 'slab'), may hold values from -6 to 6
- adj_prev: float32 [32, 6, 256, 32, 128], P('tx', None, 'slab'), may hold values from -4 to 4
- sigma: float32 [256, 32, 128], P('slab'), may hold values from 0.1 to 10
- omega: float32 [32], P('tx'), may hold values from 0.3 to 3
- res_vals: float32 [32, 6, 4096], P('tx', None, 'slab'), may hold values from -6 to 6
- rec_slab: int32 [32, 4096, 1], P('tx', 'slab'), may hold values from 0 to 15; in each aligned block of 256 rows (0 to 255, 256 to 511, ..., all dimensions but the last counted through in order) at most 32 rows name the same one
- rec_cell: int32 [32, 4096], P('tx', 'slab'), may hold values from 0 to 65535
Outputs:
- adjoint: float32 [32, 6, 256, 32, 128], P('tx', None, 'slab')
- gradient: float32 [256, 32, 128], P('slab', 'tx')
Inputs may be any that keep to these rules, and one draw needn't show every extreme that they name: `rec_slab`: among one transmitter's receivers held by one index of slab (aligned blocks of 256), at most 32 name the same slab, and some block reaches 32.
All inputs are finite; a program needn't handle non-finite values.
Results may differ from a plain program's by a relative error of at most 0.0001.
Values sent between devices are 32-bit elements; how exact they have to be, the bound alone decides.
No kernel may reach another device: no remote copies, remote signals or barrier semaphores. Data moves between devices by JAX's collectives and lax.ppermute only.
A program may use at most 128 MiB of HBM per device.

v0:
```python
import jax
import jax.numpy as jnp
from jax import lax
from jax.sharding import PartitionSpec as P

SWEEPS = 3


def extended_2(value, sides, width):
    for axis, dim in sides:
        size, length = (lax.axis_size(axis), value.shape[dim])
        up = [(i, (i + 1) % size) for i in range(size - 1)]
        down = [(j, i) for i, j in up]
        last = lax.slice_in_dim(value, length - width, length, axis=dim)
        leading = lax.slice_in_dim(value, 0, width, axis=dim)
        before = lax.ppermute(last, axis, up)
        after = lax.ppermute(leading, axis, down)
        value = jnp.concatenate([before, value, after], axis=dim)
    return value


def neighbour_sum(extended):
    middle = extended[:, :, 1:-1]
    beside = extended[:, :, 2:] + extended[:, :, :-2]
    padded_y = jnp.pad(middle, ((0, 0), (0, 0), (0, 0), (1, 1), (0, 0)))
    beside = beside + padded_y[:, :, :, 2:] + padded_y[:, :, :, :-2]
    padded_z = jnp.pad(middle, ((0, 0), (0, 0), (0, 0), (0, 0), (1, 1)))
    beside = beside + padded_z[:, :, :, :, 2:] + padded_z[:, :, :, :, :-2]
    return beside


def relax(extended, source, coef_a, coef_b):
    rhs = source + neighbour_sum(extended)
    real_part = rhs[:, :3]
    imag_part = rhs[:, 3:]
    return jnp.concatenate(
        [coef_a * real_part - coef_b * imag_part, coef_a * imag_part + coef_b * real_part], 1
    )


def coefficients(omega, sigma_cells):
    beta = omega[:, None, None, None, None] * sigma_cells
    den = 36.0 + beta * beta
    return (6.0 / den, beta / den)


def shards(fwd_field, adj_prev, sigma, omega, res_vals, rec_slab, rec_cell):
    pairs, comps, width_x, width_y, width_z = fwd_field.shape
    cells = width_x * width_y * width_z
    rec_count = rec_cell.shape[1]
    slabs = lax.axis_size("slab")
    capacity = 2 * rec_count // slabs
    pair_rows = jnp.arange(pairs)[:, None]
    target = rec_slab[:, :, 0]
    onehot = (target[:, :, None] == jnp.arange(slabs)[None, None, :]).astype(jnp.int32)
    slot = jnp.sum(jnp.cumsum(onehot, axis=1) * onehot, axis=2) - 1
    send_vals = jnp.zeros((pairs, slabs, comps, capacity), jnp.float32)
    send_vals = send_vals.at[pair_rows, target, :, slot].set(jnp.transpose(res_vals, (0, 2, 1)))
    send_cells = jnp.zeros((pairs, slabs, capacity), jnp.float32)
    send_cells = send_cells.at[pair_rows, target, slot].set(rec_cell.astype(jnp.float32))
    got_vals, got_cells = (
        lax.all_to_all(send_vals, "slab", split_axis=1, concat_axis=1, tiled=True),
        lax.all_to_all(send_cells, "slab", split_axis=1, concat_axis=1, tiled=True),
    )
    where_cells = got_cells.reshape(pairs, slabs * capacity).astype(jnp.int32)
    arrived = jnp.transpose(got_vals, (0, 2, 1, 3)).reshape(pairs, comps, slabs * capacity)
    source = jnp.zeros((pairs, comps, cells), jnp.float32)
    source = source.at[pair_rows, :, where_cells].add(jnp.transpose(arrived, (0, 2, 1)))
    source = source.reshape(pairs, comps, width_x, width_y, width_z)
    coef_a, coef_b = coefficients(omega, sigma[None, None])
    field = adj_prev
    for sweep in range(SWEEPS):
        extended = extended_2(field, (("slab", 2),), 1)
        field = relax(extended, source, coef_a, coef_b)
    pairs_all = pairs * lax.axis_size("tx")
    factor = 1.0 / jnp.sqrt(jnp.float32(3 * pairs_all))
    terms = fwd_field[:, :3] * field[:, 3:] + fwd_field[:, 3:] * field[:, :3]
    partial_grad = jnp.sum(omega[:, None, None, None, None] * terms, axis=(0, 1)) * factor
    gradient = lax.psum_scatter(partial_grad, "tx", scatter_dimension=1, tiled=True)
    return (field, gradient)


def solution(mesh):
    placed = (
        P("tx", None, "slab", None, None),
        P("tx", None, "slab", None, None),
        P("slab", None, None),
        P("tx"),
        P("tx", None, "slab"),
        P("tx", "slab", None),
        P("tx", "slab"),
    )
    return jax.shard_map(
        shards,
        mesh=mesh,
        in_specs=placed,
        out_specs=(P("tx", None, "slab", None, None), P("slab", "tx", None)),
        check_vma=False,
    )
```

profile of v0, /device:TPU:24, one launch (start us, length us, event | category | flops | bytes accessed | tf_op | source)
XLA Modules:
  0.0 356.6 jit_solution(9852213011015703934)
XLA Ops:
  7.2 0.7 compare_convert_fusion
  7.9 0.6 reduce-window.6
  8.9 0.7 fusion.27
  9.7 0.7 compare_select_fusion.3
  10.4 0.7 convert_element_type.35
  11.1 0.6 broadcast.186
  11.7 35.8 %scatter_fusion = f32[16,32]{1,0:T(8,128)} fusion(f32[16,32]{1,0:T(8,128)} %broadcast.186, s32[256]{0:T(256)S(1)} %bitcast.47, f32[256]{0:T(256)S(1)} %bitcast.59), kind=kCustom, calls=%fused_computation | custom fusion | bytes 5120 | tf_op jit(solution)/shard_map/scatter | solution.py:60
  47.5 17.7 %all-to-all-start = ((f32[1,16,32]{2,0,1:T(1,128)}), f32[1,16,32]{2,0,1:T(1,128)S(1)}, u32[]{:S(2)}, u32[]{:S(2)}) async-start(f32[1,16,32]{2,0,1:T(1,128)} %bitcast.14), calls=%async_computation | async-start | bytes 16384 | tf_op jit(solution)/shard_map/all_to_all | solution.py:63
  65.2 1.0 fusion.29
  66.2 2.8 collective-permute-start
  68.9 9.1 %collective-permute-start.1 = (f32[1,6,1,32,128]{4,3,2,1,0:T(8,128)S(1)}, f32[1,6,1,32,128]{4,3,2,1,0:T(8,128)S(1)}, u32[]{:S(2)}, u32[]{:S(2)}) collective-permute-start(f32[1,6,1,32,128]{4,3,2,1,0:T(8,128)S(1)} %get-tuple-element.20), channel_id=1, source_target_pairs={{0,1},{1,2},{2,3},{3,4},{4,5},{5,6},{6,7},{7,8},{8,9},{9,10},{10,1... | collective-permute-start | bytes 294920 | tf_op jit(solution)/shard_map/ppermute | solution.py:16
  78.9 12.2 %scatter_fusion.1 = f32[16,6,32]{1,2,0:T(8,128)S(1)} fusion(f32[16,6,32]{1,2,0:T(8,128)S(1)} %broadcast.188, s32[256]{0:T(256)S(1)} %bitcast.48, f32[256,6]{1,0:T(8,128)S(1)} %bitcast.51), kind=kCustom, calls=%fused_computation.1 | custom fusion | bytes 20480 | tf_op jit(solution)/shard_map/scatter | solution.py:58
  91.3 0.6 broadcast.209
  91.9 0.8 reduce.7
  92.8 0.7 reshape.254
  93.5 14.1 %all-to-all-start.1 = ((f32[16,1,192]{2,1,0:T(1,128)}), f32[16,1,192]{2,1,0:T(1,128)S(1)}, u32[]{:S(2)}, u32[]{:S(2)}) async-start(f32[16,1,192]{2,1,0:T(1,128)} %reshape.254), calls=%async_computation.1 | async-start | bytes 32768 | tf_op jit(solution)/shard_map/all_to_all | solution.py:62
  107.8 12.7 %all-to-all-done.1 = f32[16,1,192]{2,1,0:T(1,128)S(1)} async-done(((f32[16,1,192]{2,1,0:T(1,128)}), f32[16,1,192]{2,1,0:T(1,128)S(1)}, u32[]{:S(2)}, u32[]{:S(2)}) %all-to-all-start.1) | async-done | bytes 12320 | tf_op jit(solution)/shard_map/all_to_all | solution.py:62
  120.4 0.7 reduce.8
  121.6 16.5 %scatter_custom_fusion.2 = f32[6,65536]{0,1:T(8,128)} fusion(s32[512]{0:T(512)S(1)} %bitcast.63, f32[]{:T(128)} %constant.11.clone.1, f32[1,512,6]{2,1,0:T(8,128)S(1)} %copy.56), kind=kCustom, calls=%fused_computation.3 | custom fusion | flops 3072 | bytes 1835012 | tf_op jit(solution)/shard_map/scatter-add | solution.py:68
  138.1 19.6 %copy.52 = f32[1,6,16,32,128]{4,3,2,1,0:T(8,128)S(1)} copy(f32[1,6,16,32,128]{1,4,3,2,0:T(8,128)} %bitcast.46) | data formatting | bytes 3145728 | tf_op jit(solution)/shard_map/reshape | solution.py:69
  157.7 6.0 %fusion.6 = f32[1,6,16,32,128]{4,3,2,1,0:T(8,128)S(1)} fusion(f32[1,6,16,32,128]{4,3,2,1,0:T(8,128)S(1)} %copy.52, f32[1,6,16,32,128]{4,3,2,1,0:T(8,128)} %param.8, f32[1,6,1,32,128]{4,3,2,1,0:T(8,128)S(1)} %collective-permute-done.1, f32[1,6,1,32,128]{4,3,2,1,0:T(8,128)S(1)} %collective-permute-done), kind=kLoop, calls=%fused_computation.31 | loop fusion | flops 3145728 | bytes 4915200 | tf_op jit(solution)/shard_map/add | solution.py:33
  164.0 1.9 collective-permute-start.2
  165.9 10.1 %collective-permute-start.3 = (f32[1,6,1,32,128]{4,3,2,1,0:T(8,128)S(1)}, f32[1,6,1,32,128]{4,3,2,1,0:T(8,128)S(1)}, u32[]{:S(2)}, u32[]{:S(2)}) collective-permute-start(f32[1,6,1,32,128]{4,3,2,1,0:T(8,128)S(1)} %get-tuple-element.18), channel_id=1, source_target_pairs={{0,1},{1,2},{2,3},{3,4},{4,5},{5,6},{6,7},{7,8},{8,9},{9,10},{10,1... | collective-permute-start | bytes 294920 | tf_op jit(solution)/shard_map/ppermute | solution.py:16
  176.2 3.9 %collective-permute-done.2 = f32[1,6,1,32,128]{4,3,2,1,0:T(8,128)S(1)} collective-permute-done((f32[1,6,1,32,128]{4,3,2,1,0:T(8,128)S(1)}, f32[1,6,1,32,128]{4,3,2,1,0:T(8,128)S(1)}, u32[]{:S(2)}, u32[]{:S(2)}) %collective-permute-start.2) | collective-permute-done | bytes 98336 | tf_op jit(solution)/shard_map/ppermute | solution.py:17
  180.1 1.0 fusion.11
  181.5 1.9 collective-permute-start.4
  183.5 9.9 %collective-permute-start.5 = (f32[1,6,1,32,128]{4,3,2,1,0:T(8,128)S(1)}, f32[1,6,1,32,128]{4,3,2,1,0:T(8,128)S(1)}, u32[]{:S(2)}, u32[]{:S(2)}) collective-permute-start(f32[1,6,1,32,128]{4,3,2,1,0:T(8,128)S(1)} %get-tuple-element.16), channel_id=1, source_target_pairs={{0,1},{1,2},{2,3},{3,4},{4,5},{5,6},{6,7},{7,8},{8,9},{9,10},{10,1... | collective-permute-start | bytes 294920 | tf_op jit(solution)/shard_map/ppermute | solution.py:16
  193.6 4.6 %collective-permute-done.4 = f32[1,6,1,32,128]{4,3,2,1,0:T(8,128)S(1)} collective-permute-done((f32[1,6,1,32,128]{4,3,2,1,0:T(8,128)S(1)}, f32[1,6,1,32,128]{4,3,2,1,0:T(8,128)S(1)}, u32[]{:S(2)}, u32[]{:S(2)}) %collective-permute-start.4) | collective-permute-done | bytes 98336 | tf_op jit(solution)/shard_map/ppermute | solution.py:17
  198.3 1.0 fusion.16
  199.9 0.8 copy.53
  200.8 1.3 pad_maximum_fusion.12
  202.0 147.8 %reduce-scatter.2.cloned.1.call-done = f32[16,1,128]{2,0,1:T(8,128)} async-done(((f32[16,32,128]{2,0,1:T(8,128)}), f32[16,1,128]{2,0,1:T(8,128)}) %reduce-scatter.2.cloned.1.call-update) | async-done | bytes 8208 | tf_op jit(solution)/shard_map/reduce_scatter | solution.py:79
  (46 shorter events, 3.0 us)
Async XLA Ops:
  7.2 71.5 %copy-start.1 = (f32[16,32,128]{2,1,0:T(8,128)S(1)}, f32[16,32,128]{2,1,0:T(8,128)}, u32[]{:S(2)}) copy-start(f32[16,32,128]{2,1,0:T(8,128)} %param.9) | copy-start | bytes 786436
  11.7 67.1 %copy-start.2 = (f32[1,6,256]{2,0,1:T(1,128)S(1)}, f32[1,6,256]{2,0,1:T(1,128)}, u32[]{:S(2)}) copy-start(f32[1,6,256]{2,0,1:T(1,128)} %param.11) | copy-start | bytes 18436
  47.5 46.0 %all-to-all-start = ((f32[1,16,32]{2,0,1:T(1,128)}), f32[1,16,32]{2,0,1:T(1,128)S(1)}, u32[]{:S(2)}, u32[]{:S(2)}) async-start(f32[1,16,32]{2,0,1:T(1,128)} %bitcast.14), calls=%async_computation | async-start | bytes 16384 | tf_op jit(solution)/shard_map/all_to_all | solution.py:63
  66.2 91.5 %collective-permute-start = (f32[1,6,1,32,128]{4,3,2,1,0:T(8,128)S(1)}, f32[1,6,1,32,128]{4,3,2,1,0:T(8,128)S(1)}, u32[]{:S(2)}, u32[]{:S(2)}) collective-permute-start(f32[1,6,1,32,128]{4,3,2,1,0:T(8,128)S(1)} %get-tuple-element.19), channel_id=1, source_target_pairs={{1,0},{2,1},{3,2},{4,3},{5,4},{6,5},{7,6},{8,7},{9,8},{10,9},{11,1... | collective-permute-start | bytes 294920 | tf_op jit(solution)/shard_map/ppermute | solution.py:17
  68.9 88.8 %collective-permute-start.1 = (f32[1,6,1,32,128]{4,3,2,1,0:T(8,128)S(1)}, f32[1,6,1,32,128]{4,3,2,1,0:T(8,128)S(1)}, u32[]{:S(2)}, u32[]{:S(2)}) collective-permute-start(f32[1,6,1,32,128]{4,3,2,1,0:T(8,128)S(1)} %get-tuple-element.20), channel_id=1, source_target_pairs={{0,1},{1,2},{2,3},{3,4},{4,5},{5,6},{6,7},{7,8},{8,9},{9,10},{10,1... | collective-permute-start | bytes 294920 | tf_op jit(solution)/shard_map/ppermute | solution.py:16
  93.5 27.0 %all-to-all-start.1 = ((f32[16,1,192]{2,1,0:T(1,128)}), f32[16,1,192]{2,1,0:T(1,128)S(1)}, u32[]{:S(2)}, u32[]{:S(2)}) async-start(f32[16,1,192]{2,1,0:T(1,128)} %reshape.254), calls=%async_computation.1 | async-start | bytes 32768 | tf_op jit(solution)/shard_map/all_to_all | solution.py:62
  107.6 242.2 %reduce-scatter.2.cloned.1.call-start = ((), (), s32[]{:S(2)}) async-start(), calls=%async_computation.3 | async-start | bytes 270336 | tf_op jit(solution)/shard_map/reduce_scatter | solution.py:79
  164.0 16.1 %collective-permute-start.2 = (f32[1,6,1,32,128]{4,3,2,1,0:T(8,128)S(1)}, f32[1,6,1,32,128]{4,3,2,1,0:T(8,128)S(1)}, u32[]{:S(2)}, u32[]{:S(2)}) collective-permute-start(f32[1,6,1,32,128]{4,3,2,1,0:T(8,128)S(1)} %get-tuple-element.17), channel_id=1, source_target_pairs={{1,0},{2,1},{3,2},{4,3},{5,4},{6,5},{7,6},{8,7},{9,8},{10,9},{11,1... | collective-permute-start | bytes 294920 | tf_op jit(solution)/shard_map/ppermute | solution.py:17
  165.9 14.2 %collective-permute-start.3 = (f32[1,6,1,32,128]{4,3,2,1,0:T(8,128)S(1)}, f32[1,6,1,32,128]{4,3,2,1,0:T(8,128)S(1)}, u32[]{:S(2)}, u32[]{:S(2)}) collective-permute-start(f32[1,6,1,32,128]{4,3,2,1,0:T(8,128)S(1)} %get-tuple-element.18), channel_id=1, source_target_pairs={{0,1},{1,2},{2,3},{3,4},{4,5},{5,6},{6,7},{7,8},{8,9},{9,10},{10,1... | collective-permute-start | bytes 294920 | tf_op jit(solution)/shard_map/ppermute | solution.py:16
  181.5 16.7 %collective-permute-start.4 = (f32[1,6,1,32,128]{4,3,2,1,0:T(8,128)S(1)}, f32[1,6,1,32,128]{4,3,2,1,0:T(8,128)S(1)}, u32[]{:S(2)}, u32[]{:S(2)}) collective-permute-start(f32[1,6,1,32,128]{4,3,2,1,0:T(8,128)S(1)} %get-tuple-element.15), channel_id=1, source_target_pairs={{1,0},{2,1},{3,2},{4,3},{5,4},{6,5},{7,6},{8,7},{9,8},{10,9},{11,1... | collective-permute-start | bytes 294920 | tf_op jit(solution)/shard_map/ppermute | solution.py:17
  183.5 14.8 %collective-permute-start.5 = (f32[1,6,1,32,128]{4,3,2,1,0:T(8,128)S(1)}, f32[1,6,1,32,128]{4,3,2,1,0:T(8,128)S(1)}, u32[]{:S(2)}, u32[]{:S(2)}) collective-permute-start(f32[1,6,1,32,128]{4,3,2,1,0:T(8,128)S(1)} %get-tuple-element.16), channel_id=1, source_target_pairs={{0,1},{1,2},{2,3},{3,4},{4,5},{5,6},{6,7},{7,8},{8,9},{9,10},{10,1... | collective-permute-start | bytes 294920 | tf_op jit(solution)/shard_map/ppermute | solution.py:16
  193.6 5.7 %copy-start = (f32[1,6,16,32,128]{4,3,2,1,0:T(8,128)S(1)}, f32[1,6,16,32,128]{4,3,2,1,0:T(8,128)}, u32[]{:S(2)}) copy-start(f32[1,6,16,32,128]{4,3,2,1,0:T(8,128)} %param.7) | copy-start | bytes 4718596
Sparse Core Ops, SparseCore 0:
  200.9 148.8 reduce-scatter.1
where the time goes:
time: 358 us; the launch traced here: 357 us
  waiting for transfers between devices  169 us (47%)
  local copies, waits for them, and re-layouts  72.5 us (20%)
  starting transfers between devices  67.6 us (19%)
  other arithmetic  32.5 us (9%)
  between operations  15 us (4%)
    reduce_scatter x1, waiting for transfers between devices, shards(): lax.psum_scatter(partial_grad, 'tx', scatter_dimension=1, tiled=True)  148 us
    scatter x1, local copies, waits for them, and re-layouts, shards(): send_cells.at[pair_rows, target, slot].set(rec_cell.astype(jnp.float32))  35.8 us
    ppermute x3, starting transfers between devices, extended_2(): before = lax.ppermute(last, axis, up)  29.2 us
    reshape x1, local copies, waits for them, and re-layouts, shards(): source = source.reshape(pairs, comps, width_x, width_y, width_z)  19.6 us
    all_to_all x1, starting transfers between devices, shards(): lax.all_to_all(send_cells, 'slab', split_axis=1, concat_axis=1, tiled=True)  17.7 us
    scatter-add x1, other arithmetic, shards(): source.at[pair_rows, :, where_cells].add(jnp.transpose(arrived, (0, 2, 1)))  16.5 us
    all_to_all x1, starting transfers between devices, shards(): lax.all_to_all(send_vals, 'slab', split_axis=1, concat_axis=1, tiled=True)  14.1 us
    all_to_all x1, waiting for transfers between devices, shards(): lax.all_to_all(send_vals, 'slab', split_axis=1, concat_axis=1, tiled=True)  12.7 us
  transfers between devices with their start and end apart: 9, of which 4 were waited for; matrix products, arithmetic and copies ran while one was open for 15% of the time, Pallas kernels for 0%

commit v1 on v0

v1 whole, which is shorter than its diff:
```python
import functools

import jax
import jax.numpy as jnp
from jax import lax
from jax.experimental import pallas as pl
from jax.experimental.pallas import tpu as pltpu
from jax.sharding import PartitionSpec as P

SWEEPS = 3
CAP = 32
LANES = 128
NT = (((1,), (1,)), ((), ()))


def dot_nt(a, b):
    return lax.dot_general(a, b, NT, preferred_element_type=jnp.float32)


def split_3(value):
    high = value.astype(jnp.bfloat16)
    rest = value - high.astype(jnp.float32)
    middle = rest.astype(jnp.bfloat16)
    low = (rest - middle.astype(jnp.float32)).astype(jnp.bfloat16)
    return high, middle, low


def ones_where(mask):
    return jnp.where(mask, 1.0, 0.0).astype(jnp.bfloat16)


def pack_kernel(slabs, vals_ref, slab_ref, cell_ref, out_ref, rows_ref):
    count = vals_ref.shape[1]
    rows_ref[...] = jnp.zeros_like(rows_ref)
    rows_ref[0:6, :] = vals_ref[...]
    rows_ref[6:7, :] = cell_ref[...].astype(jnp.float32)
    target = slab_ref[...]
    member = ones_where(lax.broadcasted_iota(jnp.int32, (slabs, count), 0) == target)
    before = ones_where(
        lax.broadcasted_iota(jnp.int32, (count, count), 0)
        < lax.broadcasted_iota(jnp.int32, (count, count), 1)
    )
    ahead = jnp.dot(member, before, preferred_element_type=jnp.float32)
    rank = jnp.sum(ahead * member.astype(jnp.float32), axis=0, keepdims=True)
    key = (target + 1) * CAP + rank.astype(jnp.int32)
    width = slabs * CAP + LANES
    chosen = ones_where(lax.broadcasted_iota(jnp.int32, (width, count), 0) == key)
    packed = sum(dot_nt(part, chosen) for part in split_3(rows_ref[...]))
    lane = lax.broadcasted_iota(jnp.int32, (8, LANES), 1)
    per_tile = LANES // CAP
    tiles = [packed[:, q * LANES:(q + 1) * LANES] for q in range(width // LANES)]
    for d in range(slabs):
        q, m = divmod(d, per_tile)
        if m == 0:
            out_ref[d] = tiles[q]
        else:
            shift = LANES - m * CAP
            out_ref[d] = jnp.where(
                lane < shift, pltpu.roll(tiles[q], shift, 1), pltpu.roll(tiles[q + 1], shift, 1)
            )


def pack(vals, target, cells, slabs):
    return pl.pallas_call(
        functools.partial(pack_kernel, slabs),
        out_shape=jax.ShapeDtypeStruct((slabs, 8, LANES), jnp.float32),
        scratch_shapes=[pltpu.VMEM((8, vals.shape[1]), jnp.float32)],
        cost_estimate=pl.CostEstimate(flops=20_000_000, bytes_accessed=100_000, transcendentals=0),
        name="pack",
    )(vals, target, cells)


def regroup(got_ref, part):
    lane = lax.broadcasted_iota(jnp.int32, (8, LANES), 1) // CAP
    per_tile = LANES // CAP
    tiles = []
    for first in range(0, got_ref.shape[0], per_tile):
        tile = None
        for j in range(per_tile):
            block = got_ref[first + j]
            shift = (j - part) * CAP % LANES
            if shift:
                block = pltpu.roll(block, shift, 1)
            tile = block if tile is None else jnp.where(lane == j, block, tile)
        tiles.append(tile)
    return jnp.concatenate(tiles, axis=1)


def split_2(value):
    high = value.astype(jnp.bfloat16).astype(jnp.float32)
    return high, value - high


def sweep_kernel(
    slab_count, factor, omega_ref, got_ref, sigma_ref, prev_hbm, fwd_hbm, up_hbm, down_hbm,
    adjoint_hbm, grad_ref,
    field_0, field_1, field_2, field_3, fwd, sig, source, coef_a, coef_b, onehot, sems,
):
    comps, width, ny, nz = field_3.shape
    wide = SWEEPS
    rim = wide - 1
    loads = [
        pltpu.make_async_copy(prev_hbm, field_0.at[:, pl.ds(wide, width)], sems.at[0]),
        pltpu.make_async_copy(fwd_hbm, fwd, sems.at[1]),
        pltpu.make_async_copy(up_hbm.at[pl.ds(0, comps)], field_0.at[:, pl.ds(0, wide)], sems.at[2]),
        pltpu.make_async_copy(down_hbm.at[pl.ds(0, comps)], field_0.at[:, pl.ds(wide + width, wide)], sems.at[3]),
        pltpu.make_async_copy(up_hbm.at[comps], sig.at[pl.ds(0, wide)], sems.at[4]),
        pltpu.make_async_copy(down_hbm.at[comps], sig.at[pl.ds(wide, wide)], sems.at[5]),
    ]
    for load in loads:
        load.start()

    own = regroup(got_ref, 1)
    count = own.shape[1]
    cell = own[6:7].astype(jnp.int32)
    row, z = cell // nz, cell % nz
    at_z = lax.broadcasted_iota(jnp.int32, (nz, count), 0) == z
    for c in range(comps):
        for half, part in enumerate(split_2(own[c:c + 1])):
            onehot[c * nz:(c + 1) * nz, half * count:(half + 1) * count] = jnp.where(at_z, part, 0.0).astype(jnp.bfloat16)
    block = 4
    for first in range(0, width, block):
        at_row = ones_where(lax.broadcasted_iota(jnp.int32, (block * ny, count), 0) + first * ny == row)
        result = dot_nt(jnp.concatenate([at_row, at_row], axis=1), onehot[...])
        for c in range(comps):
            source[c, rim + first:rim + first + block] = result[:, c * nz:(c + 1) * nz].reshape(block, ny, nz)
    for part, first, at in ((0, width - rim, 0), (2, 0, rim + width)):
        side = regroup(got_ref, part)
        cell = side[6:7].astype(jnp.int32)
        row, z = cell // nz - first * ny, cell % nz
        at_z = ones_where(lax.broadcasted_iota(jnp.int32, (nz, count), 0) == z)
        at_row = lax.broadcasted_iota(jnp.int32, (rim * ny, count), 0) == row
        for c in range(comps):
            high, low = split_2(side[c:c + 1])
            result = dot_nt(jnp.where(at_row, high, 0.0).astype(jnp.bfloat16), at_z)
            result += dot_nt(jnp.where(at_row, low, 0.0).astype(jnp.bfloat16), at_z)
            source[c, at:at + rim] = result.reshape(rim, ny, nz)

    omega = omega_ref[0]

    def coefficients(cells):
        beta = omega * cells
        inverse = 1.0 / (36.0 + beta * beta)
        return 6.0 * inverse, beta * inverse

    coef_a[rim:rim + width], coef_b[rim:rim + width] = coefficients(sigma_ref[...])
    for load in loads:
        load.wait()
    me = lax.axis_index("slab")
    for there, first, at in ((me > 0, 1, 0), (me < slab_count - 1, wide, rim + width)):
        inside = jnp.where(there, 1.0, 0.0)
        side_a, side_b = coefficients(sig[first:first + rim])
        coef_a[at:at + rim], coef_b[at:at + rim] = side_a * inside, side_b * inside

    ys = lax.broadcasted_iota(jnp.int32, (ny, nz), 0)
    zs = lax.broadcasted_iota(jnp.int32, (ny, nz), 1)
    first_y, last_y, first_z, last_z = ys == 0, ys == ny - 1, zs == 0, zs == nz - 1

    def beside(field, c, x):
        middle = field[c, x + 1]
        total = field[c, x] + field[c, x + 2]
        total += jnp.where(first_y, 0.0, pltpu.roll(middle, 1, 0)) + jnp.where(last_y, 0.0, pltpu.roll(middle, ny - 1, 0))
        total += jnp.where(first_z, 0.0, pltpu.roll(middle, 1, 1)) + jnp.where(last_z, 0.0, pltpu.roll(middle, nz - 1, 1))
        return total

    def sweep(old, new, layers, skip, last):
        def layer(x, carry):
            a, b = coef_a[x + skip], coef_b[x + skip]
            terms = jnp.zeros((ny, nz), jnp.float32)
            for c in range(comps // 2):
                d = c + comps // 2
                real = source[c, x + skip] + beside(old, c, x)
                imag = source[d, x + skip] + beside(old, d, x)
                real, imag = a * real - b * imag, a * imag + b * real
                new[c, x] = real
                new[d, x] = imag
                if last:
                    terms += fwd[c, x] * imag + fwd[d, x] * real
            if last:
                grad_ref[:, pl.ds(x, 1), :] = (terms * (omega * factor)).reshape(ny, 1, nz)
            return carry
        lax.fori_loop(0, layers, layer, 0)

    sweep(field_0, field_1, width + 4, 0, False)
    sweep(field_1, field_2, width + 2, 1, False)
    sweep(field_2, field_3, width, 2, True)
    store = pltpu.make_async_copy(field_3, adjoint_hbm, sems.at[6])
    store.start()
    store.wait()


def sweeps(omega, got, sigma, prev, fwd, up, down, slab_count, factor):
    comps, width, ny, nz = prev.shape
    f32 = jnp.float32
    count = got.shape[0] * CAP
    hbm = pl.BlockSpec(memory_space=pl.ANY)
    vmem = pl.BlockSpec(memory_space=pltpu.VMEM)
    return pl.pallas_call(
        functools.partial(sweep_kernel, slab_count, factor),
        out_shape=(
            jax.ShapeDtypeStruct(prev.shape, f32),
            jax.ShapeDtypeStruct((ny, width, nz), f32),
        ),
        in_specs=[pl.BlockSpec(memory_space=pltpu.SMEM), vmem, vmem, hbm, hbm, hbm, hbm],
        out_specs=(hbm, vmem),
        scratch_shapes=[
            pltpu.VMEM((comps, width + 6, ny, nz), f32),
            pltpu.VMEM((comps, width + 4, ny, nz), f32),
            pltpu.VMEM((comps, width + 2, ny, nz), f32),
            pltpu.VMEM((comps, width, ny, nz), f32),
            pltpu.VMEM((comps, width, ny, nz), f32),
            pltpu.VMEM((6, ny, nz), f32),
            pltpu.VMEM((comps, width + 4, ny, nz), f32),
            pltpu.VMEM((width + 4, ny, nz), f32),
            pltpu.VMEM((width + 4, ny, nz), f32),
            pltpu.VMEM((comps * nz, 2 * count), jnp.bfloat16),
            pltpu.SemaphoreType.DMA((7,)),
        ],
        compiler_params=pltpu.CompilerParams(vmem_limit_bytes=40 * 1024 * 1024),
        cost_estimate=pl.CostEstimate(flops=1_000_000_000, bytes_accessed=6_000_000, transcendentals=0),
        name="sweeps",
    )(omega, got, sigma, prev, fwd, up, down)


def shards(fwd_field, adj_prev, sigma, omega, res_vals, rec_slab, rec_cell):
    pairs, comps, width, ny, nz = adj_prev.shape
    slabs, groups = lax.axis_size("slab"), lax.axis_size("tx")
    prev, fwd = adj_prev[0], fwd_field[0]
    up = [(i, i + 1) for i in range(slabs - 1)]
    down = [(j, i) for i, j in up]
    highest = jnp.concatenate([prev[:, width - SWEEPS:], sigma[None, width - SWEEPS:]], axis=0)
    lowest = jnp.concatenate([prev[:, :SWEEPS], sigma[None, :SWEEPS]], axis=0)
    from_before = lax.ppermute(highest, "slab", up)
    from_after = lax.ppermute(lowest, "slab", down)
    send = pack(res_vals[0], rec_slab.reshape(1, -1), rec_cell, slabs)
    got = lax.all_to_all(send, "slab", split_axis=0, concat_axis=0, tiled=True)
    factor = 1.0 / (3.0 * pairs * groups) ** 0.5
    adjoint, terms = sweeps(omega, got, sigma, prev, fwd, from_before, from_after, slabs, factor)
    parts = lax.all_to_all(terms, "tx", split_axis=0, concat_axis=0, tiled=True)
    gradient = jnp.sum(parts, axis=0)[:, None, :]
    return (adjoint[None], gradient)


def solution(mesh):
    placed = (
        P("tx", None, "slab", None, None),
        P("tx", None, "slab", None, None),
        P("slab", None, None),
        P("tx"),
        P("tx", None, "slab"),
        P("tx", "slab", None),
        P("tx", "slab"),
    )
    return jax.shard_map(
        shards,
        mesh=mesh,
        in_specs=placed,
        out_specs=(P("tx", None, "slab", None, None), P("slab", "tx", None)),
        check_vma=False,
    )
```

time: 358 us -> 93.1 us (0.26)
  waiting for transfers between devices: 169 us -> 20.5 us
  local copies, waits for them, and re-layouts: 72.5 us -> 4.08 us
  starting transfers between devices: 67.6 us -> 27.2 us
  other arithmetic: 32.5 us -> 0.68 us
  blocking collectives: 0 us -> 24.3 us
  Pallas kernels: 0 us -> 13.8 us
  between operations: 15 us -> 1.38 us
    reduce_scatter x1 -> x0, waiting for transfers between devices: 148 us -> none  [shards(): lax.psum_scatter(partial_grad, 'tx', scatter_dimension=1, tiled=True)]
    scatter x3 -> x0, local copies, waits for them, and re-layouts: 48.2 us -> none  [the longest x1 35.8 us: shards(): send_cells.at[pair_rows, target, slot].set(rec_cell.astype(jnp.float32))]
    ppermute x6 -> x2, starting transfers between devices: 35.8 us -> 10.7 us  [the longest x1 8.76 us: shards(): from_before = lax.ppermute(highest, 'slab', up)]
    all_to_all x0 -> x1, blocking collectives: none -> 24.3 us  [shards(): parts = lax.all_to_all(terms, 'tx', split_axis=0, concat_axis=0, tiled=True)]
    reshape x2 -> x0, local copies, waits for them, and re-layouts: 19.7 us -> none  [the longest x1 19.6 us: shards(): source = source.reshape(pairs, comps, width_x, width_y, width_z)]
    scatter-add x1 -> x0, other arithmetic: 16.5 us -> none  [shards(): source.at[pair_rows, :, where_cells].add(jnp.transpose(arrived, (0, 2, 1)))]
    all_to_all x2 -> x1, starting transfers between devices: 31.8 us -> 16.5 us  [shards(): got = lax.all_to_all(send, 'slab', split_axis=0, concat_axis=0, tiled=True)]
    pallas_call x0 -> x2, Pallas kernels: none -> 13.8 us  [the longest x1 11.8 us: sweeps(): pl.pallas_call(functools.partial(sweep_kernel, slab_count, factor), out_s...]
  transfers between devices with their start and end apart: 9 -> 3, of which waited for: 4 -> 1; matrix products, arithmetic and copies ran while one was open for 15% -> 1% of each run, Pallas kernels for 0% -> 2%
where the time goes in v1:
time: 93.1 us; the launch traced here: 92 us
  starting transfers between devices  27.2 us (29%)
  blocking collectives  24.3 us (26%)
  waiting for transfers between devices  20.5 us (22%)
  Pallas kernels  13.8 us (15%)
  local copies, waits for them, and re-layouts  4.08 us (4%)
  between operations  1.38 us (1%)
    all_to_all x1, blocking collectives, shards(): parts = lax.all_to_all(terms, 'tx', split_axis=0, concat_axis=0, tiled=True)  24.3 us
    all_to_all x1, waiting for transfers between devices, shards(): got = lax.all_to_all(send, 'slab', split_axis=0, concat_axis=0, tiled=True)  20.5 us
    all_to_all x1, starting transfers between devices, shards(): got = lax.all_to_all(send, 'slab', split_axis=0, concat_axis=0, tiled=True)  16.5 us
    pallas_call x1, Pallas kernels, sweeps(): pl.pallas_call(functools.partial(sweep_kernel, slab_count, factor), out_s...  11.8 us
    ppermute x1, starting transfers between devices, shards(): from_before = lax.ppermute(highest, 'slab', up)  8.76 us
    unnamed x9, local copies, waits for them, and re-layouts  2.02 us
    pallas_call x1, Pallas kernels, pack(): pl.pallas_call(functools.partial(pack_kernel, slabs), out_shape=jax.Shape...  1.97 us
    ppermute x1, starting transfers between devices, shards(): from_after = lax.ppermute(lowest, 'slab', down)  1.92 us
  transfers between devices with their start and end apart: 3, of which 1 were waited for; matrix products, arithmetic and copies ran while one was open for 1% of the time, Pallas kernels for 2%

profile of v1, /device:TPU:24, one launch (start us, length us, event | category | flops | bytes accessed | tf_op | source)
XLA Modules:
  0.0 92.0 jit_solution(3015279592391781342)
XLA Ops:
  0.6 0.0 copy-start.2
  0.6 0.0 copy-start
  0.7 0.0 copy-start.3
  0.7 1.0 %slice_bitcast_fusion = (f32[1,3,32,128]{3,2,1,0:T(8,128)S(1)}, f32[1,3,32,128]{3,2,1,0:T(8,128)S(1)}) fusion(f32[16,32,128]{2,1,0:T(8,128)} %sigma_ref.1), kind=kLoop, calls=%fused_computation.2 | loop fusion | bytes 196608 | tf_op jit(solution)/shard_map/broadcast_in_dim | solution.py:232
  1.6 1.1 %fusion = (f32[6,3,32,128]{3,2,1,0:T(8,128)S(1)}, f32[6,3,32,128]{3,2,1,0:T(8,128)S(1)}) fusion(f32[6,16,32,128]{3,2,1,0:T(8,128)} %bitcast.12), kind=kLoop, calls=%fused_computation.5 | loop fusion | bytes 1179648 | tf_op jit(solution)/shard_map/slice | solution.py:232
  2.8 8.8 %collective-permute-start = (f32[7,3,32,128]{3,2,1,0:T(8,128)S(1)}, f32[7,3,32,128]{3,2,1,0:T(8,128)S(1)}, u32[]{:S(2)}, u32[]{:S(2)}) collective-permute-start(f32[7,3,32,128]{3,2,1,0:T(8,128)S(1)} %pad_maximum_fusion), channel_id=1, source_target_pairs={{0,1},{1,2},{2,3},{3,4},{4,5},{5,6},{6,7},{7,8},{8,9},{9,10},{10,1... | collective-permute-start | bytes 1032200 | tf_op jit(solution)/shard_map/ppermute | solution.py:233
  11.6 1.9 %collective-permute-start.1 = (f32[7,3,32,128]{3,2,1,0:T(8,128)S(1)}, f32[7,3,32,128]{3,2,1,0:T(8,128)S(1)}, u32[]{:S(2)}, u32[]{:S(2)}) collective-permute-start(f32[7,3,32,128]{3,2,1,0:T(8,128)S(1)} %pad_maximum_fusion.1), channel_id=1, source_target_pairs={{1,0},{2,1},{3,2},{4,3},{5,4},{6,5},{7,6},{8,7},{9,8},{10,9},{11,1... | collective-permute-start | bytes 1032200 | tf_op jit(solution)/shard_map/ppermute | solution.py:234
  13.5 0.0 copy-done.3
  13.5 0.6 copy.11
  14.1 2.0 %pack.1 = f32[16,8,128]{2,1,0:T(8,128)} custom-call(f32[6,256]{1,0:T(8,128)} %bitcast.15, s32[1,256]{1,0:T(1,128)} %bitcast.17, s32[1,256]{1,0:T(1,128)} %cell_ref.1), custom_call_target="tpu_custom_call" | custom-call | flops 20000000 | bytes 100000 | tf_op jit(solution)/shard_map/pack/pallas_call | solution.py:64
  16.1 16.5 %all-to-all-start = ((f32[16,8,128]{2,1,0:T(8,128)}), f32[16,8,128]{2,1,0:T(8,128)S(1)}, u32[]{:S(2)}, u32[]{:S(2)}) async-start(f32[16,8,128]{2,1,0:T(8,128)} %pack.1), calls=%async_computation | async-start | bytes 131072 | tf_op jit(solution)/shard_map/all_to_all | solution.py:236
  33.2 20.5 %all-to-all-done.got_ref = f32[16,8,128]{2,1,0:T(8,128)S(1)} async-done(((f32[16,8,128]{2,1,0:T(8,128)}), f32[16,8,128]{2,1,0:T(8,128)S(1)}, u32[]{:S(2)}, u32[]{:S(2)}) %all-to-all-start) | async-done | bytes 65568 | tf_op jit(solution)/shard_map/all_to_all | solution.py:236
  53.7 0.0 collective-permute-done.up_hbm
  53.7 0.0 collective-permute-done.1.down_hbm
  53.8 0.0 copy-done.2
  53.8 0.0 copy-done
  53.8 0.0 copy-start.1
  53.8 1.4 %copy-done.1 = f32[1,6,16,32,128]{4,3,2,1,0:T(8,128)S(1)} copy-done((f32[1,6,16,32,128]{4,3,2,1,0:T(8,128)S(1)}, f32[1,6,16,32,128]{4,3,2,1,0:T(8,128)}, u32[]{:S(2)}) %copy-start.1) | copy-done | bytes 1572888
  55.2 11.8 %sweeps.1 = (f32[6,16,32,128]{3,2,1,0:T(8,128)}, f32[32,16,128]{2,1,0:T(8,128)S(1)}) custom-call(f32[1]{0:T(128)S(6)} %copy.12.omega_ref, f32[16,8,128]{2,1,0:T(8,128)S(1)} %all-to-all-done.got_ref, f32[16,32,128]{2,1,0:T(8,128)S(1)} %copy-done.2, f32[6,16,32,128]{3,2,1,0:T(8,128)S(1)} %bitcast.13, f32[6,16,32,128]{3,2,1,0:T(8,128)S(1)} %bitcast.14, ...), custom_call_target="tpu_custom_call" | custom-call | flops 1000000000 | bytes 6000000 | tf_op jit(solution)/shard_map/sweeps/pallas_call | solution.py:198
  67.0 24.3 %all_to_all.10 = f32[32,16,128]{2,1,0:T(8,128)S(1)} all-to-all(f32[32,16,128]{2,1,0:T(8,128)S(1)} %get-tuple-element.5), channel_id=1, replica_groups=mesh['tx'=32,'slab'=16] {'tx'}, dimensions={0} | all-to-all | bytes 524288 | tf_op jit(solution)/shard_map/all_to_all | solution.py:239
  91.3 0.6 reduce_sum.9
  (2 shorter events, 0.0 us)
Async XLA Ops:
  0.6 53.1 %copy-start.2 = (f32[16,32,128]{2,1,0:T(8,128)S(1)}, f32[16,32,128]{2,1,0:T(8,128)}, u32[]{:S(2)}) copy-start(f32[16,32,128]{2,1,0:T(8,128)} %sigma_ref.1) | copy-start | bytes 786436
  0.6 53.1 %copy-start = (f32[1,6,16,32,128]{4,3,2,1,0:T(8,128)S(1)}, f32[1,6,16,32,128]{4,3,2,1,0:T(8,128)}, u32[]{:S(2)}) copy-start(f32[1,6,16,32,128]{4,3,2,1,0:T(8,128)} %param.8) | copy-start | bytes 4718596
  0.7 12.8 %copy-start.3 = (f32[1,6,256]{2,0,1:T(1,128)S(1)}, f32[1,6,256]{2,0,1:T(1,128)}, u32[]{:S(2)}) copy-start(f32[1,6,256]{2,0,1:T(1,128)} %param.11) | copy-start | bytes 18436
  2.8 51.0 %collective-permute-start = (f32[7,3,32,128]{3,2,1,0:T(8,128)S(1)}, f32[7,3,32,128]{3,2,1,0:T(8,128)S(1)}, u32[]{:S(2)}, u32[]{:S(2)}) collective-permute-start(f32[7,3,32,128]{3,2,1,0:T(8,128)S(1)} %pad_maximum_fusion), channel_id=1, source_target_pairs={{0,1},{1,2},{2,3},{3,4},{4,5},{5,6},{6,7},{7,8},{8,9},{9,10},{10,1... | collective-permute-start | bytes 1032200 | tf_op jit(solution)/shard_map/ppermute | solution.py:233
  11.6 42.2 %collective-permute-start.1 = (f32[7,3,32,128]{3,2,1,0:T(8,128)S(1)}, f32[7,3,32,128]{3,2,1,0:T(8,128)S(1)}, u32[]{:S(2)}, u32[]{:S(2)}) collective-permute-start(f32[7,3,32,128]{3,2,1,0:T(8,128)S(1)} %pad_maximum_fusion.1), channel_id=1, source_target_pairs={{1,0},{2,1},{3,2},{4,3},{5,4},{6,5},{7,6},{8,7},{9,8},{10,9},{11,1... | collective-permute-start | bytes 1032200 | tf_op jit(solution)/shard_map/ppermute | solution.py:234
  16.1 37.7 %all-to-all-start = ((f32[16,8,128]{2,1,0:T(8,128)}), f32[16,8,128]{2,1,0:T(8,128)S(1)}, u32[]{:S(2)}, u32[]{:S(2)}) async-start(f32[16,8,128]{2,1,0:T(8,128)} %pack.1), calls=%async_computation | async-start | bytes 131072 | tf_op jit(solution)/shard_map/all_to_all | solution.py:236
  53.8 1.4 %copy-start.1 = (f32[1,6,16,32,128]{4,3,2,1,0:T(8,128)S(1)}, f32[1,6,16,32,128]{4,3,2,1,0:T(8,128)}, u32[]{:S(2)}) copy-start(f32[1,6,16,32,128]{4,3,2,1,0:T(8,128)} %param.7) | copy-start | bytes 4718596

commit v2 on v1

--- a/solution.py
+++ b/solution.py
@@ -10,6 +10,7 @@
 SWEEPS = 3
 CAP = 32
 LANES = 128
+COLUMNS = 4
 NT = (((1,), (1,)), ((), ()))
 
 
@@ -91,24 +92,37 @@
     return high, value - high
 
 
-def sweep_kernel(
-    slab_count, factor, omega_ref, got_ref, sigma_ref, prev_hbm, fwd_hbm, up_hbm, down_hbm,
-    adjoint_hbm, grad_ref,
-    field_0, field_1, field_2, field_3, fwd, sig, source, coef_a, coef_b, onehot, sems,
+def coefficients(omega, cells):
+    beta = omega * cells
+    inverse = 1.0 / (36.0 + beta * beta)
+    return 6.0 * inverse, beta * inverse
+
+
+def neighbour_sum(ny, nz):
+    ys = lax.broadcasted_iota(jnp.int32, (ny, nz), 0)
+    zs = lax.broadcasted_iota(jnp.int32, (ny, nz), 1)
+    first_y, last_y, first_z, last_z = ys == 0, ys == ny - 1, zs == 0, zs == nz - 1
+
+    def beside(before, middle, after):
+        total = before + after
+        total += jnp.where(first_y, 0.0, pltpu.roll(middle, 1, 0)) + jnp.where(last_y, 0.0, pltpu.roll(middle, ny - 1, 0))
+        total += jnp.where(first_z, 0.0, pltpu.roll(middle, 1, 1)) + jnp.where(last_z, 0.0, pltpu.roll(middle, nz - 1, 1))
+        return total
+
+    return beside
+
+
+def inner_kernel(
+    factor, omega_ref, got_ref, sigma_ref, prev_hbm, fwd_hbm,
+    adjoint_hbm, grad_ref, field_1_hbm, field_2_hbm, source_hbm, coef_hbm,
+    field_0, field_1, field_2, field_3, fwd, source, coef, onehot, sems,
 ):
-    comps, width, ny, nz = field_3.shape
-    wide = SWEEPS
-    rim = wide - 1
-    loads = [
-        pltpu.make_async_copy(prev_hbm, field_0.at[:, pl.ds(wide, width)], sems.at[0]),
-        pltpu.make_async_copy(fwd_hbm, fwd, sems.at[1]),
-        pltpu.make_async_copy(up_hbm.at[pl.ds(0, comps)], field_0.at[:, pl.ds(0, wide)], sems.at[2]),
-        pltpu.make_async_copy(down_hbm.at[pl.ds(0, comps)], field_0.at[:, pl.ds(wide + width, wide)], sems.at[3]),
-        pltpu.make_async_copy(up_hbm.at[comps], sig.at[pl.ds(0, wide)], sems.at[4]),
-        pltpu.make_async_copy(down_hbm.at[comps], sig.at[pl.ds(wide, wide)], sems.at[5]),
-    ]
-    for load in loads:
-        load.start()
+    comps, width, ny, nz = field_0.shape
+    rim = SWEEPS - 1
+    load_prev = pltpu.make_async_copy(prev_hbm, field_0, sems.at[0])
+    load_fwd = pltpu.make_async_copy(fwd_hbm, fwd, sems.at[1])
+    load_prev.start()
+    load_fwd.start()
 
     own = regroup(got_ref, 1)
     count = own.shape[1]
@@ -137,105 +151,224 @@
             source[c, at:at + rim] = result.reshape(rim, ny, nz)
 
     omega = omega_ref[0]
-
-    def coefficients(cells):
-        beta = omega * cells
-        inverse = 1.0 / (36.0 + beta * beta)
-        return 6.0 * inverse, beta * inverse
-
-    coef_a[rim:rim + width], coef_b[rim:rim + width] = coefficients(sigma_ref[...])
-    for load in loads:
-        load.wait()
-    me = lax.axis_index("slab")
-    for there, first, at in ((me > 0, 1, 0), (me < slab_count - 1, wide, rim + width)):
-        inside = jnp.where(there, 1.0, 0.0)
-        side_a, side_b = coefficients(sig[first:first + rim])
-        coef_a[at:at + rim], coef_b[at:at + rim] = side_a * inside, side_b * inside
-
-    ys = lax.broadcasted_iota(jnp.int32, (ny, nz), 0)
-    zs = lax.broadcasted_iota(jnp.int32, (ny, nz), 1)
-    first_y, last_y, first_z, last_z = ys == 0, ys == ny - 1, zs == 0, zs == nz - 1
-
-    def beside(field, c, x):
-        middle = field[c, x + 1]
-        total = field[c, x] + field[c, x + 2]
-        total += jnp.where(first_y, 0.0, pltpu.roll(middle, 1, 0)) + jnp.where(last_y, 0.0, pltpu.roll(middle, ny - 1, 0))
-        total += jnp.where(first_z, 0.0, pltpu.roll(middle, 1, 1)) + jnp.where(last_z, 0.0, pltpu.roll(middle, nz - 1, 1))
-        return total
-
-    def sweep(old, new, layers, skip, last):
-        def layer(x, carry):
-            a, b = coef_a[x + skip], coef_b[x + skip]
+    coef[0], coef[1] = coefficients(omega, sigma_ref[...])
+    beside = neighbour_sum(ny, nz)
+    load_prev.wait()
+    load_fwd.wait()
+
+    def sweep(old, new, first, last):
+        def layer(i, carry):
+            x = i + first
+            a, b = coef[0, x], coef[1, x]
             terms = jnp.zeros((ny, nz), jnp.float32)
             for c in range(comps // 2):
                 d = c + comps // 2
-                real = source[c, x + skip] + beside(old, c, x)
-                imag = source[d, x + skip] + beside(old, d, x)
+                real = source[c, x + rim] + beside(old[c, i], old[c, i + 1], old[c, i + 2])
+                imag = source[d, x + rim] + beside(old[d, i], old[d, i + 1], old[d, i + 2])
                 real, imag = a * real - b * imag, a * imag + b * real
-                new[c, x] = real
-                new[d, x] = imag
+                new[c, i] = real
+                new[d, i] = imag
                 if last:
                     terms += fwd[c, x] * imag + fwd[d, x] * real
             if last:
                 grad_ref[:, pl.ds(x, 1), :] = (terms * (omega * factor)).reshape(ny, 1, nz)
             return carry
-        lax.fori_loop(0, layers, layer, 0)
-
-    sweep(field_0, field_1, width + 4, 0, False)
-    sweep(field_1, field_2, width + 2, 1, False)
-    sweep(field_2, field_3, width, 2, True)
-    store = pltpu.make_async_copy(field_3, adjoint_hbm, sems.at[6])
-    store.start()
-    store.wait()
-
-
-def sweeps(omega, got, sigma, prev, fwd, up, down, slab_count, factor):
+        lax.fori_loop(0, new.shape[1], layer, 0)
+
+    grad_ref[...] = jnp.zeros_like(grad_ref)
+    sweep(field_0, field_1, 1, False)
+    sweep(field_1, field_2, 2, False)
+    sweep(field_2, field_3, 3, True)
+    stores = [pltpu.make_async_copy(field_3, adjoint_hbm.at[:, pl.ds(3, width - 6)], sems.at[2])]
+    for s in range(2):
+        pairs = (
+            (field_1.at[:, pl.ds(s * (width - 4), 2)], field_1_hbm.at[s]),
+            (field_2.at[:, pl.ds(s * (width - 6), 2)], field_2_hbm.at[s]),
+            (source.at[:, pl.ds(s * (width - 1), 5)], source_hbm.at[s]),
+            (coef.at[:, pl.ds(s * (width - 3), 3)], coef_hbm.at[s]),
+        )
+        stores += [pltpu.make_async_copy(src, dst, sems.at[3 + 4 * s + n]) for n, (src, dst) in enumerate(pairs)]
+    for store in stores:
+        store.start()
+    for store in stores:
+        store.wait()
+
+
+def inner(omega, got, sigma, prev, fwd, factor):
     comps, width, ny, nz = prev.shape
     f32 = jnp.float32
     count = got.shape[0] * CAP
     hbm = pl.BlockSpec(memory_space=pl.ANY)
     vmem = pl.BlockSpec(memory_space=pltpu.VMEM)
+    cells = (ny, nz)
     return pl.pallas_call(
-        functools.partial(sweep_kernel, slab_count, factor),
-        out_shape=(
-            jax.ShapeDtypeStruct(prev.shape, f32),
-            jax.ShapeDtypeStruct((ny, width, nz), f32),
-        ),
-        in_specs=[pl.BlockSpec(memory_space=pltpu.SMEM), vmem, vmem, hbm, hbm, hbm, hbm],
+        functools.partial(inner_kernel, factor),
+        out_shape=[jax.ShapeDtypeStruct(shape, f32) for shape in (
+            prev.shape, (ny, width, nz), (2, comps, 2) + cells, (2, comps, 2) + cells, (2, comps, 5) + cells, (2, 2, 3) + cells,
+        )],
+        in_specs=[pl.BlockSpec(memory_space=pltpu.SMEM), vmem, vmem, hbm, hbm],
+        out_specs=[hbm, vmem, hbm, hbm, hbm, hbm],
+        scratch_shapes=[
+            pltpu.VMEM((comps, width) + cells, f32),
+            pltpu.VMEM((comps, width - 2) + cells, f32),
+            pltpu.VMEM((comps, width - 4) + cells, f32),
+            pltpu.VMEM((comps, width - 6) + cells, f32),
+            pltpu.VMEM((comps, width) + cells, f32),
+            pltpu.VMEM((comps, width + 4) + cells, f32),
+            pltpu.VMEM((2, width) + cells, f32),
+            pltpu.VMEM((comps * nz, 2 * count), jnp.bfloat16),
+            pltpu.SemaphoreType.DMA((11,)),
+        ],
+        compiler_params=pltpu.CompilerParams(vmem_limit_bytes=40 * 1024 * 1024),
+        cost_estimate=pl.CostEstimate(flops=10_000_000_000, bytes_accessed=30_000_000, transcendentals=0),
+        name="inner",
+    )(omega, got, sigma, prev, fwd)
+
+
+def outer_kernel(
+    slab_count, factor, omega_ref, inner_grad_ref, prev_hbm, fwd_hbm, before_hbm, after_hbm, direct_hbm, staged_hbm,
+    field_1_hbm, field_2_hbm, source_hbm, coef_hbm, inner_adjoint_hbm,
+    adjoint_hbm, grad_ref,
+    field_0, field_1, field_2, field_3, fwd, sig, source, coef, sems, halo_sems,
+):
+    comps, width, ny, nz = prev_hbm.shape
+    me = lax.axis_index("slab")
+    column = me % COLUMNS
+    loads = []
+    for s in range(2):
+        pairs = (
+            (prev_hbm.at[:, pl.ds(s * (width - 2), 2)], field_0.at[s, :, pl.ds(3 - 3 * s, 2)]),
+            (fwd_hbm.at[:, pl.ds(s * (width - 3), 3)], fwd.at[s]),
+            (field_1_hbm.at[s], field_1.at[s, :, pl.ds(3 - 3 * s, 2)]),
+            (field_2_hbm.at[s], field_2.at[s, :, pl.ds(3 - 3 * s, 2)]),
+            (source_hbm.at[s], source.at[s]),
+            (coef_hbm.at[s], coef.at[s, :, pl.ds(2 - 2 * s, 3)]),
+        )
+        loads += [pltpu.make_async_copy(src, dst, sems.at[6 * s + n]) for n, (src, dst) in enumerate(pairs)]
+    split = direct_hbm.shape[0]
+    for s, (near, far) in enumerate(((before_hbm, 0), (after_hbm, COLUMNS - 1))):
+        spot = pl.ds(2 * s, 3)
+        at_edge = column == far
+
+        @pl.when(at_edge)
+        def _():
+            pltpu.make_async_copy(direct_hbm, field_0.at[s, pl.ds(0, split), spot], halo_sems.at[s, 0]).start()
+            pltpu.make_async_copy(staged_hbm.at[pl.ds(0, comps - split)], field_0.at[s, pl.ds(split, comps - split), spot], halo_sems.at[s, 1]).start()
+            pltpu.make_async_copy(staged_hbm.at[comps - split], sig.at[s], halo_sems.at[s, 2]).start()
+
+        @pl.when(jnp.logical_not(at_edge))
+        def _():
+            pltpu.make_async_copy(near.at[pl.ds(0, split)], field_0.at[s, pl.ds(0, split), spot], halo_sems.at[s, 0]).start()
+            pltpu.make_async_copy(near.at[pl.ds(split, comps - split)], field_0.at[s, pl.ds(split, comps - split), spot], halo_sems.at[s, 1]).start()
+            pltpu.make_async_copy(near.at[comps], sig.at[s], halo_sems.at[s, 2]).start()
+
+        loads_of_side = (
+            pltpu.make_async_copy(near.at[pl.ds(0, split)], field_0.at[s, pl.ds(0, split), spot], halo_sems.at[s, 0]),
+            pltpu.make_async_copy(near.at[pl.ds(split, comps - split)], field_0.at[s, pl.ds(split, comps - split), spot], halo_sems.at[s, 1]),
+            pltpu.make_async_copy(near.at[comps], sig.at[s], halo_sems.at[s, 2]),
+        )
+        if s == 0:
+            waits = list(loads_of_side)
+        else:
+            waits += loads_of_side
+    for load in loads:
+        load.start()
+    grad_ref[...] = inner_grad_ref[...]
+    for load in waits + loads:
+        load.wait()
+    omega = omega_ref[0]
+    for s, there in ((0, me > 0), (1, me < slab_count - 1)):
+        inside = jnp.where(there, 1.0, 0.0)
+        a, b = coefficients(omega, sig[s, 1 - s:3 - s])
+        coef[s, 0, 3 * s:3 * s + 2], coef[s, 1, 3 * s:3 * s + 2] = a * inside, b * inside
+
+    beside = neighbour_sum(ny, nz)
+
+    def sweep(old, new, number):
+        def layer(k, carry):
+            for s in range(2):
+                at = k + (number if s == 0 else 2 - number)
+                a, b = coef[s, 0, at], coef[s, 1, at]
+                terms = jnp.zeros((ny, nz), jnp.float32)
+                for c in range(comps // 2):
+                    d = c + comps // 2
+                    real = source[s, c, at] + beside(old[s, c, k], old[s, c, k + 1], old[s, c, k + 2])
+                    imag = source[s, d, at] + beside(old[s, d, k], old[s, d, k + 1], old[s, d, k + 2])
+                    real, imag = a * real - b * imag, a * imag + b * real
+                    to = k if number == 2 else k + 2 * s
+                    new[s, c, to] = real
+                    new[s, d, to] = imag
+                    if number == 2:
+                        terms += fwd[s, c, k] * imag + fwd[s, d, k] * real
+                if number == 2:
+                    grad_ref[:, pl.ds(k + s * (width - 3), 1), :] = (terms * (omega * factor)).reshape(ny, 1, nz)
+            return carry
+        lax.fori_loop(0, 3, layer, 0)
+
+    sweep(field_0, field_1, 0)
+    sweep(field_1, field_2, 1)
+    sweep(field_2, field_3, 2)
+    stores = [pltpu.make_async_copy(field_3.at[s], adjoint_hbm.at[:, pl.ds(s * (width - 3), 3)], sems.at[6 * s]) for s in range(2)]
+    for store in stores:
+        store.start()
+    for store in stores:
+        store.wait()
+
+
+def outer(omega, grad, prev, fwd, halos, from_inner, adjoint, slab_count, factor):
+    comps, width, ny, nz = prev.shape
+    f32 = jnp.float32
+    hbm = pl.BlockSpec(memory_space=pl.ANY)
+    vmem = pl.BlockSpec(memory_space=pltpu.VMEM)
+    cells = (ny, nz)
+    return pl.pallas_call(
+        functools.partial(outer_kernel, slab_count, factor),
+        out_shape=(jax.ShapeDtypeStruct(prev.shape, f32), jax.ShapeDtypeStruct(grad.shape, f32)),
+        in_specs=[pl.BlockSpec(memory_space=pltpu.SMEM), vmem] + [hbm] * 11,
         out_specs=(hbm, vmem),
         scratch_shapes=[
-            pltpu.VMEM((comps, width + 6, ny, nz), f32),
-            pltpu.VMEM((comps, width + 4, ny, nz), f32),
-            pltpu.VMEM((comps, width + 2, ny, nz), f32),
-            pltpu.VMEM((comps, width, ny, nz), f32),
-            pltpu.VMEM((comps, width, ny, nz), f32),
-            pltpu.VMEM((6, ny, nz), f32),
-            pltpu.VMEM((comps, width + 4, ny, nz), f32),
-            pltpu.VMEM((width + 4, ny, nz), f32),
-            pltpu.VMEM((width + 4, ny, nz), f32),
-            pltpu.VMEM((comps * nz, 2 * count), jnp.bfloat16),
-            pltpu.SemaphoreType.DMA((7,)),
+            pltpu.VMEM((2, comps, 5) + cells, f32),
+            pltpu.VMEM((2, comps, 5) + cells, f32),
+            pltpu.VMEM((2, comps, 5) + cells, f32),
+            pltpu.VMEM((2, comps, 3) + cells, f32),
+            pltpu.VMEM((2, comps, 3) + cells, f32),
+            pltpu.VMEM((2, 3) + cells, f32),
+            pltpu.VMEM((2, comps, 5) + cells, f32),
+            pltpu.VMEM((2, 2, 5) + cells, f32),
+            pltpu.SemaphoreType.DMA((12,)),
+            pltpu.SemaphoreType.DMA((2, 3)),
         ],
-        compiler_params=pltpu.CompilerParams(vmem_limit_bytes=40 * 1024 * 1024),
-        cost_estimate=pl.CostEstimate(flops=1_000_000_000, bytes_accessed=6_000_000, transcendentals=0),
-        name="sweeps",
-    )(omega, got, sigma, prev, fwd, up, down)
+        input_output_aliases={12: 0},
+        compiler_params=pltpu.CompilerParams(vmem_limit_bytes=24 * 1024 * 1024),
+        cost_estimate=pl.CostEstimate(flops=100_000_000, bytes_accessed=3_000_000, transcendentals=0),
+        name="outer",
+    )(omega, grad, prev, fwd, *halos, *from_inner, adjoint)
 
 
 def shards(fwd_field, adj_prev, sigma, omega, res_vals, rec_slab, rec_cell):
     pairs, comps, width, ny, nz = adj_prev.shape
     slabs, groups = lax.axis_size("slab"), lax.axis_size("tx")
     prev, fwd = adj_prev[0], fwd_field[0]
-    up = [(i, i + 1) for i in range(slabs - 1)]
-    down = [(j, i) for i, j in up]
+    ring = [(i, i + 1 if (i + 1) % COLUMNS else i + 1 - COLUMNS) for i in range(slabs)]
+    crossing = [(i, i + 1) for i in range(COLUMNS - 1, slabs - 1, COLUMNS)]
+    straight = [(i, i + COLUMNS) for i in range(0, slabs - COLUMNS, COLUMNS)]
+    straight += [(i + COLUMNS, i) for i in range(COLUMNS - 1, slabs - COLUMNS, COLUMNS)]
+    column = lax.axis_index("slab") % COLUMNS
     highest = jnp.concatenate([prev[:, width - SWEEPS:], sigma[None, width - SWEEPS:]], axis=0)
     lowest = jnp.concatenate([prev[:, :SWEEPS], sigma[None, :SWEEPS]], axis=0)
-    from_before = lax.ppermute(highest, "slab", up)
-    from_after = lax.ppermute(lowest, "slab", down)
+    before = lax.ppermute(highest, "slab", ring)
+    after = lax.ppermute(lowest, "slab", [(j, i) for i, j in ring])
+    split = 4
+    direct = lax.ppermute(
+        jnp.where(column == COLUMNS - 1, highest[:split], lowest[:split]), "slab", crossing + [(j, i) for i, j in crossing]
+    )
+    staged = lax.ppermute(jnp.where(column == 0, before[split:], after[split:]), "slab", straight)
     send = pack(res_vals[0], rec_slab.reshape(1, -1), rec_cell, slabs)
     got = lax.all_to_all(send, "slab", split_axis=0, concat_axis=0, tiled=True)
     factor = 1.0 / (3.0 * pairs * groups) ** 0.5
-    adjoint, terms = sweeps(omega, got, sigma, prev, fwd, from_before, from_after, slabs, factor)
+    adjoint, terms, *from_inner = inner(omega, got, sigma, prev, fwd, factor)
+    halos = (before, after, direct, staged)
+    adjoint, terms = outer(omega, terms, prev, fwd, halos, from_inner, adjoint, slabs, factor)
     parts = lax.all_to_all(terms, "tx", split_axis=0, concat_axis=0, tiled=True)
     gradient = jnp.sum(parts, axis=0)[:, None, :]
     return (adjoint[None], gradient)

time: 93.1 us -> 81.8 us (0.88)
  waiting for transfers between devices: 20.5 us -> 8.34 us
  blocking collectives: 24.3 us -> 15.6 us
  starting transfers between devices: 27.2 us -> 32.3 us
  other arithmetic: 0.68 us -> 4.43 us
  Pallas kernels: 13.8 us -> 15.1 us
    all_to_all x1, waiting for transfers between devices: 20.5 us -> 1.46 us  [shards(): got = lax.all_to_all(send, 'slab', split_axis=0, concat_axis=0, tiled=True)]
    all_to_all x1, blocking collectives: 24.3 us -> 15.6 us  [shards(): parts = lax.all_to_all(terms, 'tx', split_axis=0, concat_axis=0, tiled=True)]
    ppermute x2 -> x4, starting transfers between devices: 10.7 us -> 17.9 us  [the longest x1 7.49 us: shards(): before = lax.ppermute(highest, 'slab', ring)]
    ppermute x2 -> x4, waiting for transfers between devices: 0.01 us -> 6.88 us  [the longest x1 4.65 us: shards(): lax.ppermute(jnp.where(column == COLUMNS - 1, highest[:split], lowest[:sp...]
    select_n x0 -> x2, other arithmetic: none -> 2.29 us  [the longest x1 1.58 us: shards(): jnp.where(column == 0, before[split:], after[split:])]
    all_to_all x1, starting transfers between devices: 16.5 us -> 14.4 us  [shards(): got = lax.all_to_all(send, 'slab', split_axis=0, concat_axis=0, tiled=True)]
    pallas_call x1 -> x2, Pallas kernels: 11.8 us -> 13.1 us  [the longest x1 9.19 us: inner(): pl.pallas_call(functools.partial(inner_kernel, factor), out_shape=[jax.Sh...]
  transfers between devices with their start and end apart: 3 -> 5, of which waited for: 1 -> 3; matrix products, arithmetic and copies ran while one was open for 1% -> 5% of each run, Pallas kernels for 2% -> 14%
where the time goes in v2:
time: 81.8 us; the launch traced here: 80.8 us
  starting transfers between devices  32.3 us (39%)
  blocking collectives  15.6 us (19%)
  Pallas kernels  15.1 us (18%)
  waiting for transfers between devices  8.34 us (10%)
  other arithmetic  4.43 us (5%)
  local copies, waits for them, and re-layouts  3.61 us (4%)
  between operations  1.39 us (2%)
    all_to_all x1, blocking collectives, shards(): parts = lax.all_to_all(terms, 'tx', split_axis=0, concat_axis=0, tiled=True)  15.6 us
    all_to_all x1, starting transfers between devices, shards(): got = lax.all_to_all(send, 'slab', split_axis=0, concat_axis=0, tiled=True)  14.4 us
    pallas_call x1, Pallas kernels, inner(): pl.pallas_call(functools.partial(inner_kernel, factor), out_shape=[jax.Sh...  9.19 us
    ppermute x1, starting transfers between devices, shards(): before = lax.ppermute(highest, 'slab', ring)  7.49 us
    ppermute x1, starting transfers between devices, shards(): lax.ppermute(jnp.where(column == COLUMNS - 1, highest[:split], lowest[:sp...  7.27 us
    ppermute x1, waiting for transfers between devices, shards(): lax.ppermute(jnp.where(column == COLUMNS - 1, highest[:split], lowest[:sp...  4.65 us
    pallas_call x1, Pallas kernels, outer(): pl.pallas_call(functools.partial(outer_kernel, slab_count, factor), out_s...  3.92 us
    ppermute x1, waiting for transfers between devices, shards(): lax.ppermute(jnp.where(column == 0, before[split:], after[split:]), 'slab...  2.23 us
  transfers between devices with their start and end apart: 5, of which 3 were waited for; matrix products, arithmetic and copies ran while one was open for 5% of the time, Pallas kernels for 14%

profile of v2, /device:TPU:24, one launch (start us, length us, event | category | flops | bytes accessed | tf_op | source)
XLA Modules:
  0.0 80.8 jit_solution(2627938322810242284)
XLA Ops:
  0.6 0.0 copy-start
  0.6 0.0 copy-start.3
  0.7 1.0 %slice_bitcast_fusion = (f32[1,3,32,128]{3,2,1,0:T(8,128)S(1)}, f32[1,3,32,128]{3,2,1,0:T(8,128)S(1)}) fusion(f32[16,32,128]{2,1,0:T(8,128)} %sigma_ref.1), kind=kLoop, calls=%fused_computation.4 | loop fusion | bytes 196608 | tf_op jit(solution)/shard_map/broadcast_in_dim | solution.py:358
  1.6 1.1 %fusion = (f32[6,3,32,128]{3,2,1,0:T(8,128)S(1)}, f32[6,3,32,128]{3,2,1,0:T(8,128)S(1)}) fusion(f32[6,16,32,128]{3,2,1,0:T(8,128)} %bitcast.12), kind=kLoop, calls=%fused_computation.7 | loop fusion | bytes 1179648 | tf_op jit(solution)/shard_map/slice | solution.py:358
  2.7 0.0 copy-start.1
  2.7 0.8 pad_maximum_fusion
  3.5 7.5 %collective-permute-start = (f32[7,3,32,128]{3,2,1,0:T(8,128)}, f32[7,3,32,128]{3,2,1,0:T(8,128)S(1)}, u32[]{:S(2)}, u32[]{:S(2)}) collective-permute-start(f32[7,3,32,128]{3,2,1,0:T(8,128)} %pad_maximum_fusion), channel_id=1, source_target_pairs={{0,1},{1,2},{2,3},{3,0},{4,5},{5,6},{6,7},{7,4},{8,9},{9,10},{10,1... | collective-permute-start | bytes 1032200 | tf_op jit(solution)/shard_map/ppermute | solution.py:359
  11.0 0.8 pad_maximum_fusion.1
  11.7 1.9 %collective-permute-start.1 = (f32[7,3,32,128]{3,2,1,0:T(8,128)}, f32[7,3,32,128]{3,2,1,0:T(8,128)}, u32[]{:S(2)}, u32[]{:S(2)}) collective-permute-start(f32[7,3,32,128]{3,2,1,0:T(8,128)} %pad_maximum_fusion.1), channel_id=1, source_target_pairs={{1,0},{2,1},{3,2},{0,3},{5,4},{6,5},{7,6},{4,7},{9,8},{10,9},{11,1... | collective-permute-start | bytes 1032200 | tf_op jit(solution)/shard_map/ppermute | solution.py:360
  13.6 0.0 copy-done.3
  13.6 0.6 copy.12
  14.2 2.0 %pack.1 = f32[16,8,128]{2,1,0:T(8,128)} custom-call(f32[6,256]{1,0:T(8,128)} %bitcast.19, s32[1,256]{1,0:T(1,128)} %bitcast.21, s32[1,256]{1,0:T(1,128)} %cell_ref.1), custom_call_target="tpu_custom_call" | custom-call | flops 20000000 | bytes 100000 | tf_op jit(solution)/shard_map/pack/pallas_call | solution.py:65
  16.2 14.4 %all-to-all-start = ((f32[16,8,128]{2,1,0:T(8,128)}), f32[16,8,128]{2,1,0:T(8,128)S(1)}, u32[]{:S(2)}, u32[]{:S(2)}) async-start(f32[16,8,128]{2,1,0:T(8,128)} %pack.1), calls=%async_computation | async-start | bytes 131072 | tf_op jit(solution)/shard_map/all_to_all | solution.py:367
  30.6 0.0 copy-done
  30.6 0.7 slice_select_fusion
  31.3 7.3 %collective-permute-start.2 = (f32[4,3,32,128]{3,2,1,0:T(8,128)}, f32[4,3,32,128]{3,2,1,0:T(8,128)}, u32[]{:S(2)}, u32[]{:S(2)}) collective-permute-start(f32[4,3,32,128]{3,2,1,0:T(8,128)} %slice_select_fusion), channel_id=1, source_target_pairs={{3,4},{7,8},{11,12},{4,3},{8,7},{12,11},{19,20},{23,24},{27,28},{2... | collective-permute-start | bytes 589832 | tf_op jit(solution)/shard_map/ppermute | solution.py:362
  39.2 0.0 collective-permute-done.before_hbm
  39.2 0.0 collective-permute-done.1.after_hbm
  39.3 1.6 %slice_select_fusion.1 = f32[3,3,32,128]{3,2,1,0:T(8,128)} fusion(f32[7,3,32,128]{3,2,1,0:T(8,128)} %collective-permute-done.1.after_hbm, f32[7,3,32,128]{3,2,1,0:T(8,128)S(1)} %collective-permute-done.before_hbm, pred[]{:T(512)S(6)} %eq.9), kind=kLoop, calls=%fused_computation.3 | loop fusion | flops 36864 | bytes 442369 | tf_op jit(solution)/shard_map/jit(_where)/select_n | solution.py:365
  40.8 1.3 %collective-permute-start.3 = (f32[3,3,32,128]{3,2,1,0:T(8,128)}, f32[3,3,32,128]{3,2,1,0:T(8,128)}, u32[]{:S(2)}, u32[]{:S(2)}) collective-permute-start(f32[3,3,32,128]{3,2,1,0:T(8,128)} %slice_select_fusion.1), channel_id=1, source_target_pairs={{0,4},{4,8},{8,12},{7,3},{11,7},{15,11},{16,20},{20,24},{24,28},{2... | collective-permute-start | bytes 442376 | tf_op jit(solution)/shard_map/ppermute | solution.py:365
  42.1 1.5 %all-to-all-done.got_ref = f32[16,8,128]{2,1,0:T(8,128)S(1)} async-done(((f32[16,8,128]{2,1,0:T(8,128)}), f32[16,8,128]{2,1,0:T(8,128)S(1)}, u32[]{:S(2)}, u32[]{:S(2)}) %all-to-all-start) | async-done | bytes 65568 | tf_op jit(solution)/shard_map/all_to_all | solution.py:367
  43.6 0.0 copy-done.1
  43.6 0.0 copy-start.2
  43.6 0.9 %copy-done.2 = f32[16,32,128]{2,1,0:T(8,128)S(1)} copy-done((f32[16,32,128]{2,1,0:T(8,128)S(1)}, f32[16,32,128]{2,1,0:T(8,128)}, u32[]{:S(2)}) %copy-start.2) | copy-done | bytes 262168
  44.5 9.2 %inner.1 = (f32[6,16,32,128]{3,2,1,0:T(8,128)}, f32[32,16,128]{2,1,0:T(8,128)S(1)}, f32[2,6,2,32,128]{4,3,2,1,0:T(8,128)S(1)}, f32[2,6,2,32,128]{4,3,2,1,0:T(8,1...) custom-call(f32[1]{0:T(128)S(6)} %copy.14.omega_ref, ...), custom_call_target="tpu_custom_call" | custom-call | flops 10000000000 | bytes 30000000 | tf_op jit(solution)/shard_map/inner/pallas_call | solution.py:204
  53.7 4.6 %collective-permute-done.2.direct_hbm = f32[4,3,32,128]{3,2,1,0:T(8,128)} collective-permute-done((f32[4,3,32,128]{3,2,1,0:T(8,128)}, f32[4,3,32,128]{3,2,1,0:T(8,128)}, u32[]{:S(2)}, u32[]{:S(2)}) %collective-permute-start.2) | collective-permute-done | bytes 196640 | tf_op jit(solution)/shard_map/ppermute | solution.py:362
  58.4 2.2 %collective-permute-done.3.staged_hbm = f32[3,3,32,128]{3,2,1,0:T(8,128)} collective-permute-done((f32[3,3,32,128]{3,2,1,0:T(8,128)}, f32[3,3,32,128]{3,2,1,0:T(8,128)}, u32[]{:S(2)}, u32[]{:S(2)}) %collective-permute-start.3) | collective-permute-done | bytes 147488 | tf_op jit(solution)/shard_map/ppermute | solution.py:365
  60.6 3.9 %outer.1 = (f32[6,16,32,128]{3,2,1,0:T(8,128)}, f32[32,16,128]{2,1,0:T(8,128)S(1)}) custom-call(f32[1]{0:T(128)S(6)} %copy.14.omega_ref, f32[32,16,128]{2,1,0:T(8,128)S(1)} %get-tuple-element.10.inner_grad_ref, f32[6,16,32,128]{3,2,1,0:T(8,128)S(1)} %bitcast.15, f32[6,16,32,128]{3,2,1,0:T(8,128)S(1)} %bitcast.17, ...), custom_call_target="tpu_custom_call", output_to_operand_aliasing={{0}: (12, {})} | custom-call | flops 100000000 | bytes 3000000 | tf_op jit(solution)/shard_map/outer/pallas_call | solution.py:324
  64.5 15.6 %all_to_all.10 = f32[32,16,128]{2,1,0:T(8,128)S(1)} all-to-all(f32[32,16,128]{2,1,0:T(8,128)S(1)} %get-tuple-element.17), channel_id=1, replica_groups=mesh['tx'=32,'slab'=16] {'tx'}, dimensions={0} | all-to-all | bytes 524288 | tf_op jit(solution)/shard_map/all_to_all | solution.py:372
  80.1 0.6 reduce_sum.9
Async XLA Ops:
  0.6 30.0 %copy-start = (f32[1,6,16,32,128]{4,3,2,1,0:T(8,128)S(1)}, f32[1,6,16,32,128]{4,3,2,1,0:T(8,128)}, u32[]{:S(2)}) copy-start(f32[1,6,16,32,128]{4,3,2,1,0:T(8,128)} %param.8) | copy-start | bytes 4718596
  0.6 13.0 %copy-start.3 = (f32[1,6,256]{2,0,1:T(1,128)S(1)}, f32[1,6,256]{2,0,1:T(1,128)}, u32[]{:S(2)}) copy-start(f32[1,6,256]{2,0,1:T(1,128)} %param.11) | copy-start | bytes 18436
  2.7 40.9 %copy-start.1 = (f32[1,6,16,32,128]{4,3,2,1,0:T(8,128)S(1)}, f32[1,6,16,32,128]{4,3,2,1,0:T(8,128)}, u32[]{:S(2)}) copy-start(f32[1,6,16,32,128]{4,3,2,1,0:T(8,128)} %param.7) | copy-start | bytes 4718596
  3.5 35.8 %collective-permute-start = (f32[7,3,32,128]{3,2,1,0:T(8,128)}, f32[7,3,32,128]{3,2,1,0:T(8,128)S(1)}, u32[]{:S(2)}, u32[]{:S(2)}) collective-permute-start(f32[7,3,32,128]{3,2,1,0:T(8,128)} %pad_maximum_fusion), channel_id=1, source_target_pairs={{0,1},{1,2},{2,3},{3,0},{4,5},{5,6},{6,7},{7,4},{8,9},{9,10},{10,1... | collective-permute-start | bytes 1032200 | tf_op jit(solution)/shard_map/ppermute | solution.py:359
  11.7 27.5 %collective-permute-start.1 = (f32[7,3,32,128]{3,2,1,0:T(8,128)}, f32[7,3,32,128]{3,2,1,0:T(8,128)}, u32[]{:S(2)}, u32[]{:S(2)}) collective-permute-start(f32[7,3,32,128]{3,2,1,0:T(8,128)} %pad_maximum_fusion.1), channel_id=1, source_target_pairs={{1,0},{2,1},{3,2},{0,3},{5,4},{6,5},{7,6},{4,7},{9,8},{10,9},{11,1... | collective-permute-start | bytes 1032200 | tf_op jit(solution)/shard_map/ppermute | solution.py:360
  16.2 27.4 %all-to-all-start = ((f32[16,8,128]{2,1,0:T(8,128)}), f32[16,8,128]{2,1,0:T(8,128)S(1)}, u32[]{:S(2)}, u32[]{:S(2)}) async-start(f32[16,8,128]{2,1,0:T(8,128)} %pack.1), calls=%async_computation | async-start | bytes 131072 | tf_op jit(solution)/shard_map/all_to_all | solution.py:367
  31.3 27.1 %collective-permute-start.2 = (f32[4,3,32,128]{3,2,1,0:T(8,128)}, f32[4,3,32,128]{3,2,1,0:T(8,128)}, u32[]{:S(2)}, u32[]{:S(2)}) collective-permute-start(f32[4,3,32,128]{3,2,1,0:T(8,128)} %slice_select_fusion), channel_id=1, source_target_pairs={{3,4},{7,8},{11,12},{4,3},{8,7},{12,11},{19,20},{23,24},{27,28},{2... | collective-permute-start | bytes 589832 | tf_op jit(solution)/shard_map/ppermute | solution.py:362
  40.8 19.8 %collective-permute-start.3 = (f32[3,3,32,128]{3,2,1,0:T(8,128)}, f32[3,3,32,128]{3,2,1,0:T(8,128)}, u32[]{:S(2)}, u32[]{:S(2)}) collective-permute-start(f32[3,3,32,128]{3,2,1,0:T(8,128)} %slice_select_fusion.1), channel_id=1, source_target_pairs={{0,4},{4,8},{8,12},{7,3},{11,7},{15,11},{16,20},{20,24},{24,28},{2... | collective-permute-start | bytes 442376 | tf_op jit(solution)/shard_map/ppermute | solution.py:365
  43.6 1.0 %copy-start.2 = (f32[16,32,128]{2,1,0:T(8,128)S(1)}, f32[16,32,128]{2,1,0:T(8,128)}, u32[]{:S(2)}) copy-start(f32[16,32,128]{2,1,0:T(8,128)} %sigma_ref.1) | copy-start | bytes 786436

commit v3 on v2

--- a/solution.py
+++ b/solution.py
@@ -30,26 +30,64 @@
     return jnp.where(mask, 1.0, 0.0).astype(jnp.bfloat16)
 
 
-def pack_kernel(slabs, vals_ref, slab_ref, cell_ref, out_ref, rows_ref):
-    count = vals_ref.shape[1]
+def pack_kernel(
+    slabs, vals_ref, slab_ref, cell_ref, prev_hbm, sigma_hbm,
+    out_ref, highest_hbm, lowest_hbm, cross_a_hbm, cross_b_hbm, rows_ref, sems,
+):
+    comps, width = prev_hbm.shape[:2]
+    split = cross_a_hbm.shape[0]
+    last = lax.axis_index("slab") % COLUMNS == COLUMNS - 1
+    upper, lower = pl.ds(width - SWEEPS, SWEEPS), pl.ds(0, SWEEPS)
+
+    def crossing(layers):
+        return [
+            pltpu.make_async_copy(prev_hbm.at[pl.ds(0, split), layers], cross_a_hbm, sems.at[4]),
+            pltpu.make_async_copy(
+                prev_hbm.at[pl.ds(split, comps - split), layers], cross_b_hbm.at[pl.ds(0, comps - split)], sems.at[5]
+            ),
+            pltpu.make_async_copy(sigma_hbm.at[layers], cross_b_hbm.at[comps - split], sems.at[6]),
+        ]
+
+    whole = [
+        pltpu.make_async_copy(prev_hbm.at[:, upper], highest_hbm.at[pl.ds(0, comps)], sems.at[0]),
+        pltpu.make_async_copy(sigma_hbm.at[upper], highest_hbm.at[comps], sems.at[1]),
+        pltpu.make_async_copy(prev_hbm.at[:, lower], lowest_hbm.at[pl.ds(0, comps)], sems.at[2]),
+        pltpu.make_async_copy(sigma_hbm.at[lower], lowest_hbm.at[comps], sems.at[3]),
+    ]
+
+    @pl.when(last)
+    def _():
+        for copy in crossing(upper):
+            copy.start()
+
+    @pl.when(jnp.logical_not(last))
+    def _():
+        for copy in crossing(lower):
+            copy.start()
+
+    for copy in whole:
+        copy.start()
+
+    count = vals_ref.shape[2]
     rows_ref[...] = jnp.zeros_like(rows_ref)
-    rows_ref[0:6, :] = vals_ref[...]
-    rows_ref[6:7, :] = cell_ref[...].astype(jnp.float32)
+    for c in range(comps):
+        rows_ref[c:c + 1, :] = vals_ref[c]
+    rows_ref[comps:comps + 1, :] = cell_ref[...].astype(jnp.float32)
     target = slab_ref[...]
     member = ones_where(lax.broadcasted_iota(jnp.int32, (slabs, count), 0) == target)
-    before = ones_where(
+    earlier = ones_where(
         lax.broadcasted_iota(jnp.int32, (count, count), 0)
         < lax.broadcasted_iota(jnp.int32, (count, count), 1)
     )
-    ahead = jnp.dot(member, before, preferred_element_type=jnp.float32)
+    ahead = jnp.dot(member, earlier, preferred_element_type=jnp.float32)
     rank = jnp.sum(ahead * member.astype(jnp.float32), axis=0, keepdims=True)
     key = (target + 1) * CAP + rank.astype(jnp.int32)
-    width = slabs * CAP + LANES
-    chosen = ones_where(lax.broadcasted_iota(jnp.int32, (width, count), 0) == key)
+    lanes = slabs * CAP + LANES
+    chosen = ones_where(lax.broadcasted_iota(jnp.int32, (lanes, count), 0) == key)
     packed = sum(dot_nt(part, chosen) for part in split_3(rows_ref[...]))
     lane = lax.broadcasted_iota(jnp.int32, (8, LANES), 1)
     per_tile = LANES // CAP
-    tiles = [packed[:, q * LANES:(q + 1) * LANES] for q in range(width // LANES)]
+    tiles = [packed[:, q * LANES:(q + 1) * LANES] for q in range(lanes // LANES)]
     for d in range(slabs):
         q, m = divmod(d, per_tile)
         if m == 0:
@@ -59,16 +97,26 @@
             out_ref[d] = jnp.where(
                 lane < shift, pltpu.roll(tiles[q], shift, 1), pltpu.roll(tiles[q + 1], shift, 1)
             )
-
-
-def pack(vals, target, cells, slabs):
+    for copy in crossing(lower) + whole:
+        copy.wait()
+
+
+def pack(vals, target, cells, prev, sigma, slabs, split):
+    comps, _, ny, nz = prev.shape
+    f32 = jnp.float32
+    hbm = pl.BlockSpec(memory_space=pl.ANY)
+    vmem = pl.BlockSpec(memory_space=pltpu.VMEM)
     return pl.pallas_call(
         functools.partial(pack_kernel, slabs),
-        out_shape=jax.ShapeDtypeStruct((slabs, 8, LANES), jnp.float32),
-        scratch_shapes=[pltpu.VMEM((8, vals.shape[1]), jnp.float32)],
+        out_shape=[jax.ShapeDtypeStruct((slabs, 8, LANES), f32)] + [
+            jax.ShapeDtypeStruct((blocks, SWEEPS, ny, nz), f32) for blocks in (comps + 1, comps + 1, split, comps + 1 - split)
+        ],
+        in_specs=[vmem, vmem, vmem, hbm, hbm],
+        out_specs=[vmem, hbm, hbm, hbm, hbm],
+        scratch_shapes=[pltpu.VMEM((8, vals.shape[2]), f32), pltpu.SemaphoreType.DMA((7,))],
         cost_estimate=pl.CostEstimate(flops=20_000_000, bytes_accessed=100_000, transcendentals=0),
         name="pack",
-    )(vals, target, cells)
+    )(vals, target, cells, prev, sigma)
 
 
 def regroup(got_ref, part):
@@ -349,25 +397,25 @@
     pairs, comps, width, ny, nz = adj_prev.shape
     slabs, groups = lax.axis_size("slab"), lax.axis_size("tx")
     prev, fwd = adj_prev[0], fwd_field[0]
-    ring = [(i, i + 1 if (i + 1) % COLUMNS else i + 1 - COLUMNS) for i in range(slabs)]
-    crossing = [(i, i + 1) for i in range(COLUMNS - 1, slabs - 1, COLUMNS)]
-    straight = [(i, i + COLUMNS) for i in range(0, slabs - COLUMNS, COLUMNS)]
-    straight += [(i + COLUMNS, i) for i in range(COLUMNS - 1, slabs - COLUMNS, COLUMNS)]
-    column = lax.axis_index("slab") % COLUMNS
-    highest = jnp.concatenate([prev[:, width - SWEEPS:], sigma[None, width - SWEEPS:]], axis=0)
-    lowest = jnp.concatenate([prev[:, :SWEEPS], sigma[None, :SWEEPS]], axis=0)
-    before = lax.ppermute(highest, "slab", ring)
-    after = lax.ppermute(lowest, "slab", [(j, i) for i, j in ring])
-    split = 4
-    direct = lax.ppermute(
-        jnp.where(column == COLUMNS - 1, highest[:split], lowest[:split]), "slab", crossing + [(j, i) for i, j in crossing]
-    )
-    staged = lax.ppermute(jnp.where(column == 0, before[split:], after[split:]), "slab", straight)
-    send = pack(res_vals[0], rec_slab.reshape(1, -1), rec_cell, slabs)
+    rows = range(0, slabs, COLUMNS)
+    up = [(r + i, r + i + 1) for r in rows for i in range(COLUMNS - 1)]
+    down = [(j, i) for i, j in up]
+    stage_a = [(r + 3, r) for r in rows] + [(r, r + 3) for r in rows]
+    stage_b = [(r + 3, r + 1) for r in rows] + [(r, r + 2) for r in rows]
+    cross_a = [(r, r + COLUMNS) for r in rows[:-1]] + [(r + 3, r + 3 - COLUMNS) for r in rows[1:]]
+    cross_b = [(r + 1, r + COLUMNS) for r in rows[:-1]] + [(r + 2, r + 3 - COLUMNS) for r in rows[1:]]
+    vals = jnp.transpose(res_vals, (1, 0, 2))
+    send, highest, lowest, part_a, part_b = pack(vals, rec_slab.reshape(1, -1), rec_cell, prev, sigma, slabs, 4)
+    part_a = lax.ppermute(part_a, "slab", stage_a)
+    part_b = lax.ppermute(part_b, "slab", stage_b)
     got = lax.all_to_all(send, "slab", split_axis=0, concat_axis=0, tiled=True)
+    part_a = lax.ppermute(part_a, "slab", cross_a)
+    part_b = lax.ppermute(part_b, "slab", cross_b)
+    before = lax.ppermute(highest, "slab", up)
+    after = lax.ppermute(lowest, "slab", down)
     factor = 1.0 / (3.0 * pairs * groups) ** 0.5
     adjoint, terms, *from_inner = inner(omega, got, sigma, prev, fwd, factor)
-    halos = (before, after, direct, staged)
+    halos = (before, after, part_a, part_b)
     adjoint, terms = outer(omega, terms, prev, fwd, halos, from_inner, adjoint, slabs, factor)
     parts = lax.all_to_all(terms, "tx", split_axis=0, concat_axis=0, tiled=True)
     gradient = jnp.sum(parts, axis=0)[:, None, :]

time: 81.8 us -> 110 us (1.34)
  Pallas kernels: 15.1 us -> 47.2 us
  other arithmetic: 4.43 us -> 0.63 us
  waiting for transfers between devices: 8.34 us -> 11.8 us
  local copies, waits for them, and re-layouts: 3.61 us -> 1.41 us
  starting transfers between devices: 32.3 us -> 30.4 us
    pallas_call x1, Pallas kernels: 1.97 us -> 33.9 us  [pack(): pl.pallas_call(functools.partial(pack_kernel, slabs), out_shape=[jax.Shap...]
    ppermute x4 -> x6, starting transfers between devices: 17.9 us -> 12.5 us  [the longest x1 4.57 us: shards(): after = lax.ppermute(lowest, 'slab', down)]
    ppermute x4 -> x6, waiting for transfers between devices: 6.88 us -> 11.7 us  [the longest x1 7.12 us: shards(): part_b = lax.ppermute(part_b, 'slab', cross_b)]
    all_to_all x1, starting transfers between devices: 14.4 us -> 18 us  [shards(): got = lax.all_to_all(send, 'slab', split_axis=0, concat_axis=0, tiled=True)]
    select_n x2 -> x0, other arithmetic: 2.29 us -> none  [the longest x1 1.58 us: shards(): jnp.where(column == 0, before[split:], after[split:])]
    concatenate x2 -> x0, other arithmetic: 1.51 us -> none  [the longest x1 0.76 us: shards(): jnp.concatenate([prev[:, width - SWEEPS:], sigma[None, width - SWEEPS:]],...]
    all_to_all x1, waiting for transfers between devices: 1.46 us -> 0.01 us  [shards(): got = lax.all_to_all(send, 'slab', split_axis=0, concat_axis=0, tiled=True)]
  transfers between devices with their start and end apart: 5 -> 7, of which waited for: 3 -> 2; matrix products, arithmetic and copies ran while one was open for 5% -> 0% of each run, Pallas kernels for 14% -> 8%
where the time goes in v3:
time: 110 us; the launch traced here: 108 us
  Pallas kernels  47.2 us (43%)
  starting transfers between devices  30.4 us (28%)
  blocking collectives  15.6 us (14%)
  waiting for transfers between devices  11.8 us (11%)
  between operations  1.42 us (1%)
  local copies, waits for them, and re-layouts  1.41 us (1%)
    pallas_call x1, Pallas kernels, pack(): pl.pallas_call(functools.partial(pack_kernel, slabs), out_shape=[jax.Shap...  33.9 us
    all_to_all x1, starting transfers between devices, shards(): got = lax.all_to_all(send, 'slab', split_axis=0, concat_axis=0, tiled=True)  18 us
    all_to_all x1, blocking collectives, shards(): parts = lax.all_to_all(terms, 'tx', split_axis=0, concat_axis=0, tiled=True)  15.6 us
    pallas_call x1, Pallas kernels, inner(): pl.pallas_call(functools.partial(inner_kernel, factor), out_shape=[jax.Sh...  9.19 us
    ppermute x1, waiting for transfers between devices, shards(): part_b = lax.ppermute(part_b, 'slab', cross_b)  7.12 us
    ppermute x1, waiting for transfers between devices, shards(): part_a = lax.ppermute(part_a, 'slab', cross_a)  4.62 us
    ppermute x1, starting transfers between devices, shards(): after = lax.ppermute(lowest, 'slab', down)  4.57 us
    pallas_call x1, Pallas kernels, outer(): pl.pallas_call(functools.partial(outer_kernel, slab_count, factor), out_s...  4.11 us
  transfers between devices with their start and end apart: 7, of which 2 were waited for; matrix products, arithmetic and copies ran while one was open for 0% of the time, Pallas kernels for 8%

profile of v3, /device:TPU:24, one launch (start us, length us, event | category | flops | bytes accessed | tf_op | source)
XLA Modules:
  0.0 108.4 jit_solution(14968239456562318773)
XLA Ops:
  0.6 0.0 copy-start.2
  0.6 0.0 copy-start
  0.7 33.9 %pack.1 = (f32[16,8,128]{2,1,0:T(8,128)}, f32[7,3,32,128]{3,2,1,0:T(8,128)}, f32[7,3,32,128]{3,2,1,0:T(8,128)}, f32[4,3,32,128]{3,2,1,0:T(8,128)}, f32[3,3,32,128]{3,2,1,0:T(8,128)}) custom-call(f32[6,1,256]{2,1,0:T(1,128)} %bitcast.13, s32[1,256]{1,0:T(1,128)} %bitcast.14, s32[1,256]{1,0:T(1,128)} %cell_ref.1, f32[6,16,32,128]{3,2,1,0:T(8,128)} %bitcast.6, ...), custom_call_target="tpu_custom_call" | custom-call | flops 20000000 | bytes 100000 | tf_op jit(solution)/shard_map/pack/pallas_call | solution.py:109
  34.6 18.0 %all-to-all-start = ((f32[16,8,128]{2,1,0:T(8,128)}), f32[16,8,128]{2,1,0:T(8,128)S(1)}, u32[]{:S(2)}, u32[]{:S(2)}) async-start(f32[16,8,128]{2,1,0:T(8,128)} %get-tuple-element.15), calls=%async_computation | async-start | bytes 131072 | tf_op jit(solution)/shard_map/all_to_all | solution.py:411
  52.5 2.0 %collective-permute-start.2 = (f32[4,3,32,128]{3,2,1,0:T(8,128)}, f32[4,3,32,128]{3,2,1,0:T(8,128)S(1)}, u32[]{:S(2)}, u32[]{:S(2)}) collective-permute-start(f32[4,3,32,128]{3,2,1,0:T(8,128)} %get-tuple-element.19), channel_id=1, source_target_pairs={{3,0},{7,4},{11,8},{15,12},{0,3},{4,7},{8,11},{12,15},{19,16},{23,... | collective-permute-start | bytes 589832 | tf_op jit(solution)/shard_map/ppermute | solution.py:409
  54.5 2.0 %collective-permute-start.4 = (f32[3,3,32,128]{3,2,1,0:T(8,128)}, f32[3,3,32,128]{3,2,1,0:T(8,128)S(1)}, u32[]{:S(2)}, u32[]{:S(2)}) collective-permute-start(f32[3,3,32,128]{3,2,1,0:T(8,128)} %get-tuple-element.20), channel_id=1, source_target_pairs={{3,1},{7,5},{11,9},{15,13},{0,2},{4,6},{8,10},{12,14},{19,17},{23,... | collective-permute-start | bytes 442376 | tf_op jit(solution)/shard_map/ppermute | solution.py:410
  56.6 1.3 %collective-permute-start = (f32[7,3,32,128]{3,2,1,0:T(8,128)}, f32[7,3,32,128]{3,2,1,0:T(8,128)S(1)}, u32[]{:S(2)}, u32[]{:S(2)}) collective-permute-start(f32[7,3,32,128]{3,2,1,0:T(8,128)} %get-tuple-element.17), channel_id=1, source_target_pairs={{0,1},{1,2},{2,3},{4,5},{5,6},{6,7},{8,9},{9,10},{10,11},{12,13},{... | collective-permute-start | bytes 1032200 | tf_op jit(solution)/shard_map/ppermute | solution.py:414
  57.9 4.6 %collective-permute-start.1 = (f32[7,3,32,128]{3,2,1,0:T(8,128)}, f32[7,3,32,128]{3,2,1,0:T(8,128)S(1)}, u32[]{:S(2)}, u32[]{:S(2)}) collective-permute-start(f32[7,3,32,128]{3,2,1,0:T(8,128)} %get-tuple-element.18), channel_id=1, source_target_pairs={{1,0},{2,1},{3,2},{5,4},{6,5},{7,6},{9,8},{10,9},{11,10},{13,12},{... | collective-permute-start | bytes 1032200 | tf_op jit(solution)/shard_map/ppermute | solution.py:415
  63.1 0.0 collective-permute-done.4
  63.1 1.3 %collective-permute-start.5 = (f32[3,3,32,128]{3,2,1,0:T(8,128)S(1)}, f32[3,3,32,128]{3,2,1,0:T(8,128)S(1)}, u32[]{:S(2)}, u32[]{:S(2)}) collective-permute-start(f32[3,3,32,128]{3,2,1,0:T(8,128)S(1)} %collective-permute-done.4), channel_id=1, source_target_pairs={{1,4},{5,8},{9,12},{6,3},{10,7},{14,11},{17,20},{21,24},{25,28},{2... | collective-permute-start | bytes 442376 | tf_op jit(solution)/shard_map/ppermute | solution.py:413
  64.4 0.0 collective-permute-done.2
  64.4 1.3 %collective-permute-start.3 = (f32[4,3,32,128]{3,2,1,0:T(8,128)S(1)}, f32[4,3,32,128]{3,2,1,0:T(8,128)S(1)}, u32[]{:S(2)}, u32[]{:S(2)}) collective-permute-start(f32[4,3,32,128]{3,2,1,0:T(8,128)S(1)} %collective-permute-done.2), channel_id=1, source_target_pairs={{0,4},{4,8},{8,12},{7,3},{11,7},{15,11},{16,20},{20,24},{24,28},{2... | collective-permute-start | bytes 589832 | tf_op jit(solution)/shard_map/ppermute | solution.py:412
  65.7 0.0 all-to-all-done.got_ref
  65.7 0.0 copy-done.2
  65.7 0.0 copy-done
  65.7 0.0 copy-start.1
  65.8 1.4 %copy-done.1 = f32[1,6,16,32,128]{4,3,2,1,0:T(8,128)S(1)} copy-done((f32[1,6,16,32,128]{4,3,2,1,0:T(8,128)S(1)}, f32[1,6,16,32,128]{4,3,2,1,0:T(8,128)}, u32[]{:S(2)}) %copy-start.1) | copy-done | bytes 1572888
  67.2 9.2 %inner.1 = (f32[6,16,32,128]{3,2,1,0:T(8,128)}, f32[32,16,128]{2,1,0:T(8,128)S(1)}, f32[2,6,2,32,128]{4,3,2,1,0:T(8,128)S(1)}, f32[2,6,2,32,128]{4,3,2,1,0:T(8,1...) custom-call(f32[1]{0:T(128)S(6)} %copy.11.omega_ref, ...), custom_call_target="tpu_custom_call" | custom-call | flops 10000000000 | bytes 30000000 | tf_op jit(solution)/shard_map/inner/pallas_call | solution.py:252
  76.4 7.1 %collective-permute-done.5.staged_hbm = f32[3,3,32,128]{3,2,1,0:T(8,128)S(1)} collective-permute-done((f32[3,3,32,128]{3,2,1,0:T(8,128)S(1)}, f32[3,3,32,128]{3,2,1,0:T(8,128)S(1)}, u32[]{:S(2)}, u32[]{:S(2)}) %collective-permute-start.5) | collective-permute-done | bytes 147488 | tf_op jit(solution)/shard_map/ppermute | solution.py:413
  83.5 0.0 collective-permute-done.before_hbm
  83.5 0.0 collective-permute-done.1.after_hbm
  83.5 4.6 %collective-permute-done.3.direct_hbm = f32[4,3,32,128]{3,2,1,0:T(8,128)S(1)} collective-permute-done((f32[4,3,32,128]{3,2,1,0:T(8,128)S(1)}, f32[4,3,32,128]{3,2,1,0:T(8,128)S(1)}, u32[]{:S(2)}, u32[]{:S(2)}) %collective-permute-start.3) | collective-permute-done | bytes 196640 | tf_op jit(solution)/shard_map/ppermute | solution.py:412
  88.1 4.1 %outer.1 = (f32[6,16,32,128]{3,2,1,0:T(8,128)}, f32[32,16,128]{2,1,0:T(8,128)S(1)}) custom-call(f32[1]{0:T(128)S(6)} %copy.11.omega_ref, f32[32,16,128]{2,1,0:T(8,128)S(1)} %get-tuple-element.16.inner_grad_ref, f32[6,16,32,128]{3,2,1,0:T(8,128)S(1)} %bitcast.8, f32[6,16,32,128]{3,2,1,0:T(8,128)S(1)} %bitcast.10, ...), custom_call_target="tpu_custom_call", output_to_operand_aliasing={{0}: (12, {})} | custom-call | flops 100000000 | bytes 3000000 | tf_op jit(solution)/shard_map/outer/pallas_call | solution.py:372
  92.2 15.6 %all_to_all.10 = f32[32,16,128]{2,1,0:T(8,128)S(1)} all-to-all(f32[32,16,128]{2,1,0:T(8,128)S(1)} %get-tuple-element.27), channel_id=1, replica_groups=mesh['tx'=32,'slab'=16] {'tx'}, dimensions={0} | all-to-all | bytes 524288 | tf_op jit(solution)/shard_map/all_to_all | solution.py:420
  107.8 0.6 reduce_sum.9
Async XLA Ops:
  0.6 65.1 %copy-start.2 = (f32[16,32,128]{2,1,0:T(8,128)S(1)}, f32[16,32,128]{2,1,0:T(8,128)}, u32[]{:S(2)}) copy-start(f32[16,32,128]{2,1,0:T(8,128)} %sigma_ref.1) | copy-start | bytes 786436
  0.6 65.1 %copy-start = (f32[1,6,16,32,128]{4,3,2,1,0:T(8,128)S(1)}, f32[1,6,16,32,128]{4,3,2,1,0:T(8,128)}, u32[]{:S(2)}) copy-start(f32[1,6,16,32,128]{4,3,2,1,0:T(8,128)} %param.8) | copy-start | bytes 4718596
  34.6 31.2 %all-to-all-start = ((f32[16,8,128]{2,1,0:T(8,128)}), f32[16,8,128]{2,1,0:T(8,128)S(1)}, u32[]{:S(2)}, u32[]{:S(2)}) async-start(f32[16,8,128]{2,1,0:T(8,128)} %get-tuple-element.15), calls=%async_computation | async-start | bytes 131072 | tf_op jit(solution)/shard_map/all_to_all | solution.py:411
  52.5 11.9 %collective-permute-start.2 = (f32[4,3,32,128]{3,2,1,0:T(8,128)}, f32[4,3,32,128]{3,2,1,0:T(8,128)S(1)}, u32[]{:S(2)}, u32[]{:S(2)}) collective-permute-start(f32[4,3,32,128]{3,2,1,0:T(8,128)} %get-tuple-element.19), channel_id=1, source_target_pairs={{3,0},{7,4},{11,8},{15,12},{0,3},{4,7},{8,11},{12,15},{19,16},{23,... | collective-permute-start | bytes 589832 | tf_op jit(solution)/shard_map/ppermute | solution.py:409
  54.5 8.6 %collective-permute-start.4 = (f32[3,3,32,128]{3,2,1,0:T(8,128)}, f32[3,3,32,128]{3,2,1,0:T(8,128)S(1)}, u32[]{:S(2)}, u32[]{:S(2)}) collective-permute-start(f32[3,3,32,128]{3,2,1,0:T(8,128)} %get-tuple-element.20), channel_id=1, source_target_pairs={{3,1},{7,5},{11,9},{15,13},{0,2},{4,6},{8,10},{12,14},{19,17},{23,... | collective-permute-start | bytes 442376 | tf_op jit(solution)/shard_map/ppermute | solution.py:410
  56.6 26.9 %collective-permute-start = (f32[7,3,32,128]{3,2,1,0:T(8,128)}, f32[7,3,32,128]{3,2,1,0:T(8,128)S(1)}, u32[]{:S(2)}, u32[]{:S(2)}) collective-permute-start(f32[7,3,32,128]{3,2,1,0:T(8,128)} %get-tuple-element.17), channel_id=1, source_target_pairs={{0,1},{1,2},{2,3},{4,5},{5,6},{6,7},{8,9},{9,10},{10,11},{12,13},{... | collective-permute-start | bytes 1032200 | tf_op jit(solution)/shard_map/ppermute | solution.py:414
  57.9 25.6 %collective-permute-start.1 = (f32[7,3,32,128]{3,2,1,0:T(8,128)}, f32[7,3,32,128]{3,2,1,0:T(8,128)S(1)}, u32[]{:S(2)}, u32[]{:S(2)}) collective-permute-start(f32[7,3,32,128]{3,2,1,0:T(8,128)} %get-tuple-element.18), channel_id=1, source_target_pairs={{1,0},{2,1},{3,2},{5,4},{6,5},{7,6},{9,8},{10,9},{11,10},{13,12},{... | collective-permute-start | bytes 1032200 | tf_op jit(solution)/shard_map/ppermute | solution.py:415
  63.1 20.4 %collective-permute-start.5 = (f32[3,3,32,128]{3,2,1,0:T(8,128)S(1)}, f32[3,3,32,128]{3,2,1,0:T(8,128)S(1)}, u32[]{:S(2)}, u32[]{:S(2)}) collective-permute-start(f32[3,3,32,128]{3,2,1,0:T(8,128)S(1)} %collective-permute-done.4), channel_id=1, source_target_pairs={{1,4},{5,8},{9,12},{6,3},{10,7},{14,11},{17,20},{21,24},{25,28},{2... | collective-permute-start | bytes 442376 | tf_op jit(solution)/shard_map/ppermute | solution.py:413
  64.4 23.7 %collective-permute-start.3 = (f32[4,3,32,128]{3,2,1,0:T(8,128)S(1)}, f32[4,3,32,128]{3,2,1,0:T(8,128)S(1)}, u32[]{:S(2)}, u32[]{:S(2)}) collective-permute-start(f32[4,3,32,128]{3,2,1,0:T(8,128)S(1)} %collective-permute-done.2), channel_id=1, source_target_pairs={{0,4},{4,8},{8,12},{7,3},{11,7},{15,11},{16,20},{20,24},{24,28},{2... | collective-permute-start | bytes 589832 | tf_op jit(solution)/shard_map/ppermute | solution.py:412
  65.7 1.4 %copy-start.1 = (f32[1,6,16,32,128]{4,3,2,1,0:T(8,128)S(1)}, f32[1,6,16,32,128]{4,3,2,1,0:T(8,128)}, u32[]{:S(2)}) copy-start(f32[1,6,16,32,128]{4,3,2,1,0:T(8,128)} %param.7) | copy-start | bytes 4718596

commit v4 on v3

--- a/solution.py
+++ b/solution.py
@@ -30,42 +30,60 @@
     return jnp.where(mask, 1.0, 0.0).astype(jnp.bfloat16)
 
 
+def stage_kernel(prev_hbm, sigma_hbm, part_a_ref, part_b_ref, sems):
+    comps, width = prev_hbm.shape[:2]
+    split = part_a_ref.shape[0]
+    last = lax.axis_index("slab") % COLUMNS == COLUMNS - 1
+
+    def copies(first):
+        layers = pl.ds(first, SWEEPS)
+        return [
+            pltpu.make_async_copy(prev_hbm.at[pl.ds(0, split), layers], part_a_ref, sems.at[0]),
+            pltpu.make_async_copy(
+                prev_hbm.at[pl.ds(split, comps - split), layers], part_b_ref.at[pl.ds(0, comps - split)], sems.at[1]
+            ),
+            pltpu.make_async_copy(sigma_hbm.at[layers], part_b_ref.at[comps - split], sems.at[2]),
+        ]
+
+    @pl.when(last)
+    def _():
+        for copy in copies(width - SWEEPS):
+            copy.start()
+
+    @pl.when(jnp.logical_not(last))
+    def _():
+        for copy in copies(0):
+            copy.start()
+
+    for copy in copies(0):
+        copy.wait()
+
+
+def stage(prev, sigma, split):
+    comps, _, ny, nz = prev.shape
+    hbm = pl.BlockSpec(memory_space=pl.ANY)
+    vmem = pl.BlockSpec(memory_space=pltpu.VMEM)
+    return pl.pallas_call(
+        stage_kernel,
+        out_shape=[jax.ShapeDtypeStruct((blocks, SWEEPS, ny, nz), jnp.float32) for blocks in (split, comps + 1 - split)],
+        in_specs=[hbm, hbm],
+        out_specs=[vmem, vmem],
+        scratch_shapes=[pltpu.SemaphoreType.DMA((3,))],
+        cost_estimate=pl.CostEstimate(flops=0, bytes_accessed=700_000, transcendentals=0),
+        name="stage",
+    )(prev, sigma)
+
+
 def pack_kernel(
-    slabs, vals_ref, slab_ref, cell_ref, prev_hbm, sigma_hbm,
-    out_ref, highest_hbm, lowest_hbm, cross_a_hbm, cross_b_hbm, rows_ref, sems,
+    slabs, vals_ref, slab_ref, cell_ref, prev_hbm, sigma_hbm, out_ref, highest_ref, lowest_ref, rows_ref, sems,
 ):
     comps, width = prev_hbm.shape[:2]
-    split = cross_a_hbm.shape[0]
-    last = lax.axis_index("slab") % COLUMNS == COLUMNS - 1
-    upper, lower = pl.ds(width - SWEEPS, SWEEPS), pl.ds(0, SWEEPS)
-
-    def crossing(layers):
-        return [
-            pltpu.make_async_copy(prev_hbm.at[pl.ds(0, split), layers], cross_a_hbm, sems.at[4]),
-            pltpu.make_async_copy(
-                prev_hbm.at[pl.ds(split, comps - split), layers], cross_b_hbm.at[pl.ds(0, comps - split)], sems.at[5]
-            ),
-            pltpu.make_async_copy(sigma_hbm.at[layers], cross_b_hbm.at[comps - split], sems.at[6]),
-        ]
-
-    whole = [
-        pltpu.make_async_copy(prev_hbm.at[:, upper], highest_hbm.at[pl.ds(0, comps)], sems.at[0]),
-        pltpu.make_async_copy(sigma_hbm.at[upper], highest_hbm.at[comps], sems.at[1]),
-        pltpu.make_async_copy(prev_hbm.at[:, lower], lowest_hbm.at[pl.ds(0, comps)], sems.at[2]),
-        pltpu.make_async_copy(sigma_hbm.at[lower], lowest_hbm.at[comps], sems.at[3]),
-    ]
-
-    @pl.when(last)
-    def _():
-        for copy in crossing(upper):
-            copy.start()
-
-    @pl.when(jnp.logical_not(last))
-    def _():
-        for copy in crossing(lower):
-            copy.start()
-
-    for copy in whole:
+    copies = []
+    for n, (first, ref) in enumerate(((width - SWEEPS, highest_ref), (0, lowest_ref))):
+        layers = pl.ds(first, SWEEPS)
+        copies.append(pltpu.make_async_copy(prev_hbm.at[:, layers], ref.at[pl.ds(0, comps)], sems.at[2 * n]))
+        copies.append(pltpu.make_async_copy(sigma_hbm.at[layers], ref.at[comps], sems.at[2 * n + 1]))
+    for copy in copies:
         copy.start()
 
     count = vals_ref.shape[2]
@@ -97,23 +115,22 @@
             out_ref[d] = jnp.where(
                 lane < shift, pltpu.roll(tiles[q], shift, 1), pltpu.roll(tiles[q + 1], shift, 1)
             )
-    for copy in crossing(lower) + whole:
+    for copy in copies:
         copy.wait()
 
 
-def pack(vals, target, cells, prev, sigma, slabs, split):
+def pack(vals, target, cells, prev, sigma, slabs):
     comps, _, ny, nz = prev.shape
     f32 = jnp.float32
     hbm = pl.BlockSpec(memory_space=pl.ANY)
     vmem = pl.BlockSpec(memory_space=pltpu.VMEM)
     return pl.pallas_call(
         functools.partial(pack_kernel, slabs),
-        out_shape=[jax.ShapeDtypeStruct((slabs, 8, LANES), f32)] + [
-            jax.ShapeDtypeStruct((blocks, SWEEPS, ny, nz), f32) for blocks in (comps + 1, comps + 1, split, comps + 1 - split)
-        ],
+        out_shape=[jax.ShapeDtypeStruct((slabs, 8, LANES), f32)]
+        + [jax.ShapeDtypeStruct((comps + 1, SWEEPS, ny, nz), f32)] * 2,
         in_specs=[vmem, vmem, vmem, hbm, hbm],
-        out_specs=[vmem, hbm, hbm, hbm, hbm],
-        scratch_shapes=[pltpu.VMEM((8, vals.shape[2]), f32), pltpu.SemaphoreType.DMA((7,))],
+        out_specs=[vmem, vmem, vmem],
+        scratch_shapes=[pltpu.VMEM((8, vals.shape[2]), f32), pltpu.SemaphoreType.DMA((4,))],
         cost_estimate=pl.CostEstimate(flops=20_000_000, bytes_accessed=100_000, transcendentals=0),
         name="pack",
     )(vals, target, cells, prev, sigma)
@@ -161,16 +178,17 @@
 
 
 def inner_kernel(
-    factor, omega_ref, got_ref, sigma_ref, prev_hbm, fwd_hbm,
+    factor, omega_ref, got_ref, sigma_hbm, prev_hbm, fwd_hbm,
     adjoint_hbm, grad_ref, field_1_hbm, field_2_hbm, source_hbm, coef_hbm,
-    field_0, field_1, field_2, field_3, fwd, source, coef, onehot, sems,
+    field_0, field_1, field_2, field_3, fwd, sig, source, coef, onehot, sems,
 ):
     comps, width, ny, nz = field_0.shape
     rim = SWEEPS - 1
     load_prev = pltpu.make_async_copy(prev_hbm, field_0, sems.at[0])
     load_fwd = pltpu.make_async_copy(fwd_hbm, fwd, sems.at[1])
-    load_prev.start()
-    load_fwd.start()
+    load_sigma = pltpu.make_async_copy(sigma_hbm, sig, sems.at[11])
+    for load in (load_prev, load_sigma, load_fwd):
+        load.start()
 
     own = regroup(got_ref, 1)
     count = own.shape[1]
@@ -199,10 +217,10 @@
             source[c, at:at + rim] = result.reshape(rim, ny, nz)
 
     omega = omega_ref[0]
-    coef[0], coef[1] = coefficients(omega, sigma_ref[...])
+    load_sigma.wait()
+    coef[0], coef[1] = coefficients(omega, sig[...])
     beside = neighbour_sum(ny, nz)
     load_prev.wait()
-    load_fwd.wait()
 
     def sweep(old, new, first, last):
         def layer(i, carry):
@@ -221,11 +239,12 @@
             if last:
                 grad_ref[:, pl.ds(x, 1), :] = (terms * (omega * factor)).reshape(ny, 1, nz)
             return carry
-        lax.fori_loop(0, new.shape[1], layer, 0)
+        lax.fori_loop(0, new.shape[1], layer, 0, unroll=new.shape[1] // 2)
 
     grad_ref[...] = jnp.zeros_like(grad_ref)
     sweep(field_0, field_1, 1, False)
     sweep(field_1, field_2, 2, False)
+    load_fwd.wait()
     sweep(field_2, field_3, 3, True)
     stores = [pltpu.make_async_copy(field_3, adjoint_hbm.at[:, pl.ds(3, width - 6)], sems.at[2])]
     for s in range(2):
@@ -254,7 +273,7 @@
         out_shape=[jax.ShapeDtypeStruct(shape, f32) for shape in (
             prev.shape, (ny, width, nz), (2, comps, 2) + cells, (2, comps, 2) + cells, (2, comps, 5) + cells, (2, 2, 3) + cells,
         )],
-        in_specs=[pl.BlockSpec(memory_space=pltpu.SMEM), vmem, vmem, hbm, hbm],
+        in_specs=[pl.BlockSpec(memory_space=pltpu.SMEM), vmem, hbm, hbm, hbm],
         out_specs=[hbm, vmem, hbm, hbm, hbm, hbm],
         scratch_shapes=[
             pltpu.VMEM((comps, width) + cells, f32),
@@ -262,10 +281,11 @@
             pltpu.VMEM((comps, width - 4) + cells, f32),
             pltpu.VMEM((comps, width - 6) + cells, f32),
             pltpu.VMEM((comps, width) + cells, f32),
+            pltpu.VMEM((width,) + cells, f32),
             pltpu.VMEM((comps, width + 4) + cells, f32),
             pltpu.VMEM((2, width) + cells, f32),
             pltpu.VMEM((comps * nz, 2 * count), jnp.bfloat16),
-            pltpu.SemaphoreType.DMA((11,)),
+            pltpu.SemaphoreType.DMA((12,)),
         ],
         compiler_params=pltpu.CompilerParams(vmem_limit_bytes=40 * 1024 * 1024),
         cost_estimate=pl.CostEstimate(flops=10_000_000_000, bytes_accessed=30_000_000, transcendentals=0),
@@ -351,7 +371,7 @@
                 if number == 2:
                     grad_ref[:, pl.ds(k + s * (width - 3), 1), :] = (terms * (omega * factor)).reshape(ny, 1, nz)
             return carry
-        lax.fori_loop(0, 3, layer, 0)
+        lax.fori_loop(0, 3, layer, 0, unroll=3)
 
     sweep(field_0, field_1, 0)
     sweep(field_1, field_2, 1)
@@ -405,10 +425,14 @@
     cross_a = [(r, r + COLUMNS) for r in rows[:-1]] + [(r + 3, r + 3 - COLUMNS) for r in rows[1:]]
     cross_b = [(r + 1, r + COLUMNS) for r in rows[:-1]] + [(r + 2, r + 3 - COLUMNS) for r in rows[1:]]
     vals = jnp.transpose(res_vals, (1, 0, 2))
-    send, highest, lowest, part_a, part_b = pack(vals, rec_slab.reshape(1, -1), rec_cell, prev, sigma, slabs, 4)
+    part_a, part_b = stage(prev, sigma, 4)
     part_a = lax.ppermute(part_a, "slab", stage_a)
     part_b = lax.ppermute(part_b, "slab", stage_b)
+    send, highest, lowest = pack(vals, rec_slab.reshape(1, -1), rec_cell, prev, sigma, slabs)
     got = lax.all_to_all(send, "slab", split_axis=0, concat_axis=0, tiled=True)
+    edge = (lax.axis_index("slab") % COLUMNS) % (COLUMNS - 1) == 0
+    part_a = jnp.where(edge, part_a, 0.0)
+    part_a, highest, lowest = lax.optimization_barrier((part_a, highest, lowest))
     part_a = lax.ppermute(part_a, "slab", cross_a)
     part_b = lax.ppermute(part_b, "slab", cross_b)
     before = lax.ppermute(highest, "slab", up)

time: 110 us -> 79 us (0.72)
  the two profiles are of different devices: /device:TPU:24 before, /device:TPU:1 now
where the time goes in v4:
time: 79 us; the launch traced here: 78.5 us
  starting transfers between devices  35.9 us (45%)
  blocking collectives  22.3 us (28%)
  Pallas kernels  16.1 us (20%)
  other arithmetic  2.26 us (3%)
  between operations  1.47 us (2%)
    all_to_all x1, blocking collectives, shards(): parts = lax.all_to_all(terms, 'tx', split_axis=0, concat_axis=0, tiled=True)  22.3 us
    all_to_all x1, starting transfers between devices, shards(): got = lax.all_to_all(send, 'slab', split_axis=0, concat_axis=0, tiled=True)  15.5 us
    ppermute x1, starting transfers between devices, shards(): part_a = lax.ppermute(part_a, 'slab', cross_a)  8.41 us
    pallas_call x1, Pallas kernels, inner(): pl.pallas_call(functools.partial(inner_kernel, factor), out_shape=[jax.Sh...  7.89 us
    ppermute x1, starting transfers between devices, shards(): part_a = lax.ppermute(part_a, 'slab', stage_a)  5.6 us
    pallas_call x1, Pallas kernels, outer(): pl.pallas_call(functools.partial(outer_kernel, slab_count, factor), out_s...  3.3 us
    pallas_call x1, Pallas kernels, pack(): pl.pallas_call(functools.partial(pack_kernel, slabs), out_shape=[jax.Shap...  3.04 us
    ppermute x1, starting transfers between devices, shards(): before = lax.ppermute(highest, 'slab', up)  2.26 us
  transfers between devices with their start and end apart: 7, of which 1 were waited for; matrix products, arithmetic and copies ran while one was open for 2% of the time, Pallas kernels for 14%

profile of v4, /device:TPU:1, one launch (start us, length us, event | category | flops | bytes accessed | tf_op | source)
XLA Modules:
  0.0 78.5 jit_solution(6591797408726222723)
XLA Ops:
  0.6 0.0 copy-start.1
  0.6 1.9 %stage.1 = (f32[4,3,32,128]{3,2,1,0:T(8,128)}, f32[3,3,32,128]{3,2,1,0:T(8,128)}) custom-call(f32[6,16,32,128]{3,2,1,0:T(8,128)} %bitcast.6, f32[16,32,128]{2,1,0:T(8,128)} %sigma_hbm.5), custom_call_target="tpu_custom_call" | custom-call | bytes 700000 | tf_op jit(solution)/shard_map/stage/pallas_call | solution.py:66
  2.5 0.0 copy-start
  2.5 0.0 copy-start.2
  2.5 5.6 %collective-permute-start = (f32[4,3,32,128]{3,2,1,0:T(8,128)}, f32[4,3,32,128]{3,2,1,0:T(8,128)}, u32[]{:S(2)}, u32[]{:S(2)}) collective-permute-start(f32[4,3,32,128]{3,2,1,0:T(8,128)} %get-tuple-element.20), channel_id=1, source_target_pairs={{3,0},{7,4},{11,8},{15,12},{0,3},{4,7},{8,11},{12,15},{19,16},{23,... | collective-permute-start | bytes 589832 | tf_op jit(solution)/shard_map/ppermute | solution.py:429
  8.1 2.2 %collective-permute-start.4 = (f32[3,3,32,128]{3,2,1,0:T(8,128)}, f32[3,3,32,128]{3,2,1,0:T(8,128)}, u32[]{:S(2)}, u32[]{:S(2)}) collective-permute-start(f32[3,3,32,128]{3,2,1,0:T(8,128)} %get-tuple-element.26), channel_id=1, source_target_pairs={{3,1},{7,5},{11,9},{15,13},{0,2},{4,6},{8,10},{12,14},{19,17},{23,... | collective-permute-start | bytes 442376 | tf_op jit(solution)/shard_map/ppermute | solution.py:430
  10.3 3.0 %pack.1 = (f32[16,8,128]{2,1,0:T(8,128)}, f32[7,3,32,128]{3,2,1,0:T(8,128)}, f32[7,3,32,128]{3,2,1,0:T(8,128)}) custom-call(f32[6,1,256]{2,1,0:T(1,128)} %bitcast.14, s32[1,256]{1,0:T(1,128)} %bitcast.15, s32[1,256]{1,0:T(1,128)} %cell_ref.1, f32[6,16,32,128]{3,2,1,0:T(8,128)} %bitcast.7, f32[16,32,128]{2,1,0:T(8,128)} %sigma_hbm.5), custom_call_target="tpu_custom_call" | custom-call | flops 20000000 | bytes 100000 | tf_op jit(solution)/shard_map/pack/pallas_call | solution.py:127
  13.4 15.5 %all-to-all-start = ((f32[16,8,128]{2,1,0:T(8,128)}), f32[16,8,128]{2,1,0:T(8,128)}, u32[]{:S(2)}, u32[]{:S(2)}) async-start(f32[16,8,128]{2,1,0:T(8,128)} %get-tuple-element.18), calls=%async_computation | async-start | bytes 131072 | tf_op jit(solution)/shard_map/all_to_all | solution.py:432
  29.5 0.0 collective-permute-done.4
  29.5 0.7 collective-permute-start.5
  30.2 0.0 collective-permute-done
  30.2 1.6 %broadcast_select_fusion = f32[4,3,32,128]{3,2,1,0:T(8,128)} fusion(f32[4,3,32,128]{3,2,1,0:T(8,128)} %collective-permute-done, pred[]{:T(512)S(6)} %eq.6), kind=kLoop, calls=%fused_computation | loop fusion | flops 49152 | bytes 393217 | tf_op jit(solution)/shard_map/jit(_where)/select_n | solution.py:434
  31.8 8.4 %collective-permute-start.3 = (f32[4,3,32,128]{3,2,1,0:T(8,128)}, f32[4,3,32,128]{3,2,1,0:T(8,128)}, u32[]{:S(2)}, u32[]{:S(2)}) collective-permute-start(f32[4,3,32,128]{3,2,1,0:T(8,128)} %broadcast_select_fusion), channel_id=1, source_target_pairs={{0,4},{4,8},{8,12},{7,3},{11,7},{15,11},{16,20},{20,24},{24,28},{2... | collective-permute-start | bytes 589832 | tf_op jit(solution)/shard_map/ppermute | solution.py:436
  40.2 2.3 %collective-permute-start.1 = (f32[7,3,32,128]{3,2,1,0:T(8,128)}, f32[7,3,32,128]{3,2,1,0:T(8,128)}, u32[]{:S(2)}, u32[]{:S(2)}) collective-permute-start(f32[7,3,32,128]{3,2,1,0:T(8,128)} %get-tuple-element.23), channel_id=1, source_target_pairs={{0,1},{1,2},{2,3},{4,5},{5,6},{6,7},{8,9},{9,10},{10,11},{12,13},{... | collective-permute-start | bytes 1032200 | tf_op jit(solution)/shard_map/ppermute | solution.py:438
  42.5 1.3 %collective-permute-start.2 = (f32[7,3,32,128]{3,2,1,0:T(8,128)}, f32[7,3,32,128]{3,2,1,0:T(8,128)}, u32[]{:S(2)}, u32[]{:S(2)}) collective-permute-start(f32[7,3,32,128]{3,2,1,0:T(8,128)} %get-tuple-element.24), channel_id=1, source_target_pairs={{1,0},{2,1},{3,2},{5,4},{6,5},{7,6},{9,8},{10,9},{11,10},{13,12},{... | collective-permute-start | bytes 1032200 | tf_op jit(solution)/shard_map/ppermute | solution.py:439
  43.8 0.0 all-to-all-done.got_ref
  43.8 0.0 copy-done.1
  43.8 0.0 copy-done
  43.8 0.0 copy-done.2
  43.8 7.9 %inner.1 = (f32[6,16,32,128]{3,2,1,0:T(8,128)}, f32[32,16,128]{2,1,0:T(8,128)S(1)}, f32[2,6,2,32,128]{4,3,2,1,0:T(8,128)S(1)}, f32[2,6,2,32,128]{4,3,2,1,0:T(8,1...) custom-call(f32[1]{0:T(128)S(6)} %copy.11.omega_ref, f32[16,8,128]{2,1,0:T(8,128)} %all-to-all-done.got_ref, ...), custom_call_target="tpu_custom_call" | custom-call | flops 10000000000 | bytes 30000000 | tf_op jit(solution)/shard_map/inner/pallas_call | solution.py:271
  51.7 0.0 collective-permute-done.5.staged_hbm
  51.7 0.0 collective-permute-done.3.direct_hbm
  51.8 0.0 collective-permute-done.1.before_hbm
  51.8 0.4 collective-permute-done.2.after_hbm
  52.2 3.3 %outer.1 = (f32[6,16,32,128]{3,2,1,0:T(8,128)}, f32[32,16,128]{2,1,0:T(8,128)S(1)}) custom-call(f32[1]{0:T(128)S(6)} %copy.11.omega_ref, f32[32,16,128]{2,1,0:T(8,128)S(1)} %get-tuple-element.19.inner_grad_ref, f32[6,16,32,128]{3,2,1,0:T(8,128)S(1)} %bitcast.9, f32[6,16,32,128]{3,2,1,0:T(8,128)S(1)} %bitcast.11, ...), custom_call_target="tpu_custom_call", output_to_operand_aliasing={{0}: (12, {})} | custom-call | flops 100000000 | bytes 3000000 | tf_op jit(solution)/shard_map/outer/pallas_call | solution.py:392
  55.5 22.3 %all_to_all.10 = f32[32,16,128]{2,1,0:T(8,128)S(1)} all-to-all(f32[32,16,128]{2,1,0:T(8,128)S(1)} %get-tuple-element.33), channel_id=1, replica_groups=mesh['tx'=32,'slab'=16] {'tx'}, dimensions={0} | all-to-all | bytes 524288 | tf_op jit(solution)/shard_map/all_to_all | solution.py:444
  77.8 0.6 reduce_sum.9
Async XLA Ops:
  0.6 43.2 %copy-start.1 = (f32[1,6,16,32,128]{4,3,2,1,0:T(8,128)S(1)}, f32[1,6,16,32,128]{4,3,2,1,0:T(8,128)}, u32[]{:S(2)}) copy-start(f32[1,6,16,32,128]{4,3,2,1,0:T(8,128)} %param.7) | copy-start | bytes 4718596
  2.5 41.3 %copy-start = (f32[1,6,16,32,128]{4,3,2,1,0:T(8,128)S(1)}, f32[1,6,16,32,128]{4,3,2,1,0:T(8,128)}, u32[]{:S(2)}) copy-start(f32[1,6,16,32,128]{4,3,2,1,0:T(8,128)} %param.8) | copy-start | bytes 4718596
  2.5 41.3 %copy-start.2 = (f32[16,32,128]{2,1,0:T(8,128)S(1)}, f32[16,32,128]{2,1,0:T(8,128)}, u32[]{:S(2)}) copy-start(f32[16,32,128]{2,1,0:T(8,128)} %sigma_hbm.5) | copy-start | bytes 786436
  2.5 27.7 %collective-permute-start = (f32[4,3,32,128]{3,2,1,0:T(8,128)}, f32[4,3,32,128]{3,2,1,0:T(8,128)}, u32[]{:S(2)}, u32[]{:S(2)}) collective-permute-start(f32[4,3,32,128]{3,2,1,0:T(8,128)} %get-tuple-element.20), channel_id=1, source_target_pairs={{3,0},{7,4},{11,8},{15,12},{0,3},{4,7},{8,11},{12,15},{19,16},{23,... | collective-permute-start | bytes 589832 | tf_op jit(solution)/shard_map/ppermute | solution.py:429
  8.1 21.4 %collective-permute-start.4 = (f32[3,3,32,128]{3,2,1,0:T(8,128)}, f32[3,3,32,128]{3,2,1,0:T(8,128)}, u32[]{:S(2)}, u32[]{:S(2)}) collective-permute-start(f32[3,3,32,128]{3,2,1,0:T(8,128)} %get-tuple-element.26), channel_id=1, source_target_pairs={{3,1},{7,5},{11,9},{15,13},{0,2},{4,6},{8,10},{12,14},{19,17},{23,... | collective-permute-start | bytes 442376 | tf_op jit(solution)/shard_map/ppermute | solution.py:430
  13.4 30.4 %all-to-all-start = ((f32[16,8,128]{2,1,0:T(8,128)}), f32[16,8,128]{2,1,0:T(8,128)}, u32[]{:S(2)}, u32[]{:S(2)}) async-start(f32[16,8,128]{2,1,0:T(8,128)} %get-tuple-element.18), calls=%async_computation | async-start | bytes 131072 | tf_op jit(solution)/shard_map/all_to_all | solution.py:432
  29.5 22.2 %collective-permute-start.5 = (f32[3,3,32,128]{3,2,1,0:T(8,128)}, f32[3,3,32,128]{3,2,1,0:T(8,128)S(1)}, u32[]{:S(2)}, u32[]{:S(2)}) collective-permute-start(f32[3,3,32,128]{3,2,1,0:T(8,128)} %collective-permute-done.4), channel_id=1, source_target_pairs={{1,4},{5,8},{9,12},{6,3},{10,7},{14,11},{17,20},{21,24},{25,28},{2... | collective-permute-start | bytes 442376 | tf_op jit(solution)/shard_map/ppermute | solution.py:437
  31.8 19.9 %collective-permute-start.3 = (f32[4,3,32,128]{3,2,1,0:T(8,128)}, f32[4,3,32,128]{3,2,1,0:T(8,128)}, u32[]{:S(2)}, u32[]{:S(2)}) collective-permute-start(f32[4,3,32,128]{3,2,1,0:T(8,128)} %broadcast_select_fusion), channel_id=1, source_target_pairs={{0,4},{4,8},{8,12},{7,3},{11,7},{15,11},{16,20},{20,24},{24,28},{2... | collective-permute-start | bytes 589832 | tf_op jit(solution)/shard_map/ppermute | solution.py:436
  40.2 11.5 %collective-permute-start.1 = (f32[7,3,32,128]{3,2,1,0:T(8,128)}, f32[7,3,32,128]{3,2,1,0:T(8,128)}, u32[]{:S(2)}, u32[]{:S(2)}) collective-permute-start(f32[7,3,32,128]{3,2,1,0:T(8,128)} %get-tuple-element.23), channel_id=1, source_target_pairs={{0,1},{1,2},{2,3},{4,5},{5,6},{6,7},{8,9},{9,10},{10,11},{12,13},{... | collective-permute-start | bytes 1032200 | tf_op jit(solution)/shard_map/ppermute | solution.py:438
  42.5 9.7 %collective-permute-start.2 = (f32[7,3,32,128]{3,2,1,0:T(8,128)}, f32[7,3,32,128]{3,2,1,0:T(8,128)}, u32[]{:S(2)}, u32[]{:S(2)}) collective-permute-start(f32[7,3,32,128]{3,2,1,0:T(8,128)} %get-tuple-element.24), channel_id=1, source_target_pairs={{1,0},{2,1},{3,2},{5,4},{6,5},{7,6},{9,8},{10,9},{11,10},{13,12},{... | collective-permute-start | bytes 1032200 | tf_op jit(solution)/shard_map/ppermute | solution.py:439

commit v5 on v3

--- a/solution.py
+++ b/solution.py
@@ -10,6 +10,7 @@
 SWEEPS = 3
 CAP = 32
 LANES = 128
+CORES = 2
 COLUMNS = 4
 NT = (((1,), (1,)), ((), ()))
 
@@ -32,40 +33,38 @@
 
 def pack_kernel(
     slabs, vals_ref, slab_ref, cell_ref, prev_hbm, sigma_hbm,
-    out_ref, highest_hbm, lowest_hbm, cross_a_hbm, cross_b_hbm, rows_ref, sems,
+    out_ref, part_a_ref, part_b_ref, highest_ref, lowest_ref, rows_ref, sems,
 ):
     comps, width = prev_hbm.shape[:2]
-    split = cross_a_hbm.shape[0]
+    copies = []
+    for n, (first, ref) in enumerate(((width - SWEEPS, highest_ref), (0, lowest_ref))):
+        layers = pl.ds(first, SWEEPS)
+        copies.append(pltpu.make_async_copy(prev_hbm.at[:, layers], ref.at[pl.ds(0, comps)], sems.at[2 * n]))
+        copies.append(pltpu.make_async_copy(sigma_hbm.at[layers], ref.at[comps], sems.at[2 * n + 1]))
+    split = part_a_ref.shape[0]
     last = lax.axis_index("slab") % COLUMNS == COLUMNS - 1
-    upper, lower = pl.ds(width - SWEEPS, SWEEPS), pl.ds(0, SWEEPS)
-
-    def crossing(layers):
+
+    def parts(first):
+        layers = pl.ds(first, SWEEPS)
         return [
-            pltpu.make_async_copy(prev_hbm.at[pl.ds(0, split), layers], cross_a_hbm, sems.at[4]),
+            pltpu.make_async_copy(prev_hbm.at[pl.ds(0, split), layers], part_a_ref, sems.at[4]),
             pltpu.make_async_copy(
-                prev_hbm.at[pl.ds(split, comps - split), layers], cross_b_hbm.at[pl.ds(0, comps - split)], sems.at[5]
+                prev_hbm.at[pl.ds(split, comps - split), layers], part_b_ref.at[pl.ds(0, comps - split)], sems.at[5]
             ),
-            pltpu.make_async_copy(sigma_hbm.at[layers], cross_b_hbm.at[comps - split], sems.at[6]),
+            pltpu.make_async_copy(sigma_hbm.at[layers], part_b_ref.at[comps - split], sems.at[6]),
         ]
-
-    whole = [
-        pltpu.make_async_copy(prev_hbm.at[:, upper], highest_hbm.at[pl.ds(0, comps)], sems.at[0]),
-        pltpu.make_async_copy(sigma_hbm.at[upper], highest_hbm.at[comps], sems.at[1]),
-        pltpu.make_async_copy(prev_hbm.at[:, lower], lowest_hbm.at[pl.ds(0, comps)], sems.at[2]),
-        pltpu.make_async_copy(sigma_hbm.at[lower], lowest_hbm.at[comps], sems.at[3]),
-    ]
 
     @pl.when(last)
     def _():
-        for copy in crossing(upper):
+        for copy in parts(width - SWEEPS):
             copy.start()
 
     @pl.when(jnp.logical_not(last))
     def _():
-        for copy in crossing(lower):
+        for copy in parts(0):
             copy.start()
 
-    for copy in whole:
+    for copy in copies:
         copy.start()
 
     count = vals_ref.shape[2]
@@ -97,7 +96,7 @@
             out_ref[d] = jnp.where(
                 lane < shift, pltpu.roll(tiles[q], shift, 1), pltpu.roll(tiles[q + 1], shift, 1)
             )
-    for copy in crossing(lower) + whole:
+    for copy in parts(0) + copies:
         copy.wait()
 
 
@@ -108,11 +107,13 @@
     vmem = pl.BlockSpec(memory_space=pltpu.VMEM)
     return pl.pallas_call(
         functools.partial(pack_kernel, slabs),
-        out_shape=[jax.ShapeDtypeStruct((slabs, 8, LANES), f32)] + [
-            jax.ShapeDtypeStruct((blocks, SWEEPS, ny, nz), f32) for blocks in (comps + 1, comps + 1, split, comps + 1 - split)
+        out_shape=[jax.ShapeDtypeStruct((slabs, 8, LANES), f32)]
+        + [
+            jax.ShapeDtypeStruct((blocks, SWEEPS, ny, nz), f32)
+            for blocks in (split, comps + 1 - split, comps + 1, comps + 1)
         ],
         in_specs=[vmem, vmem, vmem, hbm, hbm],
-        out_specs=[vmem, hbm, hbm, hbm, hbm],
+        out_specs=[vmem] * 5,
         scratch_shapes=[pltpu.VMEM((8, vals.shape[2]), f32), pltpu.SemaphoreType.DMA((7,))],
         cost_estimate=pl.CostEstimate(flops=20_000_000, bytes_accessed=100_000, transcendentals=0),
         name="pack",
@@ -161,16 +162,17 @@
 
 
 def inner_kernel(
-    factor, omega_ref, got_ref, sigma_ref, prev_hbm, fwd_hbm,
+    factor, omega_ref, got_ref, sigma_hbm, prev_hbm, fwd_hbm,
     adjoint_hbm, grad_ref, field_1_hbm, field_2_hbm, source_hbm, coef_hbm,
-    field_0, field_1, field_2, field_3, fwd, source, coef, onehot, sems,
+    field_0, field_1, field_2, field_3, fwd, sig, source, coef, onehot, sems,
 ):
     comps, width, ny, nz = field_0.shape
     rim = SWEEPS - 1
     load_prev = pltpu.make_async_copy(prev_hbm, field_0, sems.at[0])
     load_fwd = pltpu.make_async_copy(fwd_hbm, fwd, sems.at[1])
-    load_prev.start()
-    load_fwd.start()
+    load_sigma = pltpu.make_async_copy(sigma_hbm, sig, sems.at[11])
+    for load in (load_prev, load_sigma, load_fwd):
+        load.start()
 
     own = regroup(got_ref, 1)
     count = own.shape[1]
@@ -199,10 +201,10 @@
             source[c, at:at + rim] = result.reshape(rim, ny, nz)
 
     omega = omega_ref[0]
-    coef[0], coef[1] = coefficients(omega, sigma_ref[...])
+    load_sigma.wait()
+    coef[0], coef[1] = coefficients(omega, sig[...])
     beside = neighbour_sum(ny, nz)
     load_prev.wait()
-    load_fwd.wait()
 
     def sweep(old, new, first, last):
         def layer(i, carry):
@@ -221,11 +223,12 @@
             if last:
                 grad_ref[:, pl.ds(x, 1), :] = (terms * (omega * factor)).reshape(ny, 1, nz)
             return carry
-        lax.fori_loop(0, new.shape[1], layer, 0)
+        lax.fori_loop(0, new.shape[1], layer, 0, unroll=new.shape[1] // 2)
 
     grad_ref[...] = jnp.zeros_like(grad_ref)
     sweep(field_0, field_1, 1, False)
     sweep(field_1, field_2, 2, False)
+    load_fwd.wait()
     sweep(field_2, field_3, 3, True)
     stores = [pltpu.make_async_copy(field_3, adjoint_hbm.at[:, pl.ds(3, width - 6)], sems.at[2])]
     for s in range(2):
@@ -254,7 +257,7 @@
         out_shape=[jax.ShapeDtypeStruct(shape, f32) for shape in (
             prev.shape, (ny, width, nz), (2, comps, 2) + cells, (2, comps, 2) + cells, (2, comps, 5) + cells, (2, 2, 3) + cells,
         )],
-        in_specs=[pl.BlockSpec(memory_space=pltpu.SMEM), vmem, vmem, hbm, hbm],
+        in_specs=[pl.BlockSpec(memory_space=pltpu.SMEM), vmem, hbm, hbm, hbm],
         out_specs=[hbm, vmem, hbm, hbm, hbm, hbm],
         scratch_shapes=[
             pltpu.VMEM((comps, width) + cells, f32),
@@ -262,12 +265,13 @@
             pltpu.VMEM((comps, width - 4) + cells, f32),
             pltpu.VMEM((comps, width - 6) + cells, f32),
             pltpu.VMEM((comps, width) + cells, f32),
+            pltpu.VMEM((width,) + cells, f32),
             pltpu.VMEM((comps, width + 4) + cells, f32),
             pltpu.VMEM((2, width) + cells, f32),
             pltpu.VMEM((comps * nz, 2 * count), jnp.bfloat16),
-            pltpu.SemaphoreType.DMA((11,)),
+            pltpu.SemaphoreType.DMA((12,)),
         ],
-        compiler_params=pltpu.CompilerParams(vmem_limit_bytes=40 * 1024 * 1024),
+        compiler_params=pltpu.CompilerParams(vmem_limit_bytes=20 * 1024 * 1024),
         cost_estimate=pl.CostEstimate(flops=10_000_000_000, bytes_accessed=30_000_000, transcendentals=0),
         name="inner",
     )(omega, got, sigma, prev, fwd)
@@ -276,8 +280,8 @@
 def outer_kernel(
     slab_count, factor, omega_ref, inner_grad_ref, prev_hbm, fwd_hbm, before_hbm, after_hbm, direct_hbm, staged_hbm,
     field_1_hbm, field_2_hbm, source_hbm, coef_hbm, inner_adjoint_hbm,
-    adjoint_hbm, grad_ref,
-    field_0, field_1, field_2, field_3, fwd, sig, source, coef, sems, halo_sems,
+    adjoint_hbm, keep_ref, give_ref,
+    field_0, field_1, field_2, field_3, fwd, sig, source, coef, grad_ref, sems, halo_sems,
 ):
     comps, width, ny, nz = prev_hbm.shape
     me = lax.axis_index("slab")
@@ -351,7 +355,7 @@
                 if number == 2:
                     grad_ref[:, pl.ds(k + s * (width - 3), 1), :] = (terms * (omega * factor)).reshape(ny, 1, nz)
             return carry
-        lax.fori_loop(0, 3, layer, 0)
+        lax.fori_loop(0, 3, layer, 0, unroll=3)
 
     sweep(field_0, field_1, 0)
     sweep(field_1, field_2, 1)
@@ -359,6 +363,10 @@
     stores = [pltpu.make_async_copy(field_3.at[s], adjoint_hbm.at[:, pl.ds(s * (width - 3), 3)], sems.at[6 * s]) for s in range(2)]
     for store in stores:
         store.start()
+    core = lax.axis_index("tx") % CORES
+    for i in range(ny // CORES):
+        keep_ref[i] = grad_ref[CORES * i + core]
+        give_ref[i] = grad_ref[CORES * i + 1 - core]
     for store in stores:
         store.wait()
 
@@ -371,9 +379,9 @@
     cells = (ny, nz)
     return pl.pallas_call(
         functools.partial(outer_kernel, slab_count, factor),
-        out_shape=(jax.ShapeDtypeStruct(prev.shape, f32), jax.ShapeDtypeStruct(grad.shape, f32)),
+        out_shape=(jax.ShapeDtypeStruct(prev.shape, f32),) + (jax.ShapeDtypeStruct((ny // CORES, width, nz), f32),) * 2,
         in_specs=[pl.BlockSpec(memory_space=pltpu.SMEM), vmem] + [hbm] * 11,
-        out_specs=(hbm, vmem),
+        out_specs=(hbm, vmem, vmem),
         scratch_shapes=[
             pltpu.VMEM((2, comps, 5) + cells, f32),
             pltpu.VMEM((2, comps, 5) + cells, f32),
@@ -383,11 +391,12 @@
             pltpu.VMEM((2, 3) + cells, f32),
             pltpu.VMEM((2, comps, 5) + cells, f32),
             pltpu.VMEM((2, 2, 5) + cells, f32),
+            pltpu.VMEM(grad.shape, f32),
             pltpu.SemaphoreType.DMA((12,)),
             pltpu.SemaphoreType.DMA((2, 3)),
         ],
         input_output_aliases={12: 0},
-        compiler_params=pltpu.CompilerParams(vmem_limit_bytes=24 * 1024 * 1024),
+        compiler_params=pltpu.CompilerParams(vmem_limit_bytes=12 * 1024 * 1024),
         cost_estimate=pl.CostEstimate(flops=100_000_000, bytes_accessed=3_000_000, transcendentals=0),
         name="outer",
     )(omega, grad, prev, fwd, *halos, *from_inner, adjoint)
@@ -405,10 +414,13 @@
     cross_a = [(r, r + COLUMNS) for r in rows[:-1]] + [(r + 3, r + 3 - COLUMNS) for r in rows[1:]]
     cross_b = [(r + 1, r + COLUMNS) for r in rows[:-1]] + [(r + 2, r + 3 - COLUMNS) for r in rows[1:]]
     vals = jnp.transpose(res_vals, (1, 0, 2))
-    send, highest, lowest, part_a, part_b = pack(vals, rec_slab.reshape(1, -1), rec_cell, prev, sigma, slabs, 4)
+    send, part_a, part_b, highest, lowest = pack(vals, rec_slab.reshape(1, -1), rec_cell, prev, sigma, slabs, 4)
     part_a = lax.ppermute(part_a, "slab", stage_a)
     part_b = lax.ppermute(part_b, "slab", stage_b)
     got = lax.all_to_all(send, "slab", split_axis=0, concat_axis=0, tiled=True)
+    edge = (lax.axis_index("slab") % COLUMNS) % (COLUMNS - 1) == 0
+    part_a = jnp.where(edge, part_a, 0.0)
+    part_a, highest, lowest = lax.optimization_barrier((part_a, highest, lowest))
     part_a = lax.ppermute(part_a, "slab", cross_a)
     part_b = lax.ppermute(part_b, "slab", cross_b)
     before = lax.ppermute(highest, "slab", up)
@@ -416,8 +428,10 @@
     factor = 1.0 / (3.0 * pairs * groups) ** 0.5
     adjoint, terms, *from_inner = inner(omega, got, sigma, prev, fwd, factor)
     halos = (before, after, part_a, part_b)
-    adjoint, terms = outer(omega, terms, prev, fwd, halos, from_inner, adjoint, slabs, factor)
-    parts = lax.all_to_all(terms, "tx", split_axis=0, concat_axis=0, tiled=True)
+    adjoint, terms, other = outer(omega, terms, prev, fwd, halos, from_inner, adjoint, slabs, factor)
+    terms += lax.ppermute(other, "tx", [(i, i ^ 1) for i in range(groups)])
+    same_core = [list(range(core, groups, CORES)) for core in range(CORES)]
+    parts = lax.all_to_all(terms, "tx", split_axis=0, concat_axis=0, axis_index_groups=same_core, tiled=True)
     gradient = jnp.sum(parts, axis=0)[:, None, :]
     return (adjoint[None], gradient)
 

time: 110 us -> 73.4 us (0.67); the launches traced: 108 us -> 73 us
  Pallas kernels: 47.2 us -> 14.2 us
  blocking collectives: 15.6 us -> 12.7 us
  starting transfers between devices: 30.4 us -> 32 us
  waiting for transfers between devices: 11.8 us -> 10.6 us
    pallas_call x1, Pallas kernels: 33.9 us -> 3.55 us  [pack(): pl.pallas_call(functools.partial(pack_kernel, slabs), out_shape=[jax.Shap...]
    ppermute x1, waiting for transfers between devices: 7.12 us -> 1.05 us  [shards(): part_b = lax.ppermute(part_b, 'slab', cross_b)]
    ppermute x1, starting transfers between devices: 2.01 us -> 7.5 us  [shards(): part_a = lax.ppermute(part_a, 'slab', stage_a)]
    all_to_all x1, starting transfers between devices: 18 us -> 12.8 us  [shards(): got = lax.all_to_all(send, 'slab', split_axis=0, concat_axis=0, tiled=True)]
    all_to_all x1, waiting for transfers between devices: 0.01 us -> 3.82 us  [shards(): got = lax.all_to_all(send, 'slab', split_axis=0, concat_axis=0, tiled=True)]
    all_to_all x1, blocking collectives: 15.6 us -> 12.7 us  [shards(): lax.all_to_all(terms, 'tx', split_axis=0, concat_axis=0, axis_index_group...]
    pallas_call x1, Pallas kernels: 9.19 us -> 7.04 us  [inner(): pl.pallas_call(functools.partial(inner_kernel, factor), out_shape=[jax.Sh...]
    ppermute x0 -> x1, starting transfers between devices: none -> 1.92 us  [shards(): terms += lax.ppermute(other, 'tx', [(i, i ^ 1) for i in range(groups)])]
  transfers between devices with their start and end apart: 7 -> 8, of which waited for: 2 -> 4; matrix products, arithmetic and copies ran while one was open for 0% -> 0% of each run, Pallas kernels for 8% -> 10%
where the time goes in v5:
time: 73.4 us; the launch traced here: 73 us
  starting transfers between devices  32 us (44%)
  Pallas kernels  14.2 us (19%)
  blocking collectives  12.7 us (17%)
  waiting for transfers between devices  10.6 us (14%)
  local copies, waits for them, and re-layouts  1.42 us (2%)
  between operations  1.41 us (2%)
    all_to_all x1, starting transfers between devices, shards(): got = lax.all_to_all(send, 'slab', split_axis=0, concat_axis=0, tiled=True)  12.8 us
    all_to_all x1, blocking collectives, shards(): lax.all_to_all(terms, 'tx', split_axis=0, concat_axis=0, axis_index_group...  12.7 us
    ppermute x1, starting transfers between devices, shards(): part_a = lax.ppermute(part_a, 'slab', stage_a)  7.5 us
    pallas_call x1, Pallas kernels, inner(): pl.pallas_call(functools.partial(inner_kernel, factor), out_shape=[jax.Sh...  7.04 us
    ppermute x1, starting transfers between devices, shards(): after = lax.ppermute(lowest, 'slab', down)  4.57 us
    ppermute x1, waiting for transfers between devices, shards(): part_a = lax.ppermute(part_a, 'slab', cross_a)  4.43 us
    all_to_all x1, waiting for transfers between devices, shards(): got = lax.all_to_all(send, 'slab', split_axis=0, concat_axis=0, tiled=True)  3.82 us
    pallas_call x1, Pallas kernels, outer(): pl.pallas_call(functools.partial(outer_kernel, slab_count, factor), out_s...  3.58 us
  transfers between devices with their start and end apart: 8, of which 4 were waited for; matrix products, arithmetic and copies ran while one was open for 0% of the time, Pallas kernels for 10%

profile of v5, /device:TPU:24, one launch (start us, length us, event | category | flops | bytes accessed | tf_op | source)
XLA Modules:
  0.0 73.0 jit_solution(980418314323674681)
XLA Ops:
  0.6 0.0 copy-start.2
  0.6 0.0 copy-start
  0.7 3.6 %pack.1 = (f32[16,8,128]{2,1,0:T(8,128)}, f32[4,3,32,128]{3,2,1,0:T(8,128)}, f32[3,3,32,128]{3,2,1,0:T(8,128)}, f32[7,3,32,128]{3,2,1,0:T(8,128)}, f32[7,3,32,128]{3,2,1,0:T(8,128)}) custom-call(f32[6,1,256]{2,1,0:T(1,128)} %bitcast.13, s32[1,256]{1,0:T(1,128)} %bitcast.14, s32[1,256]{1,0:T(1,128)} %cell_ref.1, f32[6,16,32,128]{3,2,1,0:T(8,128)} %bitcast.6, ...), custom_call_target="tpu_custom_call" | custom-call | flops 20000000 | bytes 100000 | tf_op jit(solution)/shard_map/pack/pallas_call | solution.py:108
  4.2 7.5 %collective-permute-start = (f32[4,3,32,128]{3,2,1,0:T(8,128)}, f32[4,3,32,128]{3,2,1,0:T(8,128)S(1)}, u32[]{:S(2)}, u32[]{:S(2)}) collective-permute-start(f32[4,3,32,128]{3,2,1,0:T(8,128)} %get-tuple-element.21), channel_id=1, source_target_pairs={{3,0},{7,4},{11,8},{15,12},{0,3},{4,7},{8,11},{12,15},{19,16},{23,... | collective-permute-start | bytes 589832 | tf_op jit(solution)/shard_map/ppermute | solution.py:418
  11.7 1.3 %collective-permute-start.4 = (f32[3,3,32,128]{3,2,1,0:T(8,128)}, f32[3,3,32,128]{3,2,1,0:T(8,128)S(1)}, u32[]{:S(2)}, u32[]{:S(2)}) collective-permute-start(f32[3,3,32,128]{3,2,1,0:T(8,128)} %get-tuple-element.27), channel_id=1, source_target_pairs={{3,1},{7,5},{11,9},{15,13},{0,2},{4,6},{8,10},{12,14},{19,17},{23,... | collective-permute-start | bytes 442376 | tf_op jit(solution)/shard_map/ppermute | solution.py:419
  13.0 12.8 %all-to-all-start = ((f32[16,8,128]{2,1,0:T(8,128)}), f32[16,8,128]{2,1,0:T(8,128)S(1)}, u32[]{:S(2)}, u32[]{:S(2)}) async-start(f32[16,8,128]{2,1,0:T(8,128)} %get-tuple-element.19), calls=%async_computation | async-start | bytes 131072 | tf_op jit(solution)/shard_map/all_to_all | solution.py:420
  26.5 0.0 collective-permute-done.4
  26.5 1.3 %collective-permute-start.5 = (f32[3,3,32,128]{3,2,1,0:T(8,128)S(1)}, f32[3,3,32,128]{3,2,1,0:T(8,128)S(1)}, u32[]{:S(2)}, u32[]{:S(2)}) collective-permute-start(f32[3,3,32,128]{3,2,1,0:T(8,128)S(1)} %collective-permute-done.4), channel_id=1, source_target_pairs={{1,4},{5,8},{9,12},{6,3},{10,7},{14,11},{17,20},{21,24},{25,28},{2... | collective-permute-start | bytes 442376 | tf_op jit(solution)/shard_map/ppermute | solution.py:425
  27.8 0.0 collective-permute-done
  27.8 1.3 %collective-permute-start.3 = (f32[4,3,32,128]{3,2,1,0:T(8,128)S(1)}, f32[4,3,32,128]{3,2,1,0:T(8,128)S(1)}, u32[]{:S(2)}, u32[]{:S(2)}) collective-permute-start(f32[4,3,32,128]{3,2,1,0:T(8,128)S(1)} %broadcast_select_fusion), channel_id=1, source_target_pairs={{0,4},{4,8},{8,12},{7,3},{11,7},{15,11},{16,20},{20,24},{24,28},{2... | collective-permute-start | bytes 589832 | tf_op jit(solution)/shard_map/ppermute | solution.py:424
  29.1 1.3 %collective-permute-start.1 = (f32[7,3,32,128]{3,2,1,0:T(8,128)}, f32[7,3,32,128]{3,2,1,0:T(8,128)S(1)}, u32[]{:S(2)}, u32[]{:S(2)}) collective-permute-start(f32[7,3,32,128]{3,2,1,0:T(8,128)} %get-tuple-element.24), channel_id=1, source_target_pairs={{0,1},{1,2},{2,3},{4,5},{5,6},{6,7},{8,9},{9,10},{10,11},{12,13},{... | collective-permute-start | bytes 1032200 | tf_op jit(solution)/shard_map/ppermute | solution.py:426
  30.4 4.6 %collective-permute-start.2 = (f32[7,3,32,128]{3,2,1,0:T(8,128)}, f32[7,3,32,128]{3,2,1,0:T(8,128)S(1)}, u32[]{:S(2)}, u32[]{:S(2)}) collective-permute-start(f32[7,3,32,128]{3,2,1,0:T(8,128)} %get-tuple-element.25), channel_id=1, source_target_pairs={{1,0},{2,1},{3,2},{5,4},{6,5},{7,6},{9,8},{10,9},{11,10},{13,12},{... | collective-permute-start | bytes 1032200 | tf_op jit(solution)/shard_map/ppermute | solution.py:427
  35.0 3.8 %all-to-all-done.got_ref = f32[16,8,128]{2,1,0:T(8,128)S(1)} async-done(((f32[16,8,128]{2,1,0:T(8,128)}), f32[16,8,128]{2,1,0:T(8,128)S(1)}, u32[]{:S(2)}, u32[]{:S(2)}) %all-to-all-start) | async-done | bytes 65568 | tf_op jit(solution)/shard_map/all_to_all | solution.py:420
  38.8 0.0 copy-done.2
  38.8 0.0 copy-done
  38.8 0.0 copy-start.1
  38.8 1.4 %copy-done.1 = f32[1,6,16,32,128]{4,3,2,1,0:T(8,128)S(1)} copy-done((f32[1,6,16,32,128]{4,3,2,1,0:T(8,128)S(1)}, f32[1,6,16,32,128]{4,3,2,1,0:T(8,128)}, u32[]{:S(2)}) %copy-start.1) | copy-done | bytes 1572888
  40.2 7.0 %inner.1 = (f32[6,16,32,128]{3,2,1,0:T(8,128)}, f32[32,16,128]{2,1,0:T(8,128)S(1)}, f32[2,6,2,32,128]{4,3,2,1,0:T(8,128)S(1)}, f32[2,6,2,32,128]{4,3,2,1,0:T(8,1...) custom-call(f32[1]{0:T(128)S(6)} %copy.11.omega_ref, ...), custom_call_target="tpu_custom_call" | custom-call | flops 10000000000 | bytes 30000000 | tf_op jit(solution)/shard_map/inner/pallas_call | solution.py:255
  47.3 1.1 %collective-permute-done.5.staged_hbm = f32[3,3,32,128]{3,2,1,0:T(8,128)S(1)} collective-permute-done((f32[3,3,32,128]{3,2,1,0:T(8,128)S(1)}, f32[3,3,32,128]{3,2,1,0:T(8,128)S(1)}, u32[]{:S(2)}, u32[]{:S(2)}) %collective-permute-start.5) | collective-permute-done | bytes 147488 | tf_op jit(solution)/shard_map/ppermute | solution.py:425
  48.3 4.4 %collective-permute-done.3.direct_hbm = f32[4,3,32,128]{3,2,1,0:T(8,128)S(1)} collective-permute-done((f32[4,3,32,128]{3,2,1,0:T(8,128)S(1)}, f32[4,3,32,128]{3,2,1,0:T(8,128)S(1)}, u32[]{:S(2)}, u32[]{:S(2)}) %collective-permute-start.3) | collective-permute-done | bytes 196640 | tf_op jit(solution)/shard_map/ppermute | solution.py:424
  52.8 0.0 collective-permute-done.1.before_hbm
  52.8 0.0 collective-permute-done.2.after_hbm
  52.8 3.6 %outer.1 = (f32[6,16,32,128]{3,2,1,0:T(8,128)}, f32[16,16,128]{2,1,0:T(8,128)S(1)}, f32[16,16,128]{2,1,0:T(8,128)S(1)}) custom-call(f32[1]{0:T(128)S(6)} %copy.11.omega_ref, f32[32,16,128]{2,1,0:T(8,128)S(1)} %get-tuple-element.20.inner_grad_ref, f32[6,16,32,128]{3,2,1,0:T(8,128)S(1)} %bitcast.8, ...), custom_call_target="tpu_custom_call", output_to_operand_aliasing={{0}: (12, {})} | custom-call | flops 100000000 | bytes 3000000 | tf_op jit(solution)/shard_map/outer/pallas_call | solution.py:380
  56.4 1.9 %collective-permute-start.6 = (f32[16,16,128]{2,1,0:T(8,128)S(1)}, f32[16,16,128]{2,1,0:T(8,128)S(1)}, u32[]{:S(2)}, u32[]{:S(2)}) collective-permute-start(f32[16,16,128]{2,1,0:T(8,128)S(1)} %get-tuple-element.35), channel_id=1, source_target_pairs={{0,16},{16,0},{32,48},{48,32},{64,80},{80,64},{96,112},{112,96},{1... | collective-permute-start | bytes 393224 | tf_op jit(solution)/shard_map/ppermute | solution.py:432
  58.3 1.3 %collective-permute-done.6 = f32[16,16,128]{2,1,0:T(8,128)S(1)} collective-permute-done((f32[16,16,128]{2,1,0:T(8,128)S(1)}, f32[16,16,128]{2,1,0:T(8,128)S(1)}, u32[]{:S(2)}, u32[]{:S(2)}) %collective-permute-start.6) | collective-permute-done | bytes 131104 | tf_op jit(solution)/shard_map/ppermute | solution.py:432
  59.6 12.7 %all_to_all.10 = f32[16,16,128]{2,1,0:T(8,128)S(1)} all-to-all(f32[16,16,128]{2,1,0:T(8,128)S(1)} %add.12), channel_id=1, replica_groups={{0,32,64,96,128,160,192,224,256,288,320,352,384,416,448,480},{16,48,80,..., dimensions={0} | all-to-all | bytes 262144 | tf_op jit(solution)/shard_map/all_to_all | solution.py:434
  72.3 0.6 reduce_sum.9
  (2 shorter events, 0.0 us)
Async XLA Ops:
  0.6 38.2 %copy-start.2 = (f32[16,32,128]{2,1,0:T(8,128)S(1)}, f32[16,32,128]{2,1,0:T(8,128)}, u32[]{:S(2)}) copy-start(f32[16,32,128]{2,1,0:T(8,128)} %sigma_hbm.3) | copy-start | bytes 786436
  0.6 38.2 %copy-start = (f32[1,6,16,32,128]{4,3,2,1,0:T(8,128)S(1)}, f32[1,6,16,32,128]{4,3,2,1,0:T(8,128)}, u32[]{:S(2)}) copy-start(f32[1,6,16,32,128]{4,3,2,1,0:T(8,128)} %param.8) | copy-start | bytes 4718596
  4.2 23.6 %collective-permute-start = (f32[4,3,32,128]{3,2,1,0:T(8,128)}, f32[4,3,32,128]{3,2,1,0:T(8,128)S(1)}, u32[]{:S(2)}, u32[]{:S(2)}) collective-permute-start(f32[4,3,32,128]{3,2,1,0:T(8,128)} %get-tuple-element.21), channel_id=1, source_target_pairs={{3,0},{7,4},{11,8},{15,12},{0,3},{4,7},{8,11},{12,15},{19,16},{23,... | collective-permute-start | bytes 589832 | tf_op jit(solution)/shard_map/ppermute | solution.py:418
  11.7 14.8 %collective-permute-start.4 = (f32[3,3,32,128]{3,2,1,0:T(8,128)}, f32[3,3,32,128]{3,2,1,0:T(8,128)S(1)}, u32[]{:S(2)}, u32[]{:S(2)}) collective-permute-start(f32[3,3,32,128]{3,2,1,0:T(8,128)} %get-tuple-element.27), channel_id=1, source_target_pairs={{3,1},{7,5},{11,9},{15,13},{0,2},{4,6},{8,10},{12,14},{19,17},{23,... | collective-permute-start | bytes 442376 | tf_op jit(solution)/shard_map/ppermute | solution.py:419
  13.0 25.8 %all-to-all-start = ((f32[16,8,128]{2,1,0:T(8,128)}), f32[16,8,128]{2,1,0:T(8,128)S(1)}, u32[]{:S(2)}, u32[]{:S(2)}) async-start(f32[16,8,128]{2,1,0:T(8,128)} %get-tuple-element.19), calls=%async_computation | async-start | bytes 131072 | tf_op jit(solution)/shard_map/all_to_all | solution.py:420
  26.5 21.8 %collective-permute-start.5 = (f32[3,3,32,128]{3,2,1,0:T(8,128)S(1)}, f32[3,3,32,128]{3,2,1,0:T(8,128)S(1)}, u32[]{:S(2)}, u32[]{:S(2)}) collective-permute-start(f32[3,3,32,128]{3,2,1,0:T(8,128)S(1)} %collective-permute-done.4), channel_id=1, source_target_pairs={{1,4},{5,8},{9,12},{6,3},{10,7},{14,11},{17,20},{21,24},{25,28},{2... | collective-permute-start | bytes 442376 | tf_op jit(solution)/shard_map/ppermute | solution.py:425
  27.8 24.9 %collective-permute-start.3 = (f32[4,3,32,128]{3,2,1,0:T(8,128)S(1)}, f32[4,3,32,128]{3,2,1,0:T(8,128)S(1)}, u32[]{:S(2)}, u32[]{:S(2)}) collective-permute-start(f32[4,3,32,128]{3,2,1,0:T(8,128)S(1)} %broadcast_select_fusion), channel_id=1, source_target_pairs={{0,4},{4,8},{8,12},{7,3},{11,7},{15,11},{16,20},{20,24},{24,28},{2... | collective-permute-start | bytes 589832 | tf_op jit(solution)/shard_map/ppermute | solution.py:424
  29.1 23.6 %collective-permute-start.1 = (f32[7,3,32,128]{3,2,1,0:T(8,128)}, f32[7,3,32,128]{3,2,1,0:T(8,128)S(1)}, u32[]{:S(2)}, u32[]{:S(2)}) collective-permute-start(f32[7,3,32,128]{3,2,1,0:T(8,128)} %get-tuple-element.24), channel_id=1, source_target_pairs={{0,1},{1,2},{2,3},{4,5},{5,6},{6,7},{8,9},{9,10},{10,11},{12,13},{... | collective-permute-start | bytes 1032200 | tf_op jit(solution)/shard_map/ppermute | solution.py:426
  30.4 22.4 %collective-permute-start.2 = (f32[7,3,32,128]{3,2,1,0:T(8,128)}, f32[7,3,32,128]{3,2,1,0:T(8,128)S(1)}, u32[]{:S(2)}, u32[]{:S(2)}) collective-permute-start(f32[7,3,32,128]{3,2,1,0:T(8,128)} %get-tuple-element.25), channel_id=1, source_target_pairs={{1,0},{2,1},{3,2},{5,4},{6,5},{7,6},{9,8},{10,9},{11,10},{13,12},{... | collective-permute-start | bytes 1032200 | tf_op jit(solution)/shard_map/ppermute | solution.py:427
  38.8 1.4 %copy-start.1 = (f32[1,6,16,32,128]{4,3,2,1,0:T(8,128)S(1)}, f32[1,6,16,32,128]{4,3,2,1,0:T(8,128)}, u32[]{:S(2)}) copy-start(f32[1,6,16,32,128]{4,3,2,1,0:T(8,128)} %param.7) | copy-start | bytes 4718596
  56.4 3.2 %collective-permute-start.6 = (f32[16,16,128]{2,1,0:T(8,128)S(1)}, f32[16,16,128]{2,1,0:T(8,128)S(1)}, u32[]{:S(2)}, u32[]{:S(2)}) collective-permute-start(f32[16,16,128]{2,1,0:T(8,128)S(1)} %get-tuple-element.35), channel_id=1, source_target_pairs={{0,16},{16,0},{32,48},{48,32},{64,80},{80,64},{96,112},{112,96},{1... | collective-permute-start | bytes 393224 | tf_op jit(solution)/shard_map/ppermute | solution.py:432

commit v6 on v5

--- a/solution.py
+++ b/solution.py
@@ -32,7 +32,7 @@
 
 
 def pack_kernel(
-    slabs, vals_ref, slab_ref, cell_ref, prev_hbm, sigma_hbm,
+    slabs, vals_ref, slab_ref, cell_ref, prev_hbm, sigma_hbm, fwd_hbm,
     out_ref, part_a_ref, part_b_ref, highest_ref, lowest_ref, rows_ref, sems,
 ):
     comps, width = prev_hbm.shape[:2]
@@ -100,7 +100,7 @@
         copy.wait()
 
 
-def pack(vals, target, cells, prev, sigma, slabs, split):
+def pack(vals, target, cells, prev, sigma, fwd, slabs, split):
     comps, _, ny, nz = prev.shape
     f32 = jnp.float32
     hbm = pl.BlockSpec(memory_space=pl.ANY)
@@ -112,12 +112,12 @@
             jax.ShapeDtypeStruct((blocks, SWEEPS, ny, nz), f32)
             for blocks in (split, comps + 1 - split, comps + 1, comps + 1)
         ],
-        in_specs=[vmem, vmem, vmem, hbm, hbm],
+        in_specs=[vmem, vmem, vmem, hbm, hbm, hbm],
         out_specs=[vmem] * 5,
         scratch_shapes=[pltpu.VMEM((8, vals.shape[2]), f32), pltpu.SemaphoreType.DMA((7,))],
         cost_estimate=pl.CostEstimate(flops=20_000_000, bytes_accessed=100_000, transcendentals=0),
         name="pack",
-    )(vals, target, cells, prev, sigma)
+    )(vals, target, cells, prev, sigma, fwd)
 
 
 def regroup(got_ref, part):
@@ -223,7 +223,7 @@
             if last:
                 grad_ref[:, pl.ds(x, 1), :] = (terms * (omega * factor)).reshape(ny, 1, nz)
             return carry
-        lax.fori_loop(0, new.shape[1], layer, 0, unroll=new.shape[1] // 2)
+        lax.fori_loop(0, new.shape[1], layer, 0, unroll=new.shape[1])
 
     grad_ref[...] = jnp.zeros_like(grad_ref)
     sweep(field_0, field_1, 1, False)
@@ -414,7 +414,7 @@
     cross_a = [(r, r + COLUMNS) for r in rows[:-1]] + [(r + 3, r + 3 - COLUMNS) for r in rows[1:]]
     cross_b = [(r + 1, r + COLUMNS) for r in rows[:-1]] + [(r + 2, r + 3 - COLUMNS) for r in rows[1:]]
     vals = jnp.transpose(res_vals, (1, 0, 2))
-    send, part_a, part_b, highest, lowest = pack(vals, rec_slab.reshape(1, -1), rec_cell, prev, sigma, slabs, 4)
+    send, part_a, part_b, highest, lowest = pack(vals, rec_slab.reshape(1, -1), rec_cell, prev, sigma, fwd, slabs, 4)
     part_a = lax.ppermute(part_a, "slab", stage_a)
     part_b = lax.ppermute(part_b, "slab", stage_b)
     got = lax.all_to_all(send, "slab", split_axis=0, concat_axis=0, tiled=True)

time: 73.4 us -> 74.8 us (1.019)
  starting transfers between devices: 32 us -> 33.3 us
    all_to_all x1, waiting for transfers between devices: 3.82 us -> 2.55 us  [shards(): got = lax.all_to_all(send, 'slab', split_axis=0, concat_axis=0, tiled=True)]
    ppermute x1, waiting for transfers between devices: 4.43 us -> 5.32 us  [shards(): part_a = lax.ppermute(part_a, 'slab', cross_a)]
  transfers between devices with their start and end apart: 8 -> 8, of which waited for: 4 -> 4; matrix products, arithmetic and copies ran while one was open for 0% -> 1% of each run, Pallas kernels for 10% -> 9%
where the time goes in v6:
time: 74.8 us; the launch traced here: 74.4 us
  starting transfers between devices  33.3 us (45%)
  Pallas kernels  13.7 us (18%)
  blocking collectives  12.7 us (17%)
  waiting for transfers between devices  11 us (15%)
  between operations  1.39 us (2%)
  other arithmetic  1.34 us (2%)
  local copies, waits for them, and re-layouts  0.96 us (1%)
    all_to_all x1, starting transfers between devices, shards(): got = lax.all_to_all(send, 'slab', split_axis=0, concat_axis=0, tiled=True)  12.8 us
    all_to_all x1, blocking collectives, shards(): lax.all_to_all(terms, 'tx', split_axis=0, concat_axis=0, axis_index_group...  12.7 us
    ppermute x1, starting transfers between devices, shards(): part_a = lax.ppermute(part_a, 'slab', stage_a)  7.5 us
    pallas_call x1, Pallas kernels, inner(): pl.pallas_call(functools.partial(inner_kernel, factor), out_shape=[jax.Sh...  6.77 us
    ppermute x1, waiting for transfers between devices, shards(): part_a = lax.ppermute(part_a, 'slab', cross_a)  5.32 us
    ppermute x1, starting transfers between devices, shards(): after = lax.ppermute(lowest, 'slab', down)  5.28 us
    pallas_call x1, Pallas kernels, pack(): pl.pallas_call(functools.partial(pack_kernel, slabs), out_shape=[jax.Shap...  3.57 us
    pallas_call x1, Pallas kernels, outer(): pl.pallas_call(functools.partial(outer_kernel, slab_count, factor), out_s...  3.39 us
  transfers between devices with their start and end apart: 8, of which 4 were waited for; matrix products, arithmetic and copies ran while one was open for 1% of the time, Pallas kernels for 9%

profile of v6, /device:TPU:24, one launch (start us, length us, event | category | flops | bytes accessed | tf_op | source)
XLA Modules:
  0.0 74.4 jit_solution(5800742566326914611)
XLA Ops:
  0.6 0.0 copy-start
  0.6 0.0 copy-start.1
  0.7 3.6 %pack.1 = (f32[16,8,128]{2,1,0:T(8,128)}, f32[4,3,32,128]{3,2,1,0:T(8,128)}, f32[3,3,32,128]{3,2,1,0:T(8,128)}, f32[7,3,32,128]{3,2,1,0:T(8,128)}, f32[7,3,32,128]{3,2,1,0:T(8,128)}) custom-call(f32[6,1,256]{2,1,0:T(1,128)} %bitcast.14, s32[1,256]{1,0:T(1,128)} %bitcast.15, s32[1,256]{1,0:T(1,128)} %cell_ref.1, f32[6,16,32,128]{3,2,1,0:T(8,128)} %bitcast.6, ...), custom_call_target="tpu_custom_call" | custom-call | flops 20000000 | bytes 100000 | tf_op jit(solution)/shard_map/pack/pallas_call | solution.py:108
  4.2 7.5 %collective-permute-start = (f32[4,3,32,128]{3,2,1,0:T(8,128)}, f32[4,3,32,128]{3,2,1,0:T(8,128)S(1)}, u32[]{:S(2)}, u32[]{:S(2)}) collective-permute-start(f32[4,3,32,128]{3,2,1,0:T(8,128)} %get-tuple-element.21), channel_id=1, source_target_pairs={{3,0},{7,4},{11,8},{15,12},{0,3},{4,7},{8,11},{12,15},{19,16},{23,... | collective-permute-start | bytes 589832 | tf_op jit(solution)/shard_map/ppermute | solution.py:418
  11.7 1.9 %collective-permute-start.4 = (f32[3,3,32,128]{3,2,1,0:T(8,128)}, f32[3,3,32,128]{3,2,1,0:T(8,128)}, u32[]{:S(2)}, u32[]{:S(2)}) collective-permute-start(f32[3,3,32,128]{3,2,1,0:T(8,128)} %get-tuple-element.27), channel_id=1, source_target_pairs={{3,1},{7,5},{11,9},{15,13},{0,2},{4,6},{8,10},{12,14},{19,17},{23,... | collective-permute-start | bytes 442376 | tf_op jit(solution)/shard_map/ppermute | solution.py:419
  13.7 12.8 %all-to-all-start = ((f32[16,8,128]{2,1,0:T(8,128)}), f32[16,8,128]{2,1,0:T(8,128)S(1)}, u32[]{:S(2)}, u32[]{:S(2)}) async-start(f32[16,8,128]{2,1,0:T(8,128)} %get-tuple-element.19), calls=%async_computation | async-start | bytes 131072 | tf_op jit(solution)/shard_map/all_to_all | solution.py:420
  27.1 0.0 collective-permute-done.4
  27.1 1.3 %collective-permute-start.5 = (f32[3,3,32,128]{3,2,1,0:T(8,128)}, f32[3,3,32,128]{3,2,1,0:T(8,128)}, u32[]{:S(2)}, u32[]{:S(2)}) collective-permute-start(f32[3,3,32,128]{3,2,1,0:T(8,128)} %collective-permute-done.4), channel_id=1, source_target_pairs={{1,4},{5,8},{9,12},{6,3},{10,7},{14,11},{17,20},{21,24},{25,28},{2... | collective-permute-start | bytes 442376 | tf_op jit(solution)/shard_map/ppermute | solution.py:425
  28.4 0.0 collective-permute-done
  28.5 0.7 broadcast_select_fusion
  29.2 1.3 %collective-permute-start.3 = (f32[4,3,32,128]{3,2,1,0:T(8,128)}, f32[4,3,32,128]{3,2,1,0:T(8,128)}, u32[]{:S(2)}, u32[]{:S(2)}) collective-permute-start(f32[4,3,32,128]{3,2,1,0:T(8,128)} %broadcast_select_fusion), channel_id=1, source_target_pairs={{0,4},{4,8},{8,12},{7,3},{11,7},{15,11},{16,20},{20,24},{24,28},{2... | collective-permute-start | bytes 589832 | tf_op jit(solution)/shard_map/ppermute | solution.py:424
  30.4 1.3 %collective-permute-start.1 = (f32[7,3,32,128]{3,2,1,0:T(8,128)}, f32[7,3,32,128]{3,2,1,0:T(8,128)S(1)}, u32[]{:S(2)}, u32[]{:S(2)}) collective-permute-start(f32[7,3,32,128]{3,2,1,0:T(8,128)} %get-tuple-element.24), channel_id=1, source_target_pairs={{0,1},{1,2},{2,3},{4,5},{5,6},{6,7},{8,9},{9,10},{10,11},{12,13},{... | collective-permute-start | bytes 1032200 | tf_op jit(solution)/shard_map/ppermute | solution.py:426
  31.7 5.3 %collective-permute-start.2 = (f32[7,3,32,128]{3,2,1,0:T(8,128)}, f32[7,3,32,128]{3,2,1,0:T(8,128)}, u32[]{:S(2)}, u32[]{:S(2)}) collective-permute-start(f32[7,3,32,128]{3,2,1,0:T(8,128)} %get-tuple-element.25), channel_id=1, source_target_pairs={{1,0},{2,1},{3,2},{5,4},{6,5},{7,6},{9,8},{10,9},{11,10},{13,12},{... | collective-permute-start | bytes 1032200 | tf_op jit(solution)/shard_map/ppermute | solution.py:427
  37.0 2.5 %all-to-all-done.got_ref = f32[16,8,128]{2,1,0:T(8,128)S(1)} async-done(((f32[16,8,128]{2,1,0:T(8,128)}), f32[16,8,128]{2,1,0:T(8,128)S(1)}, u32[]{:S(2)}, u32[]{:S(2)}) %all-to-all-start) | async-done | bytes 65568 | tf_op jit(solution)/shard_map/all_to_all | solution.py:420
  39.6 0.0 copy-done
  39.6 0.0 copy-done.1
  39.6 0.0 copy-start.2
  39.6 0.9 %copy-done.2 = f32[16,32,128]{2,1,0:T(8,128)S(1)} copy-done((f32[16,32,128]{2,1,0:T(8,128)S(1)}, f32[16,32,128]{2,1,0:T(8,128)}, u32[]{:S(2)}) %copy-start.2) | copy-done | bytes 262168
  40.5 6.8 %inner.1 = (f32[6,16,32,128]{3,2,1,0:T(8,128)}, f32[32,16,128]{2,1,0:T(8,128)S(1)}, f32[2,6,2,32,128]{4,3,2,1,0:T(8,128)S(1)}, f32[2,6,2,32,128]{4,3,2,1,0:T(8,1...) custom-call(f32[1]{0:T(128)S(6)} %copy.11.omega_ref, ...), custom_call_target="tpu_custom_call" | custom-call | flops 10000000000 | bytes 30000000 | tf_op jit(solution)/shard_map/inner/pallas_call | solution.py:255
  47.3 1.8 %collective-permute-done.5.staged_hbm = f32[3,3,32,128]{3,2,1,0:T(8,128)} collective-permute-done((f32[3,3,32,128]{3,2,1,0:T(8,128)}, f32[3,3,32,128]{3,2,1,0:T(8,128)}, u32[]{:S(2)}, u32[]{:S(2)}) %collective-permute-start.5) | collective-permute-done | bytes 147488 | tf_op jit(solution)/shard_map/ppermute | solution.py:425
  49.1 5.3 %collective-permute-done.3.direct_hbm = f32[4,3,32,128]{3,2,1,0:T(8,128)} collective-permute-done((f32[4,3,32,128]{3,2,1,0:T(8,128)}, f32[4,3,32,128]{3,2,1,0:T(8,128)}, u32[]{:S(2)}, u32[]{:S(2)}) %collective-permute-start.3) | collective-permute-done | bytes 196640 | tf_op jit(solution)/shard_map/ppermute | solution.py:424
  54.4 0.0 collective-permute-done.1.before_hbm
  54.4 0.0 collective-permute-done.2.after_hbm
  54.4 3.4 %outer.1 = (f32[6,16,32,128]{3,2,1,0:T(8,128)}, f32[16,16,128]{2,1,0:T(8,128)S(1)}, f32[16,16,128]{2,1,0:T(8,128)S(1)}) custom-call(f32[1]{0:T(128)S(6)} %copy.11.omega_ref, f32[32,16,128]{2,1,0:T(8,128)S(1)} %get-tuple-element.20.inner_grad_ref, f32[6,16,32,128]{3,2,1,0:T(8,128)S(1)} %bitcast.8, ...), custom_call_target="tpu_custom_call", output_to_operand_aliasing={{0}: (12, {})} | custom-call | flops 100000000 | bytes 3000000 | tf_op jit(solution)/shard_map/outer/pallas_call | solution.py:380
  57.8 1.9 %collective-permute-start.6 = (f32[16,16,128]{2,1,0:T(8,128)S(1)}, f32[16,16,128]{2,1,0:T(8,128)S(1)}, u32[]{:S(2)}, u32[]{:S(2)}) collective-permute-start(f32[16,16,128]{2,1,0:T(8,128)S(1)} %get-tuple-element.35), channel_id=1, source_target_pairs={{0,16},{16,0},{32,48},{48,32},{64,80},{80,64},{96,112},{112,96},{1... | collective-permute-start | bytes 393224 | tf_op jit(solution)/shard_map/ppermute | solution.py:432
  59.7 1.3 %collective-permute-done.6 = f32[16,16,128]{2,1,0:T(8,128)S(1)} collective-permute-done((f32[16,16,128]{2,1,0:T(8,128)S(1)}, f32[16,16,128]{2,1,0:T(8,128)S(1)}, u32[]{:S(2)}, u32[]{:S(2)}) %collective-permute-start.6) | collective-permute-done | bytes 131104 | tf_op jit(solution)/shard_map/ppermute | solution.py:432
  61.1 12.7 %all_to_all.10 = f32[16,16,128]{2,1,0:T(8,128)S(1)} all-to-all(f32[16,16,128]{2,1,0:T(8,128)S(1)} %add.12), channel_id=1, replica_groups={{0,32,64,96,128,160,192,224,256,288,320,352,384,416,448,480},{16,48,80,..., dimensions={0} | all-to-all | bytes 262144 | tf_op jit(solution)/shard_map/all_to_all | solution.py:434
  73.8 0.6 reduce_sum.9
  (1 shorter events, 0.0 us)
Async XLA Ops:
  0.6 39.0 %copy-start = (f32[1,6,16,32,128]{4,3,2,1,0:T(8,128)S(1)}, f32[1,6,16,32,128]{4,3,2,1,0:T(8,128)}, u32[]{:S(2)}) copy-start(f32[1,6,16,32,128]{4,3,2,1,0:T(8,128)} %param.8) | copy-start | bytes 4718596
  0.6 38.9 %copy-start.1 = (f32[1,6,16,32,128]{4,3,2,1,0:T(8,128)S(1)}, f32[1,6,16,32,128]{4,3,2,1,0:T(8,128)}, u32[]{:S(2)}) copy-start(f32[1,6,16,32,128]{4,3,2,1,0:T(8,128)} %param.7) | copy-start | bytes 4718596
  4.2 24.2 %collective-permute-start = (f32[4,3,32,128]{3,2,1,0:T(8,128)}, f32[4,3,32,128]{3,2,1,0:T(8,128)S(1)}, u32[]{:S(2)}, u32[]{:S(2)}) collective-permute-start(f32[4,3,32,128]{3,2,1,0:T(8,128)} %get-tuple-element.21), channel_id=1, source_target_pairs={{3,0},{7,4},{11,8},{15,12},{0,3},{4,7},{8,11},{12,15},{19,16},{23,... | collective-permute-start | bytes 589832 | tf_op jit(solution)/shard_map/ppermute | solution.py:418
  11.7 15.4 %collective-permute-start.4 = (f32[3,3,32,128]{3,2,1,0:T(8,128)}, f32[3,3,32,128]{3,2,1,0:T(8,128)}, u32[]{:S(2)}, u32[]{:S(2)}) collective-permute-start(f32[3,3,32,128]{3,2,1,0:T(8,128)} %get-tuple-element.27), channel_id=1, source_target_pairs={{3,1},{7,5},{11,9},{15,13},{0,2},{4,6},{8,10},{12,14},{19,17},{23,... | collective-permute-start | bytes 442376 | tf_op jit(solution)/shard_map/ppermute | solution.py:419
  13.7 25.9 %all-to-all-start = ((f32[16,8,128]{2,1,0:T(8,128)}), f32[16,8,128]{2,1,0:T(8,128)S(1)}, u32[]{:S(2)}, u32[]{:S(2)}) async-start(f32[16,8,128]{2,1,0:T(8,128)} %get-tuple-element.19), calls=%async_computation | async-start | bytes 131072 | tf_op jit(solution)/shard_map/all_to_all | solution.py:420
  27.1 21.9 %collective-permute-start.5 = (f32[3,3,32,128]{3,2,1,0:T(8,128)}, f32[3,3,32,128]{3,2,1,0:T(8,128)}, u32[]{:S(2)}, u32[]{:S(2)}) collective-permute-start(f32[3,3,32,128]{3,2,1,0:T(8,128)} %collective-permute-done.4), channel_id=1, source_target_pairs={{1,4},{5,8},{9,12},{6,3},{10,7},{14,11},{17,20},{21,24},{25,28},{2... | collective-permute-start | bytes 442376 | tf_op jit(solution)/shard_map/ppermute | solution.py:425
  29.2 25.2 %collective-permute-start.3 = (f32[4,3,32,128]{3,2,1,0:T(8,128)}, f32[4,3,32,128]{3,2,1,0:T(8,128)}, u32[]{:S(2)}, u32[]{:S(2)}) collective-permute-start(f32[4,3,32,128]{3,2,1,0:T(8,128)} %broadcast_select_fusion), channel_id=1, source_target_pairs={{0,4},{4,8},{8,12},{7,3},{11,7},{15,11},{16,20},{20,24},{24,28},{2... | collective-permute-start | bytes 589832 | tf_op jit(solution)/shard_map/ppermute | solution.py:424
  30.4 24.0 %collective-permute-start.1 = (f32[7,3,32,128]{3,2,1,0:T(8,128)}, f32[7,3,32,128]{3,2,1,0:T(8,128)S(1)}, u32[]{:S(2)}, u32[]{:S(2)}) collective-permute-start(f32[7,3,32,128]{3,2,1,0:T(8,128)} %get-tuple-element.24), channel_id=1, source_target_pairs={{0,1},{1,2},{2,3},{4,5},{5,6},{6,7},{8,9},{9,10},{10,11},{12,13},{... | collective-permute-start | bytes 1032200 | tf_op jit(solution)/shard_map/ppermute | solution.py:426
  31.7 22.7 %collective-permute-start.2 = (f32[7,3,32,128]{3,2,1,0:T(8,128)}, f32[7,3,32,128]{3,2,1,0:T(8,128)}, u32[]{:S(2)}, u32[]{:S(2)}) collective-permute-start(f32[7,3,32,128]{3,2,1,0:T(8,128)} %get-tuple-element.25), channel_id=1, source_target_pairs={{1,0},{2,1},{3,2},{5,4},{6,5},{7,6},{9,8},{10,9},{11,10},{13,12},{... | collective-permute-start | bytes 1032200 | tf_op jit(solution)/shard_map/ppermute | solution.py:427
  39.6 1.0 %copy-start.2 = (f32[16,32,128]{2,1,0:T(8,128)S(1)}, f32[16,32,128]{2,1,0:T(8,128)}, u32[]{:S(2)}) copy-start(f32[16,32,128]{2,1,0:T(8,128)} %sigma_hbm.3) | copy-start | bytes 786436
  57.8 3.2 %collective-permute-start.6 = (f32[16,16,128]{2,1,0:T(8,128)S(1)}, f32[16,16,128]{2,1,0:T(8,128)S(1)}, u32[]{:S(2)}, u32[]{:S(2)}) collective-permute-start(f32[16,16,128]{2,1,0:T(8,128)S(1)} %get-tuple-element.35), channel_id=1, source_target_pairs={{0,16},{16,0},{32,48},{48,32},{64,80},{80,64},{96,112},{112,96},{1... | collective-permute-start | bytes 393224 | tf_op jit(solution)/shard_map/ppermute | solution.py:432

commit v7 on v5

--- a/solution.py
+++ b/solution.py
@@ -223,7 +223,7 @@
             if last:
                 grad_ref[:, pl.ds(x, 1), :] = (terms * (omega * factor)).reshape(ny, 1, nz)
             return carry
-        lax.fori_loop(0, new.shape[1], layer, 0, unroll=new.shape[1] // 2)
+        lax.fori_loop(0, new.shape[1], layer, 0, unroll=new.shape[1])
 
     grad_ref[...] = jnp.zeros_like(grad_ref)
     sweep(field_0, field_1, 1, False)
@@ -272,7 +272,7 @@
             pltpu.SemaphoreType.DMA((12,)),
         ],
         compiler_params=pltpu.CompilerParams(vmem_limit_bytes=20 * 1024 * 1024),
-        cost_estimate=pl.CostEstimate(flops=10_000_000_000, bytes_accessed=30_000_000, transcendentals=0),
+        cost_estimate=pl.CostEstimate(flops=10_000_000_000, bytes_accessed=8_000_000, transcendentals=0),
         name="inner",
     )(omega, got, sigma, prev, fwd)
 
@@ -397,7 +397,7 @@
         ],
         input_output_aliases={12: 0},
         compiler_params=pltpu.CompilerParams(vmem_limit_bytes=12 * 1024 * 1024),
-        cost_estimate=pl.CostEstimate(flops=100_000_000, bytes_accessed=3_000_000, transcendentals=0),
+        cost_estimate=pl.CostEstimate(flops=3_000_000_000, bytes_accessed=300_000, transcendentals=0),
         name="outer",
     )(omega, grad, prev, fwd, *halos, *from_inner, adjoint)
 

time: 73.4 us -> 73.4 us (level)
  transfers between devices with their start and end apart: 8 -> 8, of which waited for: 4 -> 4; matrix products, arithmetic and copies ran while one was open for 0% -> 0% of each run, Pallas kernels for 10% -> 9%
where the time goes in v7:
time: 73.4 us; the launch traced here: 73 us
  starting transfers between devices  32 us (44%)
  Pallas kernels  13.9 us (19%)
  blocking collectives  12.7 us (17%)
  waiting for transfers between devices  10.9 us (15%)
  local copies, waits for them, and re-layouts  1.42 us (2%)
  between operations  1.41 us (2%)
    all_to_all x1, starting transfers between devices, shards(): got = lax.all_to_all(send, 'slab', split_axis=0, concat_axis=0, tiled=True)  12.8 us
    all_to_all x1, blocking collectives, shards(): lax.all_to_all(terms, 'tx', split_axis=0, concat_axis=0, axis_index_group...  12.7 us
    ppermute x1, starting transfers between devices, shards(): part_a = lax.ppermute(part_a, 'slab', stage_a)  7.5 us
    pallas_call x1, Pallas kernels, inner(): pl.pallas_call(functools.partial(inner_kernel, factor), out_shape=[jax.Sh...  6.76 us
    ppermute x1, starting transfers between devices, shards(): after = lax.ppermute(lowest, 'slab', down)  4.57 us
    ppermute x1, waiting for transfers between devices, shards(): part_a = lax.ppermute(part_a, 'slab', cross_a)  4.43 us
    all_to_all x1, waiting for transfers between devices, shards(): got = lax.all_to_all(send, 'slab', split_axis=0, concat_axis=0, tiled=True)  3.82 us
    pallas_call x1, Pallas kernels, outer(): pl.pallas_call(functools.partial(outer_kernel, slab_count, factor), out_s...  3.58 us
  transfers between devices with their start and end apart: 8, of which 4 were waited for; matrix products, arithmetic and copies ran while one was open for 0% of the time, Pallas kernels for 9%

profile of v7, /device:TPU:24, one launch (start us, length us, event | category | flops | bytes accessed | tf_op | source)
XLA Modules:
  0.0 73.0 jit_solution(510608571054240590)
XLA Ops:
  0.6 0.0 copy-start.1
  0.6 0.0 copy-start
  0.7 3.6 %pack.1 = (f32[16,8,128]{2,1,0:T(8,128)}, f32[4,3,32,128]{3,2,1,0:T(8,128)}, f32[3,3,32,128]{3,2,1,0:T(8,128)}, f32[7,3,32,128]{3,2,1,0:T(8,128)}, f32[7,3,32,128]{3,2,1,0:T(8,128)}) custom-call(f32[6,1,256]{2,1,0:T(1,128)} %bitcast.12, s32[1,256]{1,0:T(1,128)} %bitcast.13, s32[1,256]{1,0:T(1,128)} %cell_ref.1, f32[6,16,32,128]{3,2,1,0:T(8,128)} %bitcast.6, ...), custom_call_target="tpu_custom_call" | custom-call | flops 20000000 | bytes 100000 | tf_op jit(solution)/shard_map/pack/pallas_call | solution.py:108
  4.2 7.5 %collective-permute-start = (f32[4,3,32,128]{3,2,1,0:T(8,128)}, f32[4,3,32,128]{3,2,1,0:T(8,128)S(1)}, u32[]{:S(2)}, u32[]{:S(2)}) collective-permute-start(f32[4,3,32,128]{3,2,1,0:T(8,128)} %get-tuple-element.21), channel_id=1, source_target_pairs={{3,0},{7,4},{11,8},{15,12},{0,3},{4,7},{8,11},{12,15},{19,16},{23,... | collective-permute-start | bytes 589832 | tf_op jit(solution)/shard_map/ppermute | solution.py:418
  11.7 1.3 %collective-permute-start.4 = (f32[3,3,32,128]{3,2,1,0:T(8,128)}, f32[3,3,32,128]{3,2,1,0:T(8,128)S(1)}, u32[]{:S(2)}, u32[]{:S(2)}) collective-permute-start(f32[3,3,32,128]{3,2,1,0:T(8,128)} %get-tuple-element.27), channel_id=1, source_target_pairs={{3,1},{7,5},{11,9},{15,13},{0,2},{4,6},{8,10},{12,14},{19,17},{23,... | collective-permute-start | bytes 442376 | tf_op jit(solution)/shard_map/ppermute | solution.py:419
  13.0 12.8 %all-to-all-start = ((f32[16,8,128]{2,1,0:T(8,128)}), f32[16,8,128]{2,1,0:T(8,128)S(1)}, u32[]{:S(2)}, u32[]{:S(2)}) async-start(f32[16,8,128]{2,1,0:T(8,128)} %get-tuple-element.19), calls=%async_computation | async-start | bytes 131072 | tf_op jit(solution)/shard_map/all_to_all | solution.py:420
  26.5 0.0 collective-permute-done.4
  26.5 1.3 %collective-permute-start.5 = (f32[3,3,32,128]{3,2,1,0:T(8,128)S(1)}, f32[3,3,32,128]{3,2,1,0:T(8,128)S(1)}, u32[]{:S(2)}, u32[]{:S(2)}) collective-permute-start(f32[3,3,32,128]{3,2,1,0:T(8,128)S(1)} %collective-permute-done.4), channel_id=1, source_target_pairs={{1,4},{5,8},{9,12},{6,3},{10,7},{14,11},{17,20},{21,24},{25,28},{2... | collective-permute-start | bytes 442376 | tf_op jit(solution)/shard_map/ppermute | solution.py:425
  27.8 0.0 collective-permute-done
  27.8 1.3 %collective-permute-start.3 = (f32[4,3,32,128]{3,2,1,0:T(8,128)S(1)}, f32[4,3,32,128]{3,2,1,0:T(8,128)S(1)}, u32[]{:S(2)}, u32[]{:S(2)}) collective-permute-start(f32[4,3,32,128]{3,2,1,0:T(8,128)S(1)} %broadcast_select_fusion), channel_id=1, source_target_pairs={{0,4},{4,8},{8,12},{7,3},{11,7},{15,11},{16,20},{20,24},{24,28},{2... | collective-permute-start | bytes 589832 | tf_op jit(solution)/shard_map/ppermute | solution.py:424
  29.1 1.3 %collective-permute-start.1 = (f32[7,3,32,128]{3,2,1,0:T(8,128)}, f32[7,3,32,128]{3,2,1,0:T(8,128)S(1)}, u32[]{:S(2)}, u32[]{:S(2)}) collective-permute-start(f32[7,3,32,128]{3,2,1,0:T(8,128)} %get-tuple-element.24), channel_id=1, source_target_pairs={{0,1},{1,2},{2,3},{4,5},{5,6},{6,7},{8,9},{9,10},{10,11},{12,13},{... | collective-permute-start | bytes 1032200 | tf_op jit(solution)/shard_map/ppermute | solution.py:426
  30.4 4.6 %collective-permute-start.2 = (f32[7,3,32,128]{3,2,1,0:T(8,128)}, f32[7,3,32,128]{3,2,1,0:T(8,128)S(1)}, u32[]{:S(2)}, u32[]{:S(2)}) collective-permute-start(f32[7,3,32,128]{3,2,1,0:T(8,128)} %get-tuple-element.25), channel_id=1, source_target_pairs={{1,0},{2,1},{3,2},{5,4},{6,5},{7,6},{9,8},{10,9},{11,10},{13,12},{... | collective-permute-start | bytes 1032200 | tf_op jit(solution)/shard_map/ppermute | solution.py:427
  35.0 3.8 %all-to-all-done.got_ref = f32[16,8,128]{2,1,0:T(8,128)S(1)} async-done(((f32[16,8,128]{2,1,0:T(8,128)}), f32[16,8,128]{2,1,0:T(8,128)S(1)}, u32[]{:S(2)}, u32[]{:S(2)}) %all-to-all-start) | async-done | bytes 65568 | tf_op jit(solution)/shard_map/all_to_all | solution.py:420
  38.8 0.0 copy-done.1
  38.8 0.0 copy-done
  38.8 0.0 copy-start.2
  38.8 1.4 %copy-done.2 = f32[1,6,16,32,128]{4,3,2,1,0:T(8,128)S(1)} copy-done((f32[1,6,16,32,128]{4,3,2,1,0:T(8,128)S(1)}, f32[1,6,16,32,128]{4,3,2,1,0:T(8,128)}, u32[]{:S(2)}) %copy-start.2) | copy-done | bytes 1572888
  40.2 6.8 %inner.1 = (f32[6,16,32,128]{3,2,1,0:T(8,128)}, f32[32,16,128]{2,1,0:T(8,128)S(1)}, f32[2,6,2,32,128]{4,3,2,1,0:T(8,128)S(1)}, f32[2,6,2,32,128]{4,3,2,1,0:T(8,1...) custom-call(f32[1]{0:T(128)S(6)} %copy.11.omega_ref, ...), custom_call_target="tpu_custom_call" | custom-call | flops 10000000000 | bytes 8000000 | tf_op jit(solution)/shard_map/inner/pallas_call | solution.py:255
  47.0 1.3 %collective-permute-done.5.staged_hbm = f32[3,3,32,128]{3,2,1,0:T(8,128)S(1)} collective-permute-done((f32[3,3,32,128]{3,2,1,0:T(8,128)S(1)}, f32[3,3,32,128]{3,2,1,0:T(8,128)S(1)}, u32[]{:S(2)}, u32[]{:S(2)}) %collective-permute-start.5) | collective-permute-done | bytes 147488 | tf_op jit(solution)/shard_map/ppermute | solution.py:425
  48.3 4.4 %collective-permute-done.3.direct_hbm = f32[4,3,32,128]{3,2,1,0:T(8,128)S(1)} collective-permute-done((f32[4,3,32,128]{3,2,1,0:T(8,128)S(1)}, f32[4,3,32,128]{3,2,1,0:T(8,128)S(1)}, u32[]{:S(2)}, u32[]{:S(2)}) %collective-permute-start.3) | collective-permute-done | bytes 196640 | tf_op jit(solution)/shard_map/ppermute | solution.py:424
  52.8 0.0 collective-permute-done.1.before_hbm
  52.8 0.0 collective-permute-done.2.after_hbm
  52.8 3.6 %outer.1 = (f32[6,16,32,128]{3,2,1,0:T(8,128)}, f32[16,16,128]{2,1,0:T(8,128)S(1)}, f32[16,16,128]{2,1,0:T(8,128)S(1)}) custom-call(f32[1]{0:T(128)S(6)} %copy.11.omega_ref, f32[32,16,128]{2,1,0:T(8,128)S(1)} %get-tuple-element.20.inner_grad_ref, f32[6,16,32,128]{3,2,1,0:T(8,128)S(1)} %bitcast.8, ...), custom_call_target="tpu_custom_call", output_to_operand_aliasing={{0}: (12, {})} | custom-call | flops 3000000000 | bytes 300000 | tf_op jit(solution)/shard_map/outer/pallas_call | solution.py:380
  56.4 1.9 %collective-permute-start.6 = (f32[16,16,128]{2,1,0:T(8,128)S(1)}, f32[16,16,128]{2,1,0:T(8,128)S(1)}, u32[]{:S(2)}, u32[]{:S(2)}) collective-permute-start(f32[16,16,128]{2,1,0:T(8,128)S(1)} %get-tuple-element.35), channel_id=1, source_target_pairs={{0,16},{16,0},{32,48},{48,32},{64,80},{80,64},{96,112},{112,96},{1... | collective-permute-start | bytes 393224 | tf_op jit(solution)/shard_map/ppermute | solution.py:432
  58.3 1.3 %collective-permute-done.6 = f32[16,16,128]{2,1,0:T(8,128)S(1)} collective-permute-done((f32[16,16,128]{2,1,0:T(8,128)S(1)}, f32[16,16,128]{2,1,0:T(8,128)S(1)}, u32[]{:S(2)}, u32[]{:S(2)}) %collective-permute-start.6) | collective-permute-done | bytes 131104 | tf_op jit(solution)/shard_map/ppermute | solution.py:432
  59.6 12.7 %all_to_all.10 = f32[16,16,128]{2,1,0:T(8,128)S(1)} all-to-all(f32[16,16,128]{2,1,0:T(8,128)S(1)} %add.12), channel_id=1, replica_groups={{0,32,64,96,128,160,192,224,256,288,320,352,384,416,448,480},{16,48,80,..., dimensions={0} | all-to-all | bytes 262144 | tf_op jit(solution)/shard_map/all_to_all | solution.py:434
  72.3 0.6 reduce_sum.9
  (2 shorter events, 0.0 us)
Async XLA Ops:
  0.6 38.2 %copy-start.1 = (f32[16,32,128]{2,1,0:T(8,128)S(1)}, f32[16,32,128]{2,1,0:T(8,128)}, u32[]{:S(2)}) copy-start(f32[16,32,128]{2,1,0:T(8,128)} %sigma_hbm.3) | copy-start | bytes 786436
  0.6 38.2 %copy-start = (f32[1,6,16,32,128]{4,3,2,1,0:T(8,128)S(1)}, f32[1,6,16,32,128]{4,3,2,1,0:T(8,128)}, u32[]{:S(2)}) copy-start(f32[1,6,16,32,128]{4,3,2,1,0:T(8,128)} %param.8) | copy-start | bytes 4718596
  4.2 23.6 %collective-permute-start = (f32[4,3,32,128]{3,2,1,0:T(8,128)}, f32[4,3,32,128]{3,2,1,0:T(8,128)S(1)}, u32[]{:S(2)}, u32[]{:S(2)}) collective-permute-start(f32[4,3,32,128]{3,2,1,0:T(8,128)} %get-tuple-element.21), channel_id=1, source_target_pairs={{3,0},{7,4},{11,8},{15,12},{0,3},{4,7},{8,11},{12,15},{19,16},{23,... | collective-permute-start | bytes 589832 | tf_op jit(solution)/shard_map/ppermute | solution.py:418
  11.7 14.8 %collective-permute-start.4 = (f32[3,3,32,128]{3,2,1,0:T(8,128)}, f32[3,3,32,128]{3,2,1,0:T(8,128)S(1)}, u32[]{:S(2)}, u32[]{:S(2)}) collective-permute-start(f32[3,3,32,128]{3,2,1,0:T(8,128)} %get-tuple-element.27), channel_id=1, source_target_pairs={{3,1},{7,5},{11,9},{15,13},{0,2},{4,6},{8,10},{12,14},{19,17},{23,... | collective-permute-start | bytes 442376 | tf_op jit(solution)/shard_map/ppermute | solution.py:419
  13.0 25.8 %all-to-all-start = ((f32[16,8,128]{2,1,0:T(8,128)}), f32[16,8,128]{2,1,0:T(8,128)S(1)}, u32[]{:S(2)}, u32[]{:S(2)}) async-start(f32[16,8,128]{2,1,0:T(8,128)} %get-tuple-element.19), calls=%async_computation | async-start | bytes 131072 | tf_op jit(solution)/shard_map/all_to_all | solution.py:420
  26.5 21.8 %collective-permute-start.5 = (f32[3,3,32,128]{3,2,1,0:T(8,128)S(1)}, f32[3,3,32,128]{3,2,1,0:T(8,128)S(1)}, u32[]{:S(2)}, u32[]{:S(2)}) collective-permute-start(f32[3,3,32,128]{3,2,1,0:T(8,128)S(1)} %collective-permute-done.4), channel_id=1, source_target_pairs={{1,4},{5,8},{9,12},{6,3},{10,7},{14,11},{17,20},{21,24},{25,28},{2... | collective-permute-start | bytes 442376 | tf_op jit(solution)/shard_map/ppermute | solution.py:425
  27.8 24.9 %collective-permute-start.3 = (f32[4,3,32,128]{3,2,1,0:T(8,128)S(1)}, f32[4,3,32,128]{3,2,1,0:T(8,128)S(1)}, u32[]{:S(2)}, u32[]{:S(2)}) collective-permute-start(f32[4,3,32,128]{3,2,1,0:T(8,128)S(1)} %broadcast_select_fusion), channel_id=1, source_target_pairs={{0,4},{4,8},{8,12},{7,3},{11,7},{15,11},{16,20},{20,24},{24,28},{2... | collective-permute-start | bytes 589832 | tf_op jit(solution)/shard_map/ppermute | solution.py:424
  29.1 23.6 %collective-permute-start.1 = (f32[7,3,32,128]{3,2,1,0:T(8,128)}, f32[7,3,32,128]{3,2,1,0:T(8,128)S(1)}, u32[]{:S(2)}, u32[]{:S(2)}) collective-permute-start(f32[7,3,32,128]{3,2,1,0:T(8,128)} %get-tuple-element.24), channel_id=1, source_target_pairs={{0,1},{1,2},{2,3},{4,5},{5,6},{6,7},{8,9},{9,10},{10,11},{12,13},{... | collective-permute-start | bytes 1032200 | tf_op jit(solution)/shard_map/ppermute | solution.py:426
  30.4 22.4 %collective-permute-start.2 = (f32[7,3,32,128]{3,2,1,0:T(8,128)}, f32[7,3,32,128]{3,2,1,0:T(8,128)S(1)}, u32[]{:S(2)}, u32[]{:S(2)}) collective-permute-start(f32[7,3,32,128]{3,2,1,0:T(8,128)} %get-tuple-element.25), channel_id=1, source_target_pairs={{1,0},{2,1},{3,2},{5,4},{6,5},{7,6},{9,8},{10,9},{11,10},{13,12},{... | collective-permute-start | bytes 1032200 | tf_op jit(solution)/shard_map/ppermute | solution.py:427
  38.8 1.4 %copy-start.2 = (f32[1,6,16,32,128]{4,3,2,1,0:T(8,128)S(1)}, f32[1,6,16,32,128]{4,3,2,1,0:T(8,128)}, u32[]{:S(2)}) copy-start(f32[1,6,16,32,128]{4,3,2,1,0:T(8,128)} %param.7) | copy-start | bytes 4718596
  56.4 3.2 %collective-permute-start.6 = (f32[16,16,128]{2,1,0:T(8,128)S(1)}, f32[16,16,128]{2,1,0:T(8,128)S(1)}, u32[]{:S(2)}, u32[]{:S(2)}) collective-permute-start(f32[16,16,128]{2,1,0:T(8,128)S(1)} %get-tuple-element.35), channel_id=1, source_target_pairs={{0,16},{16,0},{32,48},{48,32},{64,80},{80,64},{96,112},{112,96},{1... | collective-permute-start | bytes 393224 | tf_op jit(solution)/shard_map/ppermute | solution.py:432
